TPU v7x, 32 devices: a whole 2x2x4 slice. The times are simulated.
32 devices in a mesh: orb: 16 (over z, y, x), trial: 2 (over core).
Axes of the slice: x: 2, y: 2, z: 4, core: 2. Of those that a mesh axis runs over, the one named last changes fastest.
Arguments:
- trials: float32 [4, 64, 4096], P('trial', 'orb'), may hold values from -120 to 120
- orbitals: bfloat16 [32, 64, 4096], P('orb'), may hold values from -6 to 6
- potential: float32 [64, 4096], P('orb'), may hold values from 0.5 to 2
- coulomb: float32 [3, 64, 64], replicated, may hold values from -0.75 to 0.75
- energies: float32 [32], replicated, may hold values from -1.5 to -0.3
- frequencies: float32 [8], replicated, may hold values from 0.3 to 4
- orbital_ids: int32 [32], P('orb'), may hold values from 0 to 31, each once
- freq_index: int32 [32], P('orb'), may hold values from 0 to 7
Outputs:
- filtered: float32 [4, 64, 4096], P('trial', 'orb')
All inputs are finite; a program needn't handle non-finite values.
Results may differ from a plain program's by a relative error of at most 0.0003.
Values sent between devices are 32-bit elements; how exact they have to be, the bound alone decides.
No kernel may reach another device: no remote copies, remote signals or barrier semaphores. Data moves between devices by JAX's collectives and lax.ppermute only.
A program may use at most 64 MiB of HBM per device.

v0:
```python
import jax
import jax.numpy as jnp
from jax import lax
from jax.sharding import PartitionSpec as P

G = 64
ITERS = 3


def orbital_shifts(orbital_ids, freq_index, energies, frequencies):
    energy_slots = lax.broadcasted_iota(jnp.int32, (1, energies.shape[0]), 1)
    picked_energy = jnp.sum(
        jnp.where(orbital_ids[:, None] == energy_slots, energies[None, :], 0.0), axis=1
    )
    freq_slots = lax.broadcasted_iota(jnp.int32, (1, frequencies.shape[0]), 1)
    picked_freq = jnp.sum(
        jnp.where(freq_index[:, None] == freq_slots, frequencies[None, :], 0.0), axis=1
    )
    return picked_freq - picked_energy


def neighbour_sum(grid_field):
    grid_width = grid_field.shape[-2]
    z_index = lax.broadcasted_iota(jnp.int32, (1, grid_field.shape[-1]), 1) % grid_width
    zero_cells = jnp.zeros_like(grid_field[..., :1])
    upper_z = jnp.where(
        z_index == grid_width - 1, 0.0, jnp.concatenate([grid_field[..., 1:], zero_cells], axis=-1)
    )
    lower_z = jnp.where(
        z_index == 0, 0.0, jnp.concatenate([zero_cells, grid_field[..., :-1]], axis=-1)
    )
    zero_line = jnp.zeros_like(grid_field[..., :grid_width])
    upper_y = jnp.concatenate([grid_field[..., grid_width:], zero_line], axis=-1)
    lower_y = jnp.concatenate([zero_line, grid_field[..., :-grid_width]], axis=-1)
    zero_plane = jnp.zeros_like(grid_field[..., :1, :])
    upper_x = jnp.concatenate([grid_field[..., 1:, :], zero_plane], axis=-2)
    lower_x = jnp.concatenate([zero_plane, grid_field[..., :-1, :]], axis=-2)
    return upper_z + lower_z + upper_y + lower_y + upper_x + lower_x


def apply_shifted(grid_field, potential, level_shift):
    return (3.0 + potential + level_shift) * grid_field - 0.5 * neighbour_sum(grid_field)


def cell_inner(left_field, right_field):
    return jnp.sum(left_field * right_field, axis=(1, 2))


def sternheimer(source, potential, level_shift):
    iterate = jnp.zeros_like(source)
    residual = source
    direction = source
    norm_now = cell_inner(residual, residual)[:, None, None]
    for sweep_index in range(ITERS):
        mapped = apply_shifted(direction, potential, level_shift)
        step_size = norm_now / cell_inner(direction, mapped)[:, None, None]
        iterate = iterate + step_size * direction
        residual = residual - step_size * mapped
        norm_next = cell_inner(residual, residual)[:, None, None]
        direction = residual + norm_next / norm_now * direction
        norm_now = norm_next
    return iterate


def orbital_response(whole, orbitals, potential, shifts):

    def one_orbital(accumulated, scanned):
        orbital, level_shift = scanned
        density = orbital.astype(jnp.float32)[None]
        solved = sternheimer(density * whole, potential, level_shift)
        return (accumulated - density * solved, None)

    result, unused = lax.scan(one_orbital, jnp.zeros_like(whole), (orbitals, shifts))
    return result


def coulomb_planes(summed, factors):
    trial_count = summed.shape[0]
    plane_count = summed.shape[1]
    grid_width = factors.shape[1]
    plane_view = summed.reshape(trial_count, plane_count, grid_width, grid_width)
    plane_view = jnp.einsum(
        "cz,txyz->txyc", factors[2], plane_view, precision=lax.Precision.HIGHEST
    )
    plane_view = jnp.einsum(
        "by,txyc->txbc", factors[1], plane_view, precision=lax.Precision.HIGHEST
    )
    turned = jnp.einsum(
        "ax,txbc->tabc",
        factors[0],
        lax.all_to_all(plane_view, "orb", split_axis=2, concat_axis=1, tiled=True),
        precision=lax.Precision.HIGHEST,
    )
    plane_view = lax.all_to_all(turned, "orb", split_axis=1, concat_axis=2, tiled=True)
    return plane_view.reshape(trial_count, plane_count, grid_width * grid_width)


def shards(trials, orbitals, potential, coulomb, energies, frequencies, orbital_ids, freq_index):
    shifts = orbital_shifts(orbital_ids, freq_index, energies, frequencies)
    full_potential = lax.all_gather(potential, "orb", axis=0, tiled=True)

    def apply_kernel(planes):
        whole = lax.all_gather(planes, "orb", axis=1, tiled=True)
        partial_value = orbital_response(whole, orbitals, full_potential, shifts)
        summed = lax.psum_scatter(partial_value, "orb", scatter_dimension=1, tiled=True)
        summed = coulomb_planes(summed, coulomb)
        return summed

    mapped = apply_kernel(trials)
    squares, cross_sum, mapped_squares = lax.psum(
        (cell_inner(trials, trials), cell_inner(trials, mapped), cell_inner(mapped, mapped)), "orb"
    )
    center = (cross_sum / squares)[:, None, None]
    spread = jnp.sqrt(mapped_squares / squares)[:, None, None]
    first = (mapped - center * trials) / spread
    second_mapped = apply_kernel(first)
    second = 2.0 * (second_mapped - center * first) / spread - trials
    block = lax.all_gather(second, "trial", axis=0, tiled=True)
    columns = block.reshape(block.shape[0], -1)
    local_gram = jnp.dot(columns, columns.T, precision=lax.Precision.HIGHEST)
    gram_matrix = lax.psum(local_gram, "orb") / float(G**3)
    lower = jnp.linalg.cholesky(gram_matrix)
    identity = jnp.eye(gram_matrix.shape[0], dtype=gram_matrix.dtype)
    inverse = lax.linalg.triangular_solve(lower, identity, left_side=True, lower=True)
    trial_count = second.shape[0]
    own_rows = lax.dynamic_slice_in_dim(
        inverse, lax.axis_index("trial") * trial_count, trial_count, 0
    )
    result = jnp.dot(own_rows, columns, precision=lax.Precision.HIGHEST)
    return result.reshape(second.shape)


def solution(mesh):
    in_specs = (
        P("trial", "orb", None),
        P("orb", None, None),
        P("orb", None),
        P(),
        P(),
        P(),
        P("orb"),
        P("orb"),
    )
    out_specs = P("trial", "orb", None)
    return jax.shard_map(shards, mesh=mesh, in_specs=in_specs, out_specs=out_specs, check_vma=False)
```

profile of v0, /device:TPU:0, one launch (start us, length us, event | category | flops | bytes accessed | tf_op | source)
XLA Modules:
  0.0 725.5 jit_solution(7675088663543733976)
XLA Ops:
  7.3 1.7 copy.92
  10.8 57.4 %all-gather.9.cloned.1.call-done = f32[16,4,4096]{2,1,0:T(4,128)} async-done(((f32[1,4,4096]{2,1,0:T(4,128)}), f32[16,4,4096]{2,1,0:T(4,128)}) %all-gather.9.cloned.1.call-update) | async-done | bytes 1048592 | tf_op jit(solution)/shard_map/all_gather | solution.py:100
  68.1 2.6 reshape.158
  70.7 59.7 %all-gather.5.cloned.1.call-done = f32[2,64,4096]{2,0,1:T(2,128)} async-done(((f32[2,4,4096]{2,0,1:T(2,128)}), f32[2,64,4096]{2,0,1:T(2,128)}) %all-gather.5.cloned.1.call-update) | async-done | bytes 2097168 | tf_op jit(solution)/shard_map/all_gather | solution.py:103
  130.4 4.2 copy.93
  134.6 62.8 %while.26 = (s32[]{:T(128)}, f32[2,64,4096]{2,1,0:T(8,128)}, bf16[2,64,4096]{2,1,0:T(8,128)(2,1)}, f32[2,64,4096]{2,1,0:T(8,128)}, f32[64,4096]{1,0:T(8,128)}, /*index=5*/f32[2]{0:T(128)S(1)}, s32[]{:T(128)}, s32[]{:T(128)}) while((s32[]{:T(128)}, f32[2,64,4096]{2,1,0:T(8,128)}, bf16[2,64,4096]{2,1,0:T(8,128)(2,1)}, ...), condition=%wide.region_9.10_spmd.clone, body=%wide.region_2.9_spmd.clone.sunk | while | flops 34897920 | bytes 182869376 | solution.py:73
  134.6 1.1 bitcast_convert_fusion.4
  135.7 1.8 broadcast_multiply_fusion.5
  139.9 1.9 add_add_fusion.4
  141.9 3.5 multiply_reduce_fusion.25
  145.4 2.3 multiply_reduce_fusion.26
  147.8 2.0 multiply_add_fusion.8
  150.9 2.1 fusion.88
  153.0 3.4 multiply_reduce_fusion.27
  159.4 1.9 multiply_reduce_fusion.29
  161.3 4.4 select_subtract_fusion.4
  165.7 1.1 bitcast_convert_fusion.4
  166.8 1.8 broadcast_multiply_fusion.5
  171.0 1.9 add_add_fusion.4
  173.0 3.5 multiply_reduce_fusion.25
  176.5 2.3 multiply_reduce_fusion.26
  178.9 2.0 multiply_add_fusion.8
  182.0 2.1 fusion.88
  184.1 3.4 multiply_reduce_fusion.27
  190.5 1.9 multiply_reduce_fusion.29
  192.4 5.0 select_subtract_fusion.4
  199.3 122.9 %all-reduce.42.cloned.1.call-done = f32[2,64,4096]{2,1,0:T(8,128)} async-done(((f32[2,64,4096]{2,1,0:T(8,128)}), f32[2,64,4096]{2,1,0:T(8,128)}) %all-reduce.42.cloned.1.call-update) | async-done | bytes 2097168
  325.0 12.6 %all_to_all.66 = f32[16,1,2048]{2,1,0:T(1,128)S(1)} all-to-all(f32[16,1,2048]{2,1,0:T(1,128)S(1)} %reshape.172), channel_id=1, replica_groups=mesh['orb'=16,'trial'=2] {'orb'}, dimensions={0} | all-to-all | bytes 262144 | tf_op jit(solution)/shard_map/all_to_all | solution.py:91
  338.2 1.0 reduce.7
  340.6 10.5 %all_to_all.67 = f32[16,1,2048]{2,1,0:T(1,128)S(1)} all-to-all(f32[16,1,2048]{2,1,0:T(1,128)S(1)} %reshape.174), channel_id=1, replica_groups=mesh['orb'=16,'trial'=2] {'orb'}, dimensions={0} | all-to-all | bytes 262144 | tf_op jit(solution)/shard_map/all_to_all | solution.py:94
  351.2 1.0 reduce.8
  353.2 37.9 %all-reduce.38 = (f32[2]{0:T(128)S(1)}, f32[2]{0:T(128)S(1)}, f32[2]{0:T(128)S(1)}) all-reduce(f32[2]{0:T(128)S(1)} %multiply_reduce_fusion.12, f32[2]{0:T(128)S(1)} %get-tuple-element.258, f32[2]{0:T(128)S(1)} %get-tuple-element.257), channel_id=1, replica_groups=mesh['orb'=16,'trial'=2] {'orb'}, use_global_device_ids=true, to_apply=%region_16.17 | all-reduce | flops 6 | bytes 48 | tf_op jit(solution)/shard_map/psum | solution.py:110
  393.1 57.2 %all-gather.7.cloned.1.call-done = f32[2,64,4096]{2,0,1:T(2,128)} async-done(((f32[2,4,4096]{2,0,1:T(2,128)}), f32[2,64,4096]{2,0,1:T(2,128)}) %all-gather.7.cloned.1.call-update) | async-done | bytes 2097168 | tf_op jit(solution)/shard_map/all_gather | solution.py:103
  450.4 4.2 copy.103
  454.5 63.0 %while.27 = (s32[]{:T(128)}, f32[2,64,4096]{2,1,0:T(8,128)}, bf16[2,64,4096]{2,1,0:T(8,128)(2,1)}, f32[2,64,4096]{2,1,0:T(8,128)}, f32[64,4096]{1,0:T(8,128)}, /*index=5*/f32[2]{0:T(128)S(1)}, s32[]{:T(128)}, s32[]{:T(128)}) while((s32[]{:T(128)}, f32[2,64,4096]{2,1,0:T(8,128)}, bf16[2,64,4096]{2,1,0:T(8,128)(2,1)}, ...), condition=%wide.region_24.25_spmd.clone, body=%wide.region_17.24_spmd.clone.sunk | while | flops 34897920 | bytes 182869376 | solution.py:73
  454.5 1.1 bitcast_convert_fusion.5
  455.6 1.8 broadcast_multiply_fusion.6
  459.9 1.9 add_add_fusion.5
  461.9 3.5 multiply_reduce_fusion.30
  465.4 2.3 multiply_reduce_fusion.31
  467.7 2.0 multiply_add_fusion.10
  470.9 2.1 fusion.98
  473.0 3.4 multiply_reduce_fusion.32
  479.4 1.9 multiply_reduce_fusion.34
  481.3 4.4 select_subtract_fusion.5
  485.6 1.1 bitcast_convert_fusion.5
  486.8 1.8 broadcast_multiply_fusion.6
  491.0 1.9 add_add_fusion.5
  493.0 3.5 multiply_reduce_fusion.30
  496.5 2.3 multiply_reduce_fusion.31
  498.8 2.0 multiply_add_fusion.10
  502.0 2.1 fusion.98
  504.1 3.4 multiply_reduce_fusion.32
  510.5 1.9 multiply_reduce_fusion.34
  512.4 5.0 select_subtract_fusion.5
  517.6 124.7 %all-reduce.44.cloned.1.call-done = f32[2,64,4096]{2,1,0:T(8,128)} async-done(((f32[2,64,4096]{2,1,0:T(8,128)}), f32[2,64,4096]{2,1,0:T(8,128)}) %all-reduce.44.cloned.1.call-update) | async-done | bytes 2097168
  645.1 12.6 %all_to_all.68 = f32[16,1,2048]{2,1,0:T(1,128)S(1)} all-to-all(f32[16,1,2048]{2,1,0:T(1,128)S(1)} %reshape.176), channel_id=1, replica_groups=mesh['orb'=16,'trial'=2] {'orb'}, dimensions={0} | all-to-all | bytes 262144 | tf_op jit(solution)/shard_map/all_to_all | solution.py:91
  657.7 1.0 reduce.9
  660.8 3.5 all-to-all-start.3
  664.4 7.8 %all-to-all-done.3 = f32[16,1,2048]{2,1,0:T(1,128)S(1)} async-done(((f32[16,1,2048]{2,1,0:T(1,128)}), f32[16,1,2048]{2,1,0:T(1,128)S(1)}, u32[]{:S(2)}, u32[]{:S(2)}) %all-to-all-start.3) | async-done | bytes 131104 | tf_op jit(solution)/shard_map/all_to_all | solution.py:94
  672.1 1.0 reduce.10
  673.9 2.0 all_gather.15
  675.9 1.2 convolution_bitcast_fusion.4
  677.2 37.8 %psum.31 = f32[4,4]{0,1:T(4,128)S(1)} all-reduce(f32[4,4]{0,1:T(4,128)S(1)} %convolution_bitcast_fusion.4), channel_id=1, replica_groups=mesh['orb'=16,'trial'=2] {'orb'}, use_global_device_ids=true, to_apply=%region_26.27 | all-reduce | flops 16 | bytes 128 | tf_op jit(solution)/shard_map/psum | solution.py:121
  (164 shorter events, 47.2 us)
Async XLA Ops:
  6.5 61.6 %all-gather.9.cloned.1.call-start = ((), (), s32[]{:S(2)}) async-start(), calls=%async_computation.6 | async-start | bytes 1114112 | tf_op jit(solution)/shard_map/all_gather | solution.py:100
  7.3 123.2 %all-gather.5.cloned.1.call-start = ((), (), s32[]{:S(2)}) async-start(), calls=%async_computation.4 | async-start | bytes 2228224 | tf_op jit(solution)/shard_map/all_gather | solution.py:103
  9.0 313.2 %all-reduce.42.cloned.1.call-start = ((), (), s32[]{:S(2)}) async-start(), calls=%async_computation.7 | async-start | bytes 4194304
  157.5 1.9 copy-start
  188.6 1.9 copy-start
  197.4 0.7 copy-start.12
  197.4 125.9 %copy-start.6 = (f32[3,64,64]{2,1,0:T(8,128)S(1)}, f32[3,64,64]{2,1,0:T(8,128)}, u32[]{:S(2)}) copy-start(f32[3,64,64]{2,1,0:T(8,128)} %param.15) | copy-start | bytes 147460
  197.5 252.9 %all-gather.7.cloned.1.call-start = ((), (), s32[]{:S(2)}) async-start(), calls=%async_computation.5 | async-start | bytes 2228224 | tf_op jit(solution)/shard_map/all_gather | solution.py:103
  339.6 13.4 %copy-start.2 = (f32[2,4,4096]{2,1,0:T(4,128)S(1)}, f32[2,4,4096]{2,1,0:T(4,128)}, u32[]{:S(2)}) copy-start(f32[2,4,4096]{2,1,0:T(4,128)} %param.12) | copy-start | bytes 393220
  391.1 0.5 copy-start.8
  391.1 0.6 copy-start.10
  391.6 0.6 copy-start.4
  393.1 249.2 %all-reduce.44.cloned.1.call-start = ((), (), s32[]{:S(2)}) async-start(), calls=%async_computation.8 | async-start | bytes 4194304
  477.5 1.9 copy-start.1
  508.6 1.9 copy-start.1
  517.5 125.9 %copy-start.7 = (f32[3,64,64]{2,1,0:T(8,128)S(1)}, f32[3,64,64]{2,1,0:T(8,128)}, u32[]{:S(2)}) copy-start(f32[3,64,64]{2,1,0:T(8,128)} %param.15) | copy-start | bytes 147460
  658.9 14.8 %copy-start.3 = (f32[2,4,4096]{2,1,0:T(4,128)S(1)}, f32[2,4,4096]{2,1,0:T(4,128)}, u32[]{:S(2)}) copy-start(f32[2,4,4096]{2,1,0:T(4,128)} %param.12) | copy-start | bytes 393220
  659.0 14.8 %copy-start.5 = (f32[2,4,4096]{2,1,0:T(4,128)S(1)}, f32[2,4,4096]{2,1,0:T(4,128)}, u32[]{:S(2)}) copy-start(f32[2,4,4096]{2,1,0:T(4,128)} %copy-done.4) | copy-start | bytes 393220
  659.0 14.8 %copy-start.9 = (f32[2]{0:T(128)S(1)}, f32[2]{0:T(128)}, u32[]{:S(2)}) copy-start(f32[2]{0:T(128)} %copy-done.8) | copy-start | bytes 28
  659.0 14.8 %copy-start.11 = (f32[2]{0:T(128)S(1)}, f32[2]{0:T(128)}, u32[]{:S(2)}) copy-start(f32[2]{0:T(128)} %copy-done.10) | copy-start | bytes 28
  660.8 11.3 %all-to-all-start.3 = ((f32[16,1,2048]{2,1,0:T(1,128)}), f32[16,1,2048]{2,1,0:T(1,128)S(1)}, u32[]{:S(2)}, u32[]{:S(2)}) async-start(f32[16,1,2048]{2,1,0:T(1,128)} %reshape.178), calls=%async_computation.3 | async-start | bytes 262144 | tf_op jit(solution)/shard_map/all_to_all | solution.py:94
Sparse Core Ops, SparseCore 0:
  10.1 57.9 all-gather.8
  70.9 59.4 all-gather.4
  197.6 124.5 all-reduce.41
  393.2 57.1 all-gather.6
  517.7 124.5 all-reduce.43
where the time goes:
time: 737 us; the launch traced here: 725 us
  waiting for transfers between devices  430 us (58%)
  blocking collectives  113 us (15%)
  other arithmetic  103 us (14%)
  local copies, waits for them, and re-layouts  53.4 us (7%)
  between operations  14.4 us (2%)
    unnamed x7, waiting for transfers between devices  248 us
    all_gather x2, waiting for transfers between devices, apply_kernel(): whole = lax.all_gather(planes, 'orb', axis=1, tiled=True)  117 us
    all_gather x1, waiting for transfers between devices, shards(): full_potential = lax.all_gather(potential, 'orb', axis=0, tiled=True)  57.4 us
    reduce_sum x22, other arithmetic, cell_inner(): return jnp.sum(left_field * right_field, axis=(1, 2))  47.2 us
    psum x1, blocking collectives, shards(): lax.psum((cell_inner(trials, trials), cell_inner(trials, mapped), cell_in...  37.9 us
    psum x1, blocking collectives, shards(): gram_matrix = lax.psum(local_gram, 'orb') / float(G ** 3)  37.8 us
    all_to_all x2, blocking collectives, coulomb_planes(): lax.all_to_all(plane_view, 'orb', split_axis=2, concat_axis=1, tiled=True)  25.2 us
    unnamed x37, local copies, waits for them, and re-layouts  18.8 us
  transfers between devices with their start and end apart: 6, of which 6 were waited for; matrix products, arithmetic and copies ran while one was open for 1% of the time, Pallas kernels for 0%

commit v1 on v0

v1 whole, which is shorter than its diff:
```python
import functools
import jax
import jax.numpy as jnp
from jax import lax
from jax.experimental import pallas as pl
from jax.experimental.pallas import tpu as pltpu
from jax.sharding import PartitionSpec as P

LOW = 2
HIGH = 3
CENTER = 4.25
CHUNK = 16
HIGHEST = lax.Precision.HIGHEST


def orbital_shifts(orbital_ids, freq_index, energies, frequencies):
    energy_slots = lax.broadcasted_iota(jnp.int32, (1, energies.shape[0]), 1)
    picked_energy = jnp.sum(
        jnp.where(orbital_ids[:, None] == energy_slots, energies[None, :], 0.0), axis=1
    )
    freq_slots = lax.broadcasted_iota(jnp.int32, (1, frequencies.shape[0]), 1)
    picked_freq = jnp.sum(
        jnp.where(freq_index[:, None] == freq_slots, frequencies[None, :], 0.0), axis=1
    )
    return picked_freq - picked_energy


def spread_kernel(orbs, rows, src_ref, dst_ref):
    lane = lax.broadcasted_iota(jnp.int32, (orbs, 128), 1)
    first_half = lane < 64

    def body(r8, carry):
        for i in range(8):
            r = r8 * 8 + i
            pair = src_ref[pl.ds(r, orbs, stride=rows), :]
            turned = pltpu.roll(pair, 64, 1)
            dst_ref[2 * r] = jnp.where(first_half, pair, turned)
            dst_ref[2 * r + 1] = jnp.where(first_half, turned, pair)
        return carry

    lax.fori_loop(0, rows // 8, body, 0)


def krylov_kernel(
    slab, lines, grid_width, group,
    flag_ref, o_hbm, v_ref, d_ref, sh_ref,
    u1_hbm, u2_hbm, pay_ref,
    o_s, b_s, u1_s, u2_s, in_sem, out_sem,
):
    window = slab + LOW + HIGH
    lane = lax.broadcasted_iota(jnp.int32, (8, 128), 1) % grid_width
    at_low = lane == 0
    at_high = lane == grid_width - 1
    zero = jnp.zeros((8, 128), jnp.float32)
    pieces = 3
    cuts = [window * k // pieces for k in range(pieces + 1)]
    copies = [
        pltpu.make_async_copy(
            o_hbm.at[pl.ds(cuts[k], cuts[k + 1] - cuts[k])],
            o_s.at[pl.ds(cuts[k], cuts[k + 1] - cuts[k])],
            in_sem.at[k],
        )
        for k in range(pieces)
    ]
    for copy in copies:
        copy.start()

    def clear(w, carry):
        for ref in (b_s, u1_s, u2_s):
            ref[w, 0] = zero
            ref[w, grid_width + 1] = zero
        return carry

    lax.fori_loop(0, window, clear, 0)

    def row_of(ref, w, y0, i):
        per = y0 // lines
        return ref[per + i // lines, pl.ds(w * lines + i % lines, 1), :]

    def products(w, carry):
        def chunk(c, carry):
            y0 = c * CHUNK
            for i in range(CHUNK):
                b_s[w, y0 + i + 1] = o_s[w, y0 + i] * row_of(v_ref, w, y0, i)
            return carry

        return lax.fori_loop(0, grid_width // CHUNK, chunk, carry)

    for k in range(pieces):
        copies[k].wait()
        lax.fori_loop(cuts[k], cuts[k + 1], products, 0)

    def tree(terms):
        while len(terms) > 1:
            terms = [a + b for a, b in zip(terms[::2], terms[1::2])] + (
                [terms[-1]] if len(terms) % 2 else []
            )
        return terms[0]

    def apply(src, dst, w, carry, pairs):
        def chunk(c, carry):
            y0 = c * CHUNK
            rows = [src[w, y0 + i] for i in range(CHUNK + 2)]
            terms = [[] for _ in carry]
            for i in range(CHUNK):
                mid = rows[i + 1]
                around = (rows[i] + rows[i + 2]) + (
                    src[w - 1, y0 + i + 1] + src[w + 1, y0 + i + 1]
                )
                around = around + (
                    jnp.where(at_low, 0.0, pltpu.roll(mid, 1, 1))
                    + jnp.where(at_high, 0.0, pltpu.roll(mid, 127, 1))
                )
                new = row_of(d_ref, w, y0, i) * mid - around
                dst[w, y0 + i + 1] = new
                both = (mid, new)
                for list_at, (a, b) in zip(terms, pairs):
                    list_at.append(both[a] * both[b])
            return tuple(old + tree(t) for old, t in zip(carry, terms))

        return lax.fori_loop(0, grid_width // CHUNK, chunk, carry)

    def wipe(dst, w):
        def chunk(y, carry):
            dst[w, y + 1] = zero
            return carry

        lax.fori_loop(0, grid_width, chunk, 0)

    def halo(src, dst, w, outside):
        @pl.when(outside)
        def _():
            wipe(dst, w)

        @pl.when(jnp.logical_not(outside))
        def _():
            apply(src, dst, w, (), ())

    first = flag_ref[0]
    own = (LOW, LOW + slab)
    halo(b_s, u1_s, LOW - 1, first < 1)
    m0, m1, m2 = lax.fori_loop(
        *own, lambda w, c: apply(b_s, u1_s, w, c, ((0, 0), (0, 1), (1, 1))), (zero,) * 3
    )
    copy_u1 = pltpu.make_async_copy(
        u1_s.at[pl.ds(LOW, slab), pl.ds(1, grid_width)], u1_hbm, out_sem.at[0]
    )
    copy_u1.start()
    halo(b_s, u1_s, LOW + slab, first + slab >= grid_width)
    halo(b_s, u1_s, LOW + slab + 1, first + slab + 1 >= grid_width)
    m3, m4 = lax.fori_loop(
        *own, lambda w, c: apply(u1_s, u2_s, w, c, ((0, 1), (1, 1))), (zero,) * 2
    )
    copy_u2 = pltpu.make_async_copy(
        u2_s.at[pl.ds(LOW, slab), pl.ds(1, grid_width)], u2_hbm, out_sem.at[1]
    )
    copy_u2.start()
    halo(u1_s, u2_s, LOW + slab, first + slab >= grid_width)

    def last(w, carry):
        def chunk(c, carry):
            y0 = c * CHUNK
            rows = [u2_s[w, y0 + i + 1] for i in range(CHUNK + 1)]
            terms = []
            for i in range(CHUNK):
                mid = rows[i]
                above = (rows[i + 1] + u2_s[w + 1, y0 + i + 1]) + jnp.where(
                    at_high, 0.0, pltpu.roll(mid, 127, 1)
                )
                terms.append(mid * (row_of(d_ref, w, y0, i) * mid - 2.0 * above))
            return carry + tree(terms)

        return lax.fori_loop(0, grid_width // CHUNK, chunk, carry)

    m5 = lax.fori_loop(*own, last, zero)
    for k, moment in enumerate((m0, m1, m2, m3, m4, m5)):
        for peer in range(group):
            for row in range(8):
                pay_ref[peer, 8 * k + (row ^ peer) : 8 * k + (row ^ peer) + 1, :] = moment[
                    row : row + 1
                ]
    for peer in range(group):
        pay_ref[peer, 48:56, :] = sh_ref[...]
    copy_u1.wait()
    copy_u2.wait()


def combine_kernel(
    slab, lines, grid_width, group,
    *refs,
):
    pays = refs[:group]
    (v_ref, o_ref, u1_ref, u2_ref, ones_ref, cy_ref, cz_ref, out_ref, coef_s, field_s) = refs[group:]
    step = pl.program_id(0)
    chunks = out_ref.shape[0]

    @pl.when(step == 0)
    def _():
        total = pays[0][0:48]
        for pay in pays[1:]:
            total = total + pay[0:48]
        total = jnp.dot(total, ones_ref[...], precision=HIGHEST, preferred_element_type=jnp.float32)
        halves = 8 // group
        shift = jnp.concatenate(
            [pays[k][48 + half : 49 + half] for half in range(halves) for k in range(group)], axis=0
        )
        m = [total[8 * k : 8 * k + 8] for k in range(6)]
        inv = 1.0 / m[0]
        mu = [None] + [m[k] * inv * (8.0**-k) for k in range(1, 6)]
        sigma = 0.25 * (shift + CENTER)
        k00 = mu[1] + sigma
        k01 = mu[2] + sigma * mu[1]
        k11 = mu[3] + sigma * mu[2]
        k02 = k11
        k12 = mu[4] + sigma * mu[3]
        k22 = mu[5] + sigma * mu[4]
        r0 = 1.0 / k00
        l10 = k01 * r0
        l20 = k02 * r0
        d1 = k11 - l10 * k01
        t = k12 - l20 * k01
        l21 = t / d1
        d2 = k22 - l20 * k02 - l21 * t
        z1 = mu[1] - l10
        z2 = mu[2] - l20 - l21 * z1
        y2 = z2 / d2
        y1 = z1 / d1 - l21 * y2
        y0 = r0 - l10 * y1 - l20 * y2
        coef_s[0] = -0.25 * y0
        coef_s[1] = (-0.25 / 8.0) * y1
        coef_s[2] = (-0.25 / 64.0) * y2

    c0, c1, c2 = coef_s[0], coef_s[1], coef_s[2]
    w = step + LOW
    for y in range(grid_width):
        o = o_ref[0, y]
        b = o * v_ref[y // lines, pl.ds(w * lines + y % lines, 1), :]
        field_s[8 * y : 8 * y + 8, :] = o * (c0 * b + (c1 * u1_ref[0, y] + c2 * u2_ref[0, y]))
    planes = jnp.dot(cy_ref[...], field_s[...], precision=HIGHEST, preferred_element_type=jnp.float32)
    planes = jnp.dot(planes, cz_ref[...], precision=HIGHEST, preferred_element_type=jnp.float32)
    for k in range(chunks):
        out_ref[k, pl.ds(step * lines, lines), :] = planes[k * lines : (k + 1) * lines]


def whole_vmem():
    return pl.BlockSpec(memory_space=pltpu.VMEM)


def shards(n, cores, trials, orbitals, potential, coulomb, energies, frequencies, orbital_ids, freq_index):
    count, planes, cells = trials.shape
    held = orbitals.shape[0]
    width = coulomb.shape[1]
    lines = width // n
    group = 8 // held
    slab = width // group
    window = slab + LOW + HIGH
    send_planes = -(-window * lines // 8) * 8 // lines
    f32 = jnp.float32
    me = lax.axis_index("orb")
    core = lax.axis_index("trial")
    place = me % group
    rows = cells // 128
    each = held // cores

    def swap(x):
        return lax.ppermute(x, "trial", [(k, (k + 1) % cores) for k in range(cores)])

    def peer(x, k):
        return lax.ppermute(x, "orb", [(i, i ^ k) for i in range(n)])

    def exchange(x):
        return lax.all_to_all(x, "orb", split_axis=0, concat_axis=0, tiled=True)

    mine = lax.dynamic_slice_in_dim(orbitals, core * each, each, 0).astype(f32)
    mine = mine.reshape(each, width * rows, 128)
    mine = jnp.pad(mine, ((0, 0), (LOW * rows, HIGH * rows), (0, 0)))
    parts = []
    for k in range(group):
        part = lax.dynamic_slice_in_dim(mine, (place ^ k) * slab * rows, window * rows, 1)
        parts.append(peer(part, k) if k else part)
    own_half = jnp.stack(parts, axis=1).reshape(each * group, window * rows, 128)
    other_half = swap(own_half)
    both = jnp.concatenate([own_half, other_half], axis=0)
    orbs = both.shape[0]
    spread_orbitals = pl.pallas_call(
        functools.partial(spread_kernel, orbs, window * rows),
        out_shape=jax.ShapeDtypeStruct((window * width, orbs, 128), f32),
        in_specs=[whole_vmem()],
        out_specs=whole_vmem(),
        compiler_params=pltpu.CompilerParams(vmem_limit_bytes=40 * 2**20),
        name="spread_orbitals",
    )(both.reshape(orbs * window * rows, 128)).reshape(window, width, orbs, 128)

    shifts = orbital_shifts(orbital_ids, freq_index, energies, frequencies)
    shifts = jnp.where(core == 0, shifts, jnp.roll(shifts, -each))
    shift_rows = jnp.broadcast_to(jnp.pad(shifts, (0, 8 - held))[:, None], (8, 128))

    def lanes(x):
        x = x.reshape(count, planes, width, width)
        return x.transpose(1, 2, 0, 3).reshape(planes, n, lines, 128)

    pot = jnp.broadcast_to(potential[None], (count, planes, cells))
    send = jnp.stack([lanes(trials), lanes(2.0 * (3.0 - CENTER + pot))], 0)
    send = send.transpose(2, 0, 1, 3, 4).reshape(n, 2 * planes * lines, 128)
    got = exchange(send).reshape(n, 2, planes * lines, 128)
    trial_rows = got[:, 0].reshape(width * lines, 128)
    diag_rows = got[:, 1].reshape(width * lines, 128)

    def windows(x):
        x = jnp.pad(x, ((LOW * lines, (send_planes - LOW - slab) * lines), (0, 0)))
        return jnp.stack(
            [x[j * slab * lines : (j * slab + send_planes) * lines] for j in range(group)], 0
        )

    def to_all(x):
        return jnp.tile(x, (n // group, 1, 1))

    size = send_planes * lines
    got = exchange(to_all(jnp.concatenate([windows(trial_rows), windows(diag_rows)], axis=1)))
    trial_window = got[:, :size]
    diag_window = got[:, size:]

    flags = (place * slab).astype(jnp.int32).reshape(1)
    lane_trial = jnp.arange(128) // width
    ones = (lane_trial[:, None] == lane_trial[None, :]).astype(f32)
    cy = jnp.repeat(coulomb[1], orbs, axis=1)
    cz = jnp.kron(jnp.eye(count, dtype=f32), coulomb[2].T)
    cx = jnp.kron(coulomb[0], jnp.eye(lines, dtype=f32))

    def response(v):
        u_shape = jax.ShapeDtypeStruct((slab, width, orbs, 128), f32)
        any_spec = pl.BlockSpec(memory_space=pl.ANY)
        scratch = pltpu.VMEM((window, width + 2, orbs, 128), f32)
        u1, u2, pay = pl.pallas_call(
            functools.partial(krylov_kernel, slab, lines, width, group),
            out_shape=(u_shape, u_shape, jax.ShapeDtypeStruct((group, 56, 128), f32)),
            in_specs=[
                pl.BlockSpec(memory_space=pltpu.SMEM), any_spec, whole_vmem(), whole_vmem(), whole_vmem(),
            ],
            out_specs=(any_spec, any_spec, whole_vmem()),
            scratch_shapes=[
                pltpu.VMEM((window, width, orbs, 128), f32), scratch, scratch, scratch,
                pltpu.SemaphoreType.DMA((3,)), pltpu.SemaphoreType.DMA((2,)),
            ],
            compiler_params=pltpu.CompilerParams(vmem_limit_bytes=48 * 2**20),
            name="krylov",
        )(flags, spread_orbitals, v, diag_window, shift_rows)
        pays = [pay[0]] + [peer(pay[k], k) for k in range(1, group)]
        plane = (1, width, orbs, 128)
        part = pl.pallas_call(
            functools.partial(combine_kernel, slab, lines, width, group),
            grid=(slab,),
            out_shape=jax.ShapeDtypeStruct((n, slab * lines, 128), f32),
            in_specs=[whole_vmem()] * (group + 1)
            + [
                pl.BlockSpec(plane, lambda i: (i + LOW, 0, 0, 0)),
                pl.BlockSpec(plane, lambda i: (i, 0, 0, 0)),
                pl.BlockSpec(plane, lambda i: (i, 0, 0, 0)),
            ]
            + [whole_vmem()] * 3,
            out_specs=pl.BlockSpec((n, slab * lines, 128), lambda i: (0, 0, 0)),
            scratch_shapes=[pltpu.VMEM((3, 8, 128), f32), pltpu.VMEM((8 * width, 128), f32)],
            compiler_params=pltpu.CompilerParams(vmem_limit_bytes=40 * 2**20),
            name="combine",
        )(*pays, v, spread_orbitals, u1, u2, ones, cy, cz)
        got = exchange(part).reshape(n // group, width * lines, 128)
        return jnp.dot(cx, jnp.sum(got, axis=0), precision=HIGHEST)

    def fold(x):
        return jnp.dot(x, ones, precision=HIGHEST)

    mapped = response(trial_window)
    sums = jnp.stack(
        [jnp.sum(a * b, axis=0) for a, b in ((trial_rows, trial_rows), (trial_rows, mapped), (mapped, mapped))], 0
    )
    sums = jnp.broadcast_to(jnp.pad(sums, ((0, 5), (0, 0)))[None], (group, 8, 128))
    got = exchange(to_all(jnp.concatenate([windows(mapped), sums], axis=1)))
    totals = fold(jnp.sum(got[:, size:], axis=0))
    center = totals[1:2] / totals[0:1]
    spread = jnp.sqrt(totals[2:3] / totals[0:1])
    first_window = (got[:, :size] - center * trial_window) / spread
    first = (mapped - center * trial_rows) / spread
    second = 2.0 * (response(first_window) - center * first) / spread - trial_rows
    other = swap(second)

    def turn(x):
        return jnp.concatenate([x[..., width:], x[..., :width]], axis=-1)

    pairs = (
        (second, second), (second, turn(second)), (second, other), (second, turn(other)), (other, other), (other, turn(other)),
    )
    sums = jnp.pad(jnp.stack([jnp.sum(a * b, axis=0) for a, b in pairs], 0), ((0, 2), (0, 0)))
    sums = jnp.broadcast_to(sums[None], (n, 8, 128))
    per = planes * lines
    got = exchange(jnp.concatenate([second.reshape(n, per, 128), sums], axis=1))
    block = got[:, :per]
    block_other = swap(block)
    gram = fold(jnp.sum(got[:, per:], axis=0)) / float(width * width * width)
    s = [[gram[k, 0], gram[k, width]] for k in range(6)]
    aa = ((s[0][0], s[1][0]), (s[1][0], s[0][1]))
    bb = ((s[4][0], s[5][0]), (s[5][0], s[4][1]))
    ab = ((s[2][0], s[3][0]), (s[3][1], s[2][1]))
    is_low = core == 0
    matrix = [[None] * 4 for _ in range(4)]
    for i in range(2):
        for j in range(2):
            matrix[i][j] = jnp.where(is_low, aa[i][j], bb[i][j])
            matrix[2 + i][2 + j] = jnp.where(is_low, bb[i][j], aa[i][j])
            matrix[i][2 + j] = jnp.where(is_low, ab[i][j], ab[j][i])
            matrix[2 + j][i] = matrix[i][2 + j]
    size4 = 4
    low = [[None] * size4 for _ in range(size4)]
    inverse = [[jnp.float32(0)] * size4 for _ in range(size4)]
    for i in range(size4):
        for j in range(i + 1):
            value = matrix[i][j] - sum((low[i][k] * low[j][k] for k in range(j)), jnp.float32(0))
            low[i][j] = jnp.sqrt(value) if i == j else value / low[j][j]
    for j in range(size4):
        inverse[j][j] = 1.0 / low[j][j]
        for i in range(j + 1, size4):
            inverse[i][j] = -sum((low[i][k] * inverse[k][j] for k in range(j, i)), jnp.float32(0)) / low[i][i]

    def pick(i, j):
        top = inverse[i][j]
        here, there = (j, (j + 2) % 4)
        return jnp.where(is_low, top if i < 2 else 0.0, inverse[i + 2][there])

    def spread_lanes(a, b):
        return jnp.where(lane_trial == 0, a, b)[None, None, :]

    result = (
        spread_lanes(pick(0, 0), pick(1, 1)) * block
        + spread_lanes(pick(0, 1), pick(1, 0)) * turn(block)
        + spread_lanes(pick(0, 2), pick(1, 3)) * block_other
        + spread_lanes(pick(0, 3), pick(1, 2)) * turn(block_other)
    )
    result = result.reshape(n, planes, lines, count, width).transpose(3, 1, 0, 2, 4)
    return result.reshape(count, planes, cells)


def solution(mesh):
    n, cores = mesh.shape["orb"], mesh.shape["trial"]
    in_specs = (
        P("trial", "orb", None), P("orb", None, None), P("orb", None), P(), P(), P(), P("orb"), P("orb"),
    )
    return jax.shard_map(
        functools.partial(shards, n, cores),
        mesh=mesh, in_specs=in_specs, out_specs=P("trial", "orb", None), check_vma=False,
    )
```

time: 737 us -> 271 us (0.37); the launches traced: 725 us -> 270 us
  waiting for transfers between devices: 430 us -> 47.7 us
  other arithmetic: 103 us -> 11.2 us
  Pallas kernels: 0 us -> 84.8 us
  blocking collectives: 113 us -> 53.5 us
  starting transfers between devices: 4.02 us -> 30.1 us
  local copies, waits for them, and re-layouts: 53.4 us -> 28.6 us
    unnamed x7 -> x0, waiting for transfers between devices: 248 us -> none
    all_gather x3 -> x0, waiting for transfers between devices: 174 us -> none  [the longest x2 117 us: apply_kernel(): whole = lax.all_gather(planes, 'orb', axis=1, tiled=True)]
    pallas_call x0 -> x5, Pallas kernels: none -> 84.8 us  [the longest x2 51.4 us: response(): pl.pallas_call(functools.partial(krylov_kernel, slab, lines, width, group...]
    psum x2 -> x0, blocking collectives: 75.7 us -> none  [the longest x1 37.9 us: shards(): lax.psum((cell_inner(trials, trials), cell_inner(trials, mapped), cell_in...]
    reduce_sum x22 -> x6, other arithmetic: 47.2 us -> 0.3 us  [the longest x2 0.21 us: shards(): jnp.sum(a * b, axis=0)]
    ppermute x0 -> x12, waiting for transfers between devices: none -> 36.2 us  [the longest x9 33.3 us: peer(): return lax.ppermute(x, 'orb', [(i, i ^ k) for i in range(n)])]
    slice x36 -> x8, local copies, waits for them, and re-layouts: 27.7 us -> 3.08 us  [the longest x1 1.42 us: shards(): diag_window = got[:, size:]]
    sub x5 -> x0, other arithmetic: 18.9 us -> none  [the longest x4 18.8 us: one_orbital(): return (accumulated - density * solved, None)]
  transfers between devices with their start and end apart: 6 -> 15, of which waited for: 6 -> 13; matrix products, arithmetic and copies ran while one was open for 1% -> 7% of each run, Pallas kernels for 0% -> 3%
where the time goes in v1:
time: 271 us; the launch traced here: 270 us
  Pallas kernels  84.8 us (31%)
  blocking collectives  53.5 us (20%)
  waiting for transfers between devices  47.7 us (18%)
  starting transfers between devices  30.1 us (11%)
  local copies, waits for them, and re-layouts  28.6 us (11%)
  between operations  12.6 us (5%)
  other arithmetic  11.2 us (4%)
    all_to_all x3, blocking collectives, exchange(): return lax.all_to_all(x, 'orb', split_axis=0, concat_axis=0, tiled=True)  53.5 us
    pallas_call x2, Pallas kernels, response(): pl.pallas_call(functools.partial(krylov_kernel, slab, lines, width, group...  51.4 us
    ppermute x9, waiting for transfers between devices, peer(): return lax.ppermute(x, 'orb', [(i, i ^ k) for i in range(n)])  33.3 us
    pallas_call x2, Pallas kernels, response(): pl.pallas_call(functools.partial(combine_kernel, slab, lines, width, grou...  25.9 us
    all_to_all x3, starting transfers between devices, exchange(): return lax.all_to_all(x, 'orb', split_axis=0, concat_axis=0, tiled=True)  19.2 us
    all_to_all x3, waiting for transfers between devices, exchange(): return lax.all_to_all(x, 'orb', split_axis=0, concat_axis=0, tiled=True)  11.5 us
    unnamed x24, local copies, waits for them, and re-layouts  11.1 us
    ppermute x9, starting transfers between devices, peer(): return lax.ppermute(x, 'orb', [(i, i ^ k) for i in range(n)])  10.7 us
  transfers between devices with their start and end apart: 15, of which 13 were waited for; matrix products, arithmetic and copies ran while one was open for 7% of the time, Pallas kernels for 3%

profile of v1, /device:TPU:0, one launch (start us, length us, event | category | flops | bytes accessed | tf_op | source)
XLA Modules:
  0.0 269.8 jit_solution(641843993982427463)
XLA Ops:
  0.0 1.2 reshape.149
  1.2 0.2 copy.43
  1.4 0.2 stack_reshape.6
  1.6 0.9 add_multiply_fusion
  2.7 0.2 stack_reshape.7
  3.0 0.8 copy.32
  3.8 8.3 %all-to-all-start = ((f32[16,32,128]{2,1,0:T(8,128)}), f32[16,32,128]{2,1,0:T(8,128)S(1)}, u32[]{:S(2)}, u32[]{:S(2)}) async-start(f32[16,32,128]{2,1,0:T(8,128)} %copy.32), calls=%async_computation | async-start | bytes 524288 | tf_op jit(solution)/shard_map/all_to_all | solution.py:272
  12.1 9.9 %all-to-all-done = f32[16,32,128]{2,1,0:T(8,128)S(1)} async-done(((f32[16,32,128]{2,1,0:T(8,128)}), f32[16,32,128]{2,1,0:T(8,128)S(1)}, u32[]{:S(2)}, u32[]{:S(2)}) %all-to-all-start) | async-done | bytes 262176 | tf_op jit(solution)/shard_map/all_to_all | solution.py:272
  22.1 1.2 tile.8
  23.3 4.4 %all-to-all-start.1 = ((f32[16,176,128]{2,1,0:T(8,128)}), f32[16,176,128]{2,1,0:T(8,128)}, u32[]{:S(2)}, u32[]{:S(2)}) async-start(f32[16,176,128]{2,1,0:T(8,128)} %bitcast.23), calls=%async_computation.1 | async-start | bytes 2883584 | tf_op jit(solution)/shard_map/all_to_all | solution.py:272
  27.8 0.2 reshape.145
  28.2 1.8 collective-permute-start
  30.1 1.5 collective-permute-start.1
  31.5 0.3 collective-permute-start.2
  31.8 18.4 %collective-permute-done = f32[1,672,128]{2,1,0:T(8,128)S(1)} collective-permute-done((f32[1,672,128]{2,1,0:T(8,128)S(1)}, f32[1,672,128]{2,1,0:T(8,128)S(1)}, u32[]{:S(2)}, u32[]{:S(2)}) %collective-permute-start) | collective-permute-done | bytes 344096 | tf_op jit(solution)/shard_map/ppermute | solution.py:269
  50.2 4.4 %collective-permute-done.1 = f32[1,672,128]{2,1,0:T(8,128)S(1)} collective-permute-done((f32[1,672,128]{2,1,0:T(8,128)S(1)}, f32[1,672,128]{2,1,0:T(8,128)S(1)}, u32[]{:S(2)}, u32[]{:S(2)}) %collective-permute-start.1) | collective-permute-done | bytes 344096 | tf_op jit(solution)/shard_map/ppermute | solution.py:269
  54.6 6.5 %collective-permute-done.2 = f32[1,672,128]{2,1,0:T(8,128)} collective-permute-done((f32[1,672,128]{2,1,0:T(8,128)S(1)}, f32[1,672,128]{2,1,0:T(8,128)}, u32[]{:S(2)}, u32[]{:S(2)}) %collective-permute-start.2) | collective-permute-done | bytes 344096 | tf_op jit(solution)/shard_map/ppermute | solution.py:269
  61.2 1.2 maximum_bitcast_fusion
  62.7 0.2 fusion.22
  62.8 0.2 fusion.23
  63.0 0.6 fusion.31
  63.6 1.3 broadcast_select_fusion
  65.0 0.6 collective-permute-done.3
  65.7 1.5 pad_maximum_fusion
  67.2 7.6 %spread_orbitals.1 = f32[1344,8,128]{2,1,0:T(8,128)S(1)} custom-call(f32[5376,128]{1,0:T(8,128)S(1)} %bitcast.117), custom_call_target="tpu_custom_call" | custom-call | tf_op jit(solution)/shard_map/spread_orbitals/pallas_call | solution.py:285
  74.9 2.5 copy-done.1
  77.3 1.4 fusion.25
  78.8 25.7 %krylov.2 = (f32[16,64,8,128]{3,2,1,0:T(8,128)S(1)}, f32[16,64,8,128]{3,2,1,0:T(8,128)}, f32[4,56,128]{2,1,0:T(8,128)S(1)}) custom-call(s32[1]{0:T(128)} %bitcast.1.flag_ref, f32[21,64,8,128]{3,2,1,0:T(8,128)} %bitcast.113, f32[16,88,128]{2,1,0:T(8,128)S(1)} %get-tuple-element.26.v_ref.refs_4_, f32[16,88,128]{2,1,0:T(8,128)S(1)} %get-tuple-element.25.d_ref, ...), custom_call_target="tpu_custom_call" | custom-call | tf_op jit(solution)/shard_map/krylov/pallas_call | solution.py:334
  104.5 2.0 copy-done.3
  106.5 0.2 collective-permute-start.4
  106.7 3.4 %collective-permute-start.6 = (f32[56,128]{1,0:T(8,128)S(1)}, f32[56,128]{1,0:T(8,128)S(1)}, u32[]{:S(2)}, u32[]{:S(2)}) collective-permute-start(f32[56,128]{1,0:T(8,128)S(1)} %get-tuple-element.58), channel_id=1, source_target_pairs={{0,6},{2,4},{4,2},{6,0},{8,14},{10,12},{12,10},{14,8},{16,22},{18,... | collective-permute-start | bytes 86024 | tf_op jit(solution)/shard_map/ppermute | solution.py:269
  110.3 0.1 mul.246.refs_10_
  110.6 1.3 collective-permute-done.6.refs_3_
  111.9 2.2 copy-done.4
  114.1 2.2 copy-done.5
  116.3 13.3 %combine.2 = f32[16,64,128]{2,1,0:T(8,128)} custom-call(f32[56,128]{1,0:T(8,128)S(1)} %get-tuple-element.61.refs_0_, f32[56,128]{1,0:T(8,128)S(1)} %collective-permute-done.4.refs_1_, f32[56,128]{1,0:T(8,128)S(1)} %collective-permute-done.5.refs_2_, f32[56,128]{1,0:T(8,128)S(1)} %collective-permute-done.6.refs_3_, ...), custom_call_target="tpu_custom_call" | custom-call | tf_op jit(solution)/shard_map/combine/pallas_call | solution.py:350
  129.7 6.5 %all-to-all-start.2 = ((f32[16,64,128]{2,1,0:T(8,128)}), f32[16,64,128]{2,1,0:T(8,128)S(1)}, u32[]{:S(2)}, u32[]{:S(2)}) async-start(f32[16,64,128]{2,1,0:T(8,128)} %combine.2), calls=%async_computation.2 | async-start | bytes 1048576 | tf_op jit(solution)/shard_map/all_to_all | solution.py:272
  136.2 3.9 %broadcast_multiply_fusion = f32[64,4,64,4]{3,2,1,0:T(8,128)} fusion(f32[4,4]{1,0:T(4,128)S(1)} %fusion.21, f32[64,64]{1,0:T(8,128)S(1)} %get-tuple-element.63), kind=kLoop, calls=%fused_computation | loop fusion | flops 65536 | bytes 278592 | tf_op jit(solution)/shard_map/jit(kron)/mul | solution.py:328
  140.1 8.3 %mul.234 = f32[256,256]{1,0:T(8,128)S(1)} reshape(f32[64,4,64,4]{3,2,1,0:T(8,128)} %broadcast_multiply_fusion) | data formatting | bytes 524288 | tf_op jit(solution)/shard_map/jit(kron)/mul | solution.py:328
  148.4 1.6 all-to-all-done.2
  150.0 0.4 multiply_reduce_fusion.6
  150.6 24.4 %all_to_all.30 = f32[16,96,128]{2,1,0:T(8,128)S(1)} all-to-all(f32[16,96,128]{2,1,0:T(8,128)S(1)} %bitcast.118), channel_id=1, replica_groups=mesh['orb'=16,'trial'=2] {'orb'}, dimensions={0} | all-to-all | bytes 1572864 | tf_op jit(solution)/shard_map/all_to_all | solution.py:272
  175.0 0.2 fusion.9
  175.2 1.2 fusion.3.v_ref.refs_4_
  176.4 25.7 %krylov.3 = (f32[16,64,8,128]{3,2,1,0:T(8,128)S(1)}, f32[16,64,8,128]{3,2,1,0:T(8,128)}, f32[4,56,128]{2,1,0:T(8,128)S(1)}) custom-call(s32[1]{0:T(128)} %bitcast.1.flag_ref, f32[21,64,8,128]{3,2,1,0:T(8,128)} %bitcast.115, f32[16,88,128]{2,1,0:T(8,128)S(1)} %fusion.3.v_ref.refs_4_, f32[16,88,128]{2,1,0:T(8,128)S(1)} %get-tuple-element.25.d_ref, ...), custom_call_target="tpu_custom_call" | custom-call | tf_op jit(solution)/shard_map/krylov/pallas_call | solution.py:334
  202.1 0.7 collective-permute-start.7
  202.9 0.6 collective-permute-start.8
  203.4 2.3 collective-permute-start.9
  205.7 0.4 collective-permute-done.7.refs_1_
  206.1 0.6 collective-permute-done.8.refs_2_
  206.7 1.5 collective-permute-done.9.refs_3_
  208.2 2.2 copy-done.2
  210.4 12.5 %combine.3 = f32[16,64,128]{2,1,0:T(8,128)S(1)} custom-call(f32[56,128]{1,0:T(8,128)S(1)} %get-tuple-element.57.refs_0_, f32[56,128]{1,0:T(8,128)S(1)} %collective-permute-done.7.refs_1_, f32[56,128]{1,0:T(8,128)S(1)} %collective-permute-done.8.refs_2_, f32[56,128]{1,0:T(8,128)S(1)} %collective-permute-done.9.refs_3_, ...), custom_call_target="tpu_custom_call" | custom-call | tf_op jit(solution)/shard_map/combine/pallas_call | solution.py:350
  222.9 16.5 %all_to_all.31 = f32[16,64,128]{2,1,0:T(8,128)S(1)} all-to-all(f32[16,64,128]{2,1,0:T(8,128)S(1)} %combine.3), channel_id=1, replica_groups=mesh['orb'=16,'trial'=2] {'orb'}, dimensions={0} | all-to-all | bytes 1048576 | tf_op jit(solution)/shard_map/all_to_all | solution.py:272
  239.4 0.4 fusion.2
  240.0 1.2 collective-permute-done.10
  241.3 0.2 multiply_reduce_fusion
  241.6 12.7 %all_to_all.32 = f32[16,24,128]{2,1,0:T(8,128)S(1)} all-to-all(f32[16,24,128]{2,1,0:T(8,128)S(1)} %pad_maximum_fusion.2), channel_id=1, replica_groups=mesh['orb'=16,'trial'=2] {'orb'}, dimensions={0} | all-to-all | bytes 393216 | tf_op jit(solution)/shard_map/all_to_all | solution.py:272
  254.2 0.2 convolution_multiply_fusion
  254.4 0.7 fusion.30
  267.4 1.0 collective-permute-done.11
  268.5 0.2 fusion.7
  268.7 0.2 reshape.156
  269.0 0.9 reshape.157
  (74 shorter events, 2.4 us)
Async XLA Ops:
  0.0 27.7 %copy-start = (bf16[2,64,4096]{2,1,0:T(8,128)(2,1)S(1)}, bf16[2,64,4096]{2,1,0:T(8,128)(2,1)}, u32[]{:S(2)}) copy-start(bf16[2,64,4096]{2,1,0:T(8,128)(2,1)} %param.9) | copy-start | bytes 3145732
  3.8 18.2 %all-to-all-start = ((f32[16,32,128]{2,1,0:T(8,128)}), f32[16,32,128]{2,1,0:T(8,128)S(1)}, u32[]{:S(2)}, u32[]{:S(2)}) async-start(f32[16,32,128]{2,1,0:T(8,128)} %copy.32), calls=%async_computation | async-start | bytes 524288 | tf_op jit(solution)/shard_map/all_to_all | solution.py:272
  23.3 54.1 %all-to-all-start.1 = ((f32[16,176,128]{2,1,0:T(8,128)}), f32[16,176,128]{2,1,0:T(8,128)}, u32[]{:S(2)}, u32[]{:S(2)}) async-start(f32[16,176,128]{2,1,0:T(8,128)} %bitcast.23), calls=%async_computation.1 | async-start | bytes 2883584 | tf_op jit(solution)/shard_map/all_to_all | solution.py:272
  28.2 34.2 %copy-start.7 = (f32[3,64,64]{2,1,0:T(8,128)S(1)}, f32[3,64,64]{2,1,0:T(8,128)}, u32[]{:S(2)}) copy-start(f32[3,64,64]{2,1,0:T(8,128)} %param.11) | copy-start | bytes 147460
  28.2 21.9 %collective-permute-start = (f32[1,672,128]{2,1,0:T(8,128)S(1)}, f32[1,672,128]{2,1,0:T(8,128)S(1)}, u32[]{:S(2)}, u32[]{:S(2)}) collective-permute-start(f32[1,672,128]{2,1,0:T(8,128)S(1)} %get-tuple-element.30), channel_id=1, source_target_pairs={{0,2},{2,0},{4,6},{6,4},{8,10},{10,8},{12,14},{14,12},{16,18},{18,... | collective-permute-start | bytes 1032200 | tf_op jit(solution)/shard_map/ppermute | solution.py:269
  30.1 24.5 %collective-permute-start.1 = (f32[1,672,128]{2,1,0:T(8,128)S(1)}, f32[1,672,128]{2,1,0:T(8,128)S(1)}, u32[]{:S(2)}, u32[]{:S(2)}) collective-permute-start(f32[1,672,128]{2,1,0:T(8,128)S(1)} %get-tuple-element.29), channel_id=1, source_target_pairs={{0,4},{2,6},{4,0},{6,2},{8,12},{10,14},{12,8},{14,10},{16,20},{18,... | collective-permute-start | bytes 1032200 | tf_op jit(solution)/shard_map/ppermute | solution.py:269
  31.5 29.6 %collective-permute-start.2 = (f32[1,672,128]{2,1,0:T(8,128)S(1)}, f32[1,672,128]{2,1,0:T(8,128)}, u32[]{:S(2)}, u32[]{:S(2)}) collective-permute-start(f32[1,672,128]{2,1,0:T(8,128)S(1)} %get-tuple-element.28), channel_id=1, source_target_pairs={{0,6},{2,4},{4,2},{6,0},{8,14},{10,12},{12,10},{14,8},{16,22},{18,... | collective-permute-start | bytes 1032200 | tf_op jit(solution)/shard_map/ppermute | solution.py:269
  54.6 6.5 %copy-start.6 = (f32[1,672,128]{2,1,0:T(8,128)}, f32[1,672,128]{2,1,0:T(8,128)S(1)}, u32[]{:S(2)}) copy-start(f32[1,672,128]{2,1,0:T(8,128)S(1)} %collective-permute-done.1) | copy-start | bytes 1032196
  61.1 1.5 copy-start.8
  61.1 1.5 copy-start.9
  61.1 1.7 copy-start.10
  61.1 1.7 copy-start.11
  62.4 3.3 %collective-permute-start.3 = (f32[4,672,128]{2,1,0:T(8,128)S(1)}, f32[4,672,128]{2,1,0:T(8,128)}, u32[]{:S(2)}, u32[]{:S(2)}) collective-permute-start(f32[4,672,128]{2,1,0:T(8,128)S(1)} %maximum_bitcast_fusion), channel_id=1, source_target_pairs={{0,1},{1,0},{2,3},{3,2},{4,5},{5,4},{6,7},{7,6},{8,9},{9,8},{10,11... | collective-permute-start | bytes 4128776 | tf_op jit(solution)/shard_map/ppermute | solution.py:266
  74.8 2.5 copy-start.1
  104.5 2.0 copy-start.3
  106.5 3.9 %collective-permute-start.4 = (f32[56,128]{1,0:T(8,128)S(1)}, f32[56,128]{1,0:T(8,128)S(1)}, u32[]{:S(2)}, u32[]{:S(2)}) collective-permute-start(f32[56,128]{1,0:T(8,128)S(1)} %get-tuple-element.60), channel_id=1, source_target_pairs={{0,2},{2,0},{4,6},{6,4},{8,10},{10,8},{12,14},{14,12},{16,18},{18,... | collective-permute-start | bytes 86024 | tf_op jit(solution)/shard_map/ppermute | solution.py:269
  106.7 3.9 %collective-permute-start.5 = (f32[56,128]{1,0:T(8,128)S(1)}, f32[56,128]{1,0:T(8,128)S(1)}, u32[]{:S(2)}, u32[]{:S(2)}) collective-permute-start(f32[56,128]{1,0:T(8,128)S(1)} %get-tuple-element.59), channel_id=1, source_target_pairs={{0,4},{2,6},{4,0},{6,2},{8,12},{10,14},{12,8},{14,10},{16,20},{18,... | collective-permute-start | bytes 86024 | tf_op jit(solution)/shard_map/ppermute | solution.py:269
  106.7 5.2 %collective-permute-start.6 = (f32[56,128]{1,0:T(8,128)S(1)}, f32[56,128]{1,0:T(8,128)S(1)}, u32[]{:S(2)}, u32[]{:S(2)}) collective-permute-start(f32[56,128]{1,0:T(8,128)S(1)} %get-tuple-element.58), channel_id=1, source_target_pairs={{0,6},{2,4},{4,2},{6,0},{8,14},{10,12},{12,10},{14,8},{16,22},{18,... | collective-permute-start | bytes 86024 | tf_op jit(solution)/shard_map/ppermute | solution.py:269
  111.9 2.2 copy-start.4
  114.1 2.2 copy-start.5
  129.7 20.3 %all-to-all-start.2 = ((f32[16,64,128]{2,1,0:T(8,128)}), f32[16,64,128]{2,1,0:T(8,128)S(1)}, u32[]{:S(2)}, u32[]{:S(2)}) async-start(f32[16,64,128]{2,1,0:T(8,128)} %combine.2), calls=%async_computation.2 | async-start | bytes 1048576 | tf_op jit(solution)/shard_map/all_to_all | solution.py:272
  202.1 3.9 %collective-permute-start.7 = (f32[56,128]{1,0:T(8,128)S(1)}, f32[56,128]{1,0:T(8,128)S(1)}, u32[]{:S(2)}, u32[]{:S(2)}) collective-permute-start(f32[56,128]{1,0:T(8,128)S(1)} %get-tuple-element.56), channel_id=1, source_target_pairs={{0,2},{2,0},{4,6},{6,4},{8,10},{10,8},{12,14},{14,12},{16,18},{18,... | collective-permute-start | bytes 86024 | tf_op jit(solution)/shard_map/ppermute | solution.py:269
  202.9 3.9 %collective-permute-start.8 = (f32[56,128]{1,0:T(8,128)S(1)}, f32[56,128]{1,0:T(8,128)S(1)}, u32[]{:S(2)}, u32[]{:S(2)}) collective-permute-start(f32[56,128]{1,0:T(8,128)S(1)} %get-tuple-element.55), channel_id=1, source_target_pairs={{0,4},{2,6},{4,0},{6,2},{8,12},{10,14},{12,8},{14,10},{16,20},{18,... | collective-permute-start | bytes 86024 | tf_op jit(solution)/shard_map/ppermute | solution.py:269
  203.4 4.8 %collective-permute-start.9 = (f32[56,128]{1,0:T(8,128)S(1)}, f32[56,128]{1,0:T(8,128)S(1)}, u32[]{:S(2)}, u32[]{:S(2)}) collective-permute-start(f32[56,128]{1,0:T(8,128)S(1)} %get-tuple-element.54), channel_id=1, source_target_pairs={{0,6},{2,4},{4,2},{6,0},{8,14},{10,12},{12,10},{14,8},{16,22},{18,... | collective-permute-start | bytes 86024 | tf_op jit(solution)/shard_map/ppermute | solution.py:269
  208.2 2.2 copy-start.2
  239.8 1.4 collective-permute-start.10
  267.0 1.4 collective-permute-start.11

commit v2 on v0

v2 whole, which is shorter than its diff:
```python
import functools
import jax
import jax.numpy as jnp
from jax import lax
from jax.experimental import pallas as pl
from jax.experimental.pallas import tpu as pltpu
from jax.sharding import PartitionSpec as P

LOW = 2
HIGH = 3
CENTER = 4.25
ORBS = 16
SHIFT_LANE = 12
MOMENTS = 6
HIGHEST = lax.Precision.HIGHEST
F32 = jnp.float32
MIB = 2**20


def dot(a, b):
    return jnp.dot(a, b, precision=HIGHEST, preferred_element_type=F32)


def halves(rows, width, value=1.0):
    a = lax.broadcasted_iota(jnp.int32, (128, 128), 0) // width
    b = lax.broadcasted_iota(jnp.int32, (128, 128), 1) // width
    return jnp.where(a == b, 1.0, 0.0)


def tree(terms):
    while len(terms) > 1:
        odd = [terms[-1]] if len(terms) % 2 else []
        terms = [a + b for a, b in zip(terms[::2], terms[1::2])] + odd
    return terms[0]


def orbital_shifts(orbital_ids, freq_index, energies, frequencies):
    energy_slots = lax.broadcasted_iota(jnp.int32, (1, energies.shape[0]), 1)
    picked_energy = jnp.sum(
        jnp.where(orbital_ids[:, None] == energy_slots, energies[None, :], 0.0), axis=1
    )
    freq_slots = lax.broadcasted_iota(jnp.int32, (1, frequencies.shape[0]), 1)
    picked_freq = jnp.sum(
        jnp.where(freq_index[:, None] == freq_slots, frequencies[None, :], 0.0), axis=1
    )
    return picked_freq - picked_energy


def spread_kernel(window, pairs, own_ref, other_ref, dst_ref):
    half = ORBS // 2
    rows = window * pairs
    first_half = lax.broadcasted_iota(jnp.int32, (ORBS, 128), 1) < 64

    def body(w, carry):
        for i in range(pairs):
            at = pl.ds(w * pairs + i, half, stride=rows)
            pair = jnp.concatenate([own_ref[at, :], other_ref[at, :]], axis=0)
            turned = pltpu.roll(pair, 64, 1)
            dst_ref[w, 2 * i] = jnp.where(first_half, pair, turned).astype(jnp.bfloat16)
            dst_ref[w, 2 * i + 1] = jnp.where(first_half, turned, pair).astype(jnp.bfloat16)
        return carry

    lax.fori_loop(0, window, body, 0)


def krylov_kernel(slab, lines, width, group, filtered, *refs):
    flag_ref, o_ref, d_ref, sh_ref, t_ref = refs[:5]
    if filtered:
        m_ref, u1_ref, u2_ref, pay_ref, v_ref, cs_ref, b_s = refs[5:]
    else:
        u1_ref, u2_ref, pay_ref, b_s = refs[5:]
        v_ref = t_ref
    window = slab + LOW + HIGH
    lane = lax.broadcasted_iota(jnp.int32, (ORBS, 128), 1)
    at_low = lane % width == 0
    at_high = lane % width == width - 1
    zero = jnp.zeros((ORBS, 128), F32)
    n = t_ref.shape[0]

    if filtered:
        base = m_ref.shape[1] - 8
        total = m_ref[0, base : base + 8, :]
        for k in range(1, n):
            total = total + m_ref[k, base : base + 8, :]
        total = dot(total, halves(8, width))
        center = total[1:2] / total[0:1]
        inverse = 1.0 / jnp.sqrt(total[2:3] / total[0:1])
        cs_ref[0:1] = center
        cs_ref[1:2] = inverse
        used = v_ref.shape[1]
        for k in range(n):
            v_ref[k] = (m_ref[k, 0:used, :] - center * t_ref[k, 0:used, :]) * inverse

    def v_row(w, y):
        return v_ref[y // lines, pl.ds(w * lines + y % lines, 1), :]

    def d_row(w, y):
        return d_ref[y % lines, y // lines, pl.ds(w, 1), :]

    def products(w, carry):
        for y in range(width):
            b_s[w, y] = o_ref[w, y].astype(F32) * v_row(w, y)
        return carry

    lax.fori_loop(0, window, products, 0)

    def apply(src, src_at, dst, dst_at, w, carry, pairs):
        rows = [zero] + [src[w - src_at, y] for y in range(width)] + [zero]
        terms = [[] for _ in carry]
        for y in range(width):
            mid = rows[y + 1]
            around = (rows[y] + rows[y + 2]) + (src[w - 1 - src_at, y] + src[w + 1 - src_at, y])
            around = around + (
                jnp.where(at_low, 0.0, pltpu.roll(mid, 1, 1))
                + jnp.where(at_high, 0.0, pltpu.roll(mid, 127, 1))
            )
            new = d_row(w, y) * mid - around
            dst[w - dst_at, y] = new
            both = (mid, new)
            for list_at, (a, b) in zip(terms, pairs):
                list_at.append(both[a] * both[b])
        return tuple(old + tree(t) for old, t in zip(carry, terms))

    def halo(src, src_at, dst, dst_at, w, outside):
        @pl.when(outside)
        def _():
            dst[w - dst_at] = jnp.zeros((width, ORBS, 128), F32)

        @pl.when(jnp.logical_not(outside))
        def _():
            apply(src, src_at, dst, dst_at, w, (), ())

    first = flag_ref[0]
    own = (LOW, LOW + slab)
    halo(b_s, 0, u1_ref, 1, LOW - 1, first < 1)
    m0, m1, m2 = lax.fori_loop(
        *own, lambda w, c: apply(b_s, 0, u1_ref, 1, w, c, ((0, 0), (0, 1), (1, 1))), (zero,) * 3
    )
    halo(b_s, 0, u1_ref, 1, LOW + slab, first + slab >= width)
    halo(b_s, 0, u1_ref, 1, LOW + slab + 1, first + slab + 1 >= width)
    m3, m4 = lax.fori_loop(
        *own, lambda w, c: apply(u1_ref, 1, u2_ref, LOW, w, c, ((0, 1), (1, 1))), (zero,) * 2
    )
    halo(u1_ref, 1, u2_ref, LOW, LOW + slab, first + slab >= width)

    def last(w, carry):
        rows = [u2_ref[w - LOW, y] for y in range(width)] + [zero]
        terms = []
        for y in range(width):
            mid = rows[y]
            above = (rows[y + 1] + u2_ref[w + 1 - LOW, y]) + jnp.where(
                at_high, 0.0, pltpu.roll(mid, 127, 1)
            )
            terms.append(mid * (d_row(w, y) * mid - 2.0 * above))
        return carry + tree(terms)

    m5 = lax.fori_loop(*own, last, zero)
    column = lax.broadcasted_iota(jnp.int32, (128, 128), 1)
    half = lax.broadcasted_iota(jnp.int32, (128, 128), 0) // width
    packed = sh_ref[...]
    for k, moment in enumerate((m0, m1, m2, m3, m4, m5)):
        packed = packed + dot(moment, jnp.where(column == 2 * k + half, 1.0, 0.0))
    for peer in range(group):
        pay_ref[peer] = packed


def combine_kernel(slab, lines, width, group, pay_ref, v_ref, o_ref, u1_ref, u2_ref, cy_ref, cz_ref, out_ref, field_s):
    chunks = out_ref.shape[0]
    total = pay_ref[0]
    for k in range(1, group):
        total = total + pay_ref[k]
    row = lax.broadcasted_iota(jnp.int32, (128, 128), 0)
    half = lax.broadcasted_iota(jnp.int32, (128, 128), 1) // width
    m = [dot(total, jnp.where(row == 2 * k + half, 1.0, 0.0)) for k in range(MOMENTS)]
    shift = dot(total, jnp.where(row == SHIFT_LANE, 1.0, 0.0))
    inv = 1.0 / m[0]
    mu = [None] + [m[k] * inv * (8.0**-k) for k in range(1, MOMENTS)]
    sigma = 0.25 * (shift + CENTER)
    k00 = mu[1] + sigma
    k01 = mu[2] + sigma * mu[1]
    k11 = mu[3] + sigma * mu[2]
    k02 = k11
    k12 = mu[4] + sigma * mu[3]
    k22 = mu[5] + sigma * mu[4]
    r0 = 1.0 / k00
    l10 = k01 * r0
    l20 = k02 * r0
    d1 = k11 - l10 * k01
    t = k12 - l20 * k01
    l21 = t / d1
    d2 = k22 - l20 * k02 - l21 * t
    z1 = mu[1] - l10
    z2 = mu[2] - l20 - l21 * z1
    y2 = z2 / d2
    y1 = z1 / d1 - l21 * y2
    y0 = r0 - l10 * y1 - l20 * y2
    c0 = -0.25 * y0
    c1 = (-0.25 / 8.0) * y1
    c2 = (-0.25 / 64.0) * y2

    def plane(x, carry):
        w = x + LOW
        for y in range(width):
            o = o_ref[w, y].astype(F32)
            b = o * v_ref[y // lines, pl.ds(w * lines + y % lines, 1), :]
            share = o * (c0 * b + (c1 * u1_ref[x + LOW - 1, y] + c2 * u2_ref[x, y]))
            field_s[8 * y : 8 * y + 8, :] = share[0:8] + share[8:16]
        planes = dot(dot(cy_ref[...], field_s[...]), cz_ref[...])
        for k in range(chunks):
            out_ref[k, pl.ds(x * lines, lines), :] = planes[k * lines : (k + 1) * lines]
        return carry

    lax.fori_loop(0, slab, plane, 0)


def gathered(got_ref, cx_ref, group):
    n, rows, _ = got_ref.shape
    parts = []
    for j in range(group):
        parts.append(tree([got_ref[q * group + j] for q in range(n // group)]))
    return dot(cx_ref[...], jnp.concatenate(parts, axis=0))


def mapped_kernel(slab, lines, width, group, got_ref, cx_ref, t_ref, mapped_ref, pay_ref):
    n, size, _ = pay_ref.shape
    mapped = gathered(got_ref, cx_ref, group)
    mapped_ref[...] = mapped
    t = t_ref[...]
    sums = [jnp.sum(a * b, axis=0, keepdims=True) for a, b in ((t, t), (t, mapped), (mapped, mapped))]
    window = (slab + LOW + HIGH) * lines
    for k in range(n):
        start = (k % group) * slab * lines - LOW * lines
        low, high = max(start, 0), min(start + window, width * lines)
        pay_ref[k] = jnp.zeros((size, 128), F32)
        pay_ref[k, low - start : high - start, :] = mapped_ref[low:high, :]
        for i, s in enumerate(sums):
            pay_ref[k, size - 8 + i : size - 7 + i, :] = s


def second_kernel(group, got_ref, cx_ref, t_ref, mapped_ref, cs_ref, second_ref):
    again = gathered(got_ref, cx_ref, group)
    center, inverse = cs_ref[0:1], cs_ref[1:2]
    t = t_ref[...]
    first = (mapped_ref[...] - center * t) * inverse
    second_ref[...] = 2.0 * (again - center * first) * inverse - t


def turn(x):
    return pltpu.roll(x, 64, x.ndim - 1)


def gram_kernel(per, second_ref, other_ref, pay_ref):
    n, size, _ = pay_ref.shape
    a, b = second_ref[...], other_ref[...]
    a1, b1 = turn(a), turn(b)
    pairs = ((a, a), (a, a1), (a, b), (a, b1), (b, b), (b, b1))
    sums = [jnp.sum(p * q, axis=0, keepdims=True) for p, q in pairs]
    block = jnp.concatenate(sums + [jnp.zeros((8 - len(sums), 128), F32)], axis=0)
    for k in range(n):
        pay_ref[k, 0:per, :] = second_ref[k * per : (k + 1) * per, :]
        pay_ref[k, size - 8 : size, :] = block


def final_kernel(per, width, flag_ref, got_ref, other_ref, out_ref):
    n, size, _ = got_ref.shape
    total = tree([got_ref[k, size - 8 : size, :] for k in range(n)])
    total = dot(total, halves(8, width)) / float(width**3)
    swapped = turn(total)
    lane = lax.broadcasted_iota(jnp.int32, (1, 128), 1)
    in_first = lane < width
    is_low = jnp.zeros((1, 128), jnp.int32) + flag_ref[1] == 0

    def entry(k, t):
        here, there = total[k : k + 1], swapped[k : k + 1]
        return jnp.where(in_first, here, there) if t == 0 else jnp.where(in_first, there, here)

    aa = ((entry(0, 0), entry(1, 0)), (entry(1, 0), entry(0, 1)))
    bb = ((entry(4, 0), entry(5, 0)), (entry(5, 0), entry(4, 1)))
    ab = ((entry(2, 0), entry(3, 0)), (entry(3, 1), entry(2, 1)))
    m = [[None] * 4 for _ in range(4)]
    for i in range(2):
        for j in range(2):
            m[i][j] = jnp.where(is_low, aa[i][j], bb[i][j])
            m[2 + i][2 + j] = jnp.where(is_low, bb[i][j], aa[i][j])
            m[2 + j][i] = jnp.where(is_low, ab[i][j], ab[j][i])
    low = [[None] * 4 for _ in range(4)]
    inv = [[jnp.zeros((1, 128), F32)] * 4 for _ in range(4)]
    for j in range(4):
        pivot = m[j][j]
        for k in range(j):
            pivot = pivot - low[j][k] * low[j][k]
        inv[j][j] = 1.0 / jnp.sqrt(pivot)
        for i in range(j + 1, 4):
            value = m[i][j]
            for k in range(j):
                value = value - low[i][k] * low[j][k]
            low[i][j] = value * inv[j][j]
    for j in range(4):
        for i in range(j + 1, 4):
            value = low[i][j] * inv[j][j]
            for k in range(j + 1, i):
                value = value + low[i][k] * inv[k][j]
            inv[i][j] = -value * inv[i][i]

    def pick(i, j):
        return jnp.where(is_low, inv[i][j], inv[2 + i][(j + 2) % 4])

    c = [
        jnp.where(in_first, pick(0, a), pick(1, b)) for a, b in ((0, 1), (1, 0), (2, 3), (3, 2))
    ]
    for k in range(n):
        a, b = got_ref[k, 0:per, :], other_ref[k]
        out_ref[k] = (c[0] * a + c[1] * turn(a)) + (c[2] * b + c[3] * turn(b))


def vmem():
    return pl.BlockSpec(memory_space=pltpu.VMEM)


def smem():
    return pl.BlockSpec(memory_space=pltpu.SMEM)


def call(kernel, name, shapes, inputs, scratch=(), limit=16, in_smem=()):
    return pl.pallas_call(
        kernel,
        out_shape=shapes,
        in_specs=[smem() if k in in_smem else vmem() for k in range(len(inputs))],
        out_specs=jax.tree.map(lambda _: vmem(), shapes),
        scratch_shapes=scratch,
        compiler_params=pltpu.CompilerParams(vmem_limit_bytes=limit * MIB),
        name=name,
    )(*inputs)


def shape(*dims):
    return jax.ShapeDtypeStruct(dims, F32)


def up8(x):
    return -(-x // 8) * 8


def shards(n, cores, trials, orbitals, potential, coulomb, energies, frequencies, orbital_ids, freq_index):
    count, planes, cells = trials.shape
    held = orbitals.shape[0]
    width = coulomb.shape[1]
    lines = width // n
    group = ORBS // held
    slab = width // group
    window = slab + LOW + HIGH
    me = lax.axis_index("orb")
    core = lax.axis_index("trial")
    place = me % group
    pairs = cells // 128
    each = held // cores
    groups = [list(range(q * group, (q + 1) * group)) for q in range(n // group)]

    def swap(x):
        return lax.ppermute(x, "trial", [(k, (k + 1) % cores) for k in range(cores)])

    def exchange(x):
        return lax.all_to_all(x, "orb", split_axis=0, concat_axis=0, tiled=True)

    def exchange_group(x):
        return lax.all_to_all(
            x, "orb", split_axis=0, concat_axis=0, tiled=True, axis_index_groups=groups
        )

    mine = lax.dynamic_slice_in_dim(orbitals, core * each, each, 0).astype(F32)
    mine = mine.reshape(each, width * pairs, 128)
    mine = jnp.pad(mine, ((0, 0), (LOW * pairs, HIGH * pairs), (0, 0)))
    sent = jnp.stack(
        [mine[:, j * slab * pairs : (j * slab + window) * pairs] for j in range(group)], axis=0
    )
    own_half = exchange_group(sent.reshape(group, each * window * pairs, 128))
    own_half = own_half.reshape(ORBS // 2 * window * pairs, 128)
    other_half = swap(own_half)
    spread_orbitals = call(
        functools.partial(spread_kernel, window, pairs),
        "spread_orbitals",
        jax.ShapeDtypeStruct((window, width, ORBS, 128), jnp.bfloat16),
        (own_half, other_half),
        limit=16,
    )
    shifts = orbital_shifts(orbital_ids, freq_index, energies, frequencies)
    shifts = jnp.where(core == 0, shifts, jnp.roll(shifts, -each))
    slot_rows = [(k // each) * (ORBS // 2) + place * each + k % each for k in range(held)]
    row = lax.broadcasted_iota(jnp.int32, (ORBS, 128), 0)
    lane = lax.broadcasted_iota(jnp.int32, (ORBS, 128), 1)
    shift_rows = sum(
        jnp.where((row == slot_rows[k]) & (lane == SHIFT_LANE), shifts[k], 0.0) for k in range(held)
    )

    t_rows = trials.reshape(count, planes, width, width).transpose(1, 2, 0, 3)
    t_rows = t_rows.reshape(planes, n, lines, 128).transpose(1, 0, 2, 3).reshape(n, planes * lines, 128)
    diag = 2.0 * (3.0 - CENTER + potential)
    shared = lines % (2 * cores) == 0
    kept = lines // 2 // cores if shared else lines
    if shared:
        d_rows = diag.reshape(planes, n, cores, kept, 128)
        d_rows = lax.dynamic_index_in_dim(d_rows, core, 2, keepdims=False)
    else:
        d_rows = jnp.tile(diag.reshape(planes, n, lines, width), (1, 1, 1, 128 // width))
    d_rows = d_rows.transpose(1, 0, 2, 3).reshape(n, planes * kept, 128)
    got = exchange(jnp.concatenate([t_rows, d_rows], axis=1))
    trial_rows = got[:, : planes * lines].reshape(width * lines, 128)
    diag_rows = got[:, planes * lines :].reshape(width * kept, 128)

    def windows(x, per):
        x = jnp.pad(x, ((LOW * per, HIGH * per), (0, 0)))
        return jnp.stack([x[j * slab * per : (j * slab + window) * per] for j in range(group)], 0)

    used = window * lines
    size = up8(used + window * kept)
    both = jnp.concatenate([windows(trial_rows, lines), windows(diag_rows, kept)], axis=1)
    both = jnp.pad(both, ((0, 0), (0, size - both.shape[1]), (0, 0)))
    trial_window = exchange(jnp.tile(both, (n // group, 1, 1)))
    diag_own = trial_window[:, used : used + window * kept].reshape(n, window, kept, 128)
    diag_own = diag_own.transpose(2, 0, 1, 3)
    if shared:
        diag_other = swap(diag_own)
        low, high = jnp.where(core == 0, diag_own, diag_other), jnp.where(core == 0, diag_other, diag_own)
        both = jnp.concatenate([low, high], axis=0)
        both = jnp.stack(
            [jnp.tile(both[..., h * width : (h + 1) * width], (1, 1, 1, 2)) for h in range(2)], axis=1
        )
        diag_window = both.reshape(lines, n, window, 128)
    else:
        diag_window = diag_own

    flags = jnp.stack([place * slab, core]).astype(jnp.int32)
    cy = jnp.repeat(coulomb[1], 8, axis=1)
    cz = jnp.kron(jnp.eye(count, dtype=F32), coulomb[2].T)
    wide = lax.broadcasted_iota(jnp.int32, (width * lines, width), 0) // lines
    wide = (wide == lax.broadcasted_iota(jnp.int32, (width * lines, width), 1)).astype(F32)
    cx = jnp.dot(jnp.dot(wide, coulomb[0], precision=HIGHEST), wide.T, precision=HIGHEST)
    a = lax.broadcasted_iota(jnp.int32, cx.shape, 0) % lines
    b = lax.broadcasted_iota(jnp.int32, cx.shape, 1) % lines
    cx = jnp.where(a == b, cx, 0.0)

    def response(fields):
        filtered = len(fields) == 2
        shapes = [
            shape(slab + 3, width, ORBS, 128), shape(slab + 1, width, ORBS, 128), shape(group, ORBS, 128),
        ]
        if filtered:
            shapes += [shape(n, used, 128), shape(8, 128)]
        made = call(
            functools.partial(krylov_kernel, slab, lines, width, group, filtered),
            "krylov",
            tuple(shapes),
            (flags, spread_orbitals, diag_window, shift_rows, *fields),
            scratch=[pltpu.VMEM((window, width, ORBS, 128), F32)],
            limit=32,
            in_smem=(0,),
        )
        u1, u2, pay = made[:3]
        v = made[3] if filtered else fields[0]
        part = call(
            functools.partial(combine_kernel, slab, lines, width, group),
            "combine",
            shape(n, slab * lines, 128),
            (exchange_group(pay), v, spread_orbitals, u1, u2, cy, cz),
            scratch=[pltpu.VMEM((8 * width, 128), F32)],
            limit=32,
        )
        return exchange(part), (made[4] if filtered else None)

    got, _ = response((trial_window,))
    mapped, pay = call(
        functools.partial(mapped_kernel, slab, lines, width, group),
        "mapped",
        (shape(width * lines, 128), shape(n, up8(used) + 8, 128)),
        (got, cx, trial_rows),
    )
    got, scales = response((trial_window, exchange(pay)))
    second = call(
        functools.partial(second_kernel, group),
        "second",
        shape(width * lines, 128),
        (got, cx, trial_rows, mapped, scales),
    )
    per = planes * lines
    pay = call(functools.partial(gram_kernel, per), "gram", shape(n, up8(per) + 8, 128), (second, swap(second)))
    got = exchange(pay)
    result = call(
        functools.partial(final_kernel, per, width),
        "final",
        shape(n, per, 128),
        (flags, got, swap(got[:, :per])),
        in_smem=(0,),
    )
    result = result.reshape(n, planes, lines, count, width).transpose(3, 1, 0, 2, 4)
    return result.reshape(count, planes, cells)


def solution(mesh):
    n, cores = mesh.shape["orb"], mesh.shape["trial"]
    in_specs = (
        P("trial", "orb", None), P("orb", None, None), P("orb", None), P(), P(), P(), P("orb"), P("orb"),
    )
    return jax.shard_map(
        functools.partial(shards, n, cores),
        mesh=mesh, in_specs=in_specs, out_specs=P("trial", "orb", None), check_vma=False,
    )
```

time: 737 us -> 207 us (0.28); the launches traced: 725 us -> 206 us
  waiting for transfers between devices: 430 us -> 45.7 us
  other arithmetic: 103 us -> 7 us
  blocking collectives: 113 us -> 50.2 us
  Pallas kernels: 0 us -> 39.4 us
  starting transfers between devices: 4.02 us -> 26.6 us
  local copies, waits for them, and re-layouts: 53.4 us -> 33.5 us
  between operations: 14.4 us -> 0.62 us
    unnamed x7 -> x0, waiting for transfers between devices: 248 us -> none
    all_gather x3 -> x0, waiting for transfers between devices: 174 us -> none  [the longest x2 117 us: apply_kernel(): whole = lax.all_gather(planes, 'orb', axis=1, tiled=True)]
    psum x2 -> x0, blocking collectives: 75.7 us -> none  [the longest x1 37.9 us: shards(): lax.psum((cell_inner(trials, trials), cell_inner(trials, mapped), cell_in...]
    reduce_sum x22 -> x0, other arithmetic: 47.2 us -> none  [cell_inner(): return jnp.sum(left_field * right_field, axis=(1, 2))]
    pallas_call x0 -> x9, Pallas kernels: none -> 39.4 us  [call(): pl.pallas_call(kernel, out_shape=shapes, in_specs=[smem() if k in in_smem...]
    all_to_all x1 -> x5, waiting for transfers between devices: 7.76 us -> 41.8 us  [the longest x2 22.5 us: exchange_group(): lax.all_to_all(x, 'orb', split_axis=0, concat_axis=0, tiled=True, axis_in...]
    slice x36 -> x7, local copies, waits for them, and re-layouts: 27.7 us -> 1.42 us  [the longest x1 0.67 us: shards(): shifts = jnp.where(core == 0, shifts, jnp.roll(shifts, -each))]
    all_to_all x1 -> x5, starting transfers between devices: 3.51 us -> 26.4 us  [the longest x3 18.3 us: exchange(): return lax.all_to_all(x, 'orb', split_axis=0, concat_axis=0, tiled=True)]
  transfers between devices with their start and end apart: 6 -> 9, of which waited for: 6 -> 8; matrix products, arithmetic and copies ran while one was open for 1% -> 11% of each run, Pallas kernels for 0% -> 0%
where the time goes in v2:
time: 207 us; the launch traced here: 206 us
  blocking collectives  50.2 us (24%)
  waiting for transfers between devices  45.7 us (22%)
  Pallas kernels  39.4 us (19%)
  local copies, waits for them, and re-layouts  33.5 us (16%)
  starting transfers between devices  26.6 us (13%)
  other arithmetic  7 us (3%)
  matrix products  3.08 us (1%)
    all_to_all x3, blocking collectives, exchange(): return lax.all_to_all(x, 'orb', split_axis=0, concat_axis=0, tiled=True)  41.4 us
    pallas_call x9, Pallas kernels, call(): pl.pallas_call(kernel, out_shape=shapes, in_specs=[smem() if k in in_smem...  39.4 us
    all_to_all x2, waiting for transfers between devices, exchange_group(): lax.all_to_all(x, 'orb', split_axis=0, concat_axis=0, tiled=True, axis_in...  22.5 us
    unnamed x75, local copies, waits for them, and re-layouts  21.5 us
    all_to_all x3, waiting for transfers between devices, exchange(): return lax.all_to_all(x, 'orb', split_axis=0, concat_axis=0, tiled=True)  19.3 us
    all_to_all x3, starting transfers between devices, exchange(): return lax.all_to_all(x, 'orb', split_axis=0, concat_axis=0, tiled=True)  18.3 us
    all_to_all x1, blocking collectives, exchange_group(): lax.all_to_all(x, 'orb', split_axis=0, concat_axis=0, tiled=True, axis_in...  8.83 us
    all_to_all x2, starting transfers between devices, exchange_group(): lax.all_to_all(x, 'orb', split_axis=0, concat_axis=0, tiled=True, axis_in...  8.02 us
  transfers between devices with their start and end apart: 9, of which 8 were waited for; matrix products, arithmetic and copies ran while one was open for 11% of the time, Pallas kernels for 0%

profile of v2, /device:TPU:0, one launch (start us, length us, event | category | flops | bytes accessed | tf_op | source)
XLA Modules:
  0.0 206.1 jit_solution(4281573784797046933)
XLA Ops:
  0.0 1.0 add_multiply_fusion
  1.1 1.1 reshape.83
  2.6 0.7 copy.85
  3.4 8.3 %all-to-all-start.1 = ((f32[16,20,128]{2,1,0:T(8,128)}), f32[16,20,128]{2,1,0:T(8,128)S(1)}, u32[]{:S(2)}, u32[]{:S(2)}) async-start(f32[16,20,128]{2,1,0:T(8,128)} %copy.85), calls=%async_computation.1 | async-start | bytes 393216 | tf_op jit(solution)/shard_map/all_to_all | solution.py:363
  11.7 0.6 compare_convert_fusion
  12.7 0.7 fusion.28
  13.8 0.7 fusion.1
  14.5 0.7 fusion.9
  15.2 0.7 fusion.8
  15.9 0.7 fusion.7
  16.6 0.7 fusion.6
  17.3 0.7 fusion.5
  18.0 0.7 fusion.4
  18.7 0.7 fusion.3
  19.4 0.9 all-to-all-done.1
  20.3 4.0 %all-to-all-start = ((f32[8,416,128]{2,1,0:T(8,128)}), f32[8,416,128]{2,1,0:T(8,128)S(1)}, u32[]{:S(2)}, u32[]{:S(2)}) async-start(f32[8,416,128]{2,1,0:T(8,128)} %bitcast.17), calls=%async_computation | async-start | bytes 3407872 | tf_op jit(solution)/shard_map/all_to_all | solution.py:366
  24.7 21.2 %all-to-all-done = f32[8,416,128]{2,1,0:T(8,128)S(1)} async-done(((f32[8,416,128]{2,1,0:T(8,128)}), f32[8,416,128]{2,1,0:T(8,128)S(1)}, u32[]{:S(2)}, u32[]{:S(2)}) %all-to-all-start) | async-done | bytes 1703968 | tf_op jit(solution)/shard_map/all_to_all | solution.py:366
  45.8 0.9 tile.12
  46.7 5.7 %all-to-all-start.2 = ((f32[16,72,128]{2,1,0:T(8,128)}), f32[16,72,128]{2,1,0:T(8,128)S(1)}, u32[]{:S(2)}, u32[]{:S(2)}) async-start(f32[16,72,128]{2,1,0:T(8,128)} %bitcast.43), calls=%async_computation.2 | async-start | bytes 1179648 | tf_op jit(solution)/shard_map/all_to_all | solution.py:363
  52.4 1.5 broadcast_select_fusion.2
  53.9 0.6 fusion.27
  54.5 1.3 select_add_fusion.refs_3_
  55.8 0.8 broadcast_multiply_fusion
  56.6 0.7 broadcast_bitcast_fusion
  57.3 11.6 %all-to-all-done.2.refs_4_.v_ref = f32[16,72,128]{2,1,0:T(8,128)S(1)} async-done(((f32[16,72,128]{2,1,0:T(8,128)}), f32[16,72,128]{2,1,0:T(8,128)S(1)}, u32[]{:S(2)}, u32[]{:S(2)}) %all-to-all-start.2) | async-done | bytes 589856 | tf_op jit(solution)/shard_map/all_to_all | solution.py:363
  69.0 1.3 collective-permute-done.1
  70.7 0.3 tile.28
  71.3 0.3 tile.30
  71.8 1.6 copy-done.5
  73.4 4.4 %spread_orbitals.1.refs_1_.o_ref = bf16[13,64,16,128]{3,2,1,0:T(8,128)(2,1)S(1)} custom-call(f32[3328,128]{1,0:T(8,128)S(1)} %bitcast.156, f32[3328,128]{1,0:T(8,128)} %collective-permute-done.other_ref), custom_call_target="tpu_custom_call" | custom-call | tf_op jit(solution)/shard_map/spread_orbitals/pallas_call | solution.py:325
  77.8 10.0 %krylov.2 = (f32[11,64,16,128]{3,2,1,0:T(8,128)S(1)}, f32[9,64,16,128]{3,2,1,0:T(8,128)S(1)}, f32[8,16,128]{2,1,0:T(8,128)S(1)}) custom-call(s32[2]{0:T(128)S(1)} %pad_add_fusion.refs_0_.flag_ref, bf16[13,64,16,128]{3,2,1,0:T(8,128)(2,1)S(1)} %spread_orbitals.1.refs_1_.o_ref, f32[4,16,13,128]{3,2,1,0:T(8,128)S(1)} %bitcast.167, ...), custom_call_target="tpu_custom_call" | custom-call | tf_op jit(solution)/shard_map/krylov/pallas_call | solution.py:325
  87.8 2.5 %copy-done.6 = f32[11,64,16,128]{3,2,1,0:T(8,128)} copy-done((f32[11,64,16,128]{3,2,1,0:T(8,128)}, f32[11,64,16,128]{3,2,1,0:T(8,128)S(1)}, u32[]{:S(2)}) %copy-start.6) | copy-done | bytes 5767192
  90.3 2.2 %copy-done.8 = f32[9,64,16,128]{3,2,1,0:T(8,128)} copy-done((f32[9,64,16,128]{3,2,1,0:T(8,128)}, f32[9,64,16,128]{3,2,1,0:T(8,128)S(1)}, u32[]{:S(2)}) %copy-start.8) | copy-done | bytes 4718616
  92.5 0.6 copy-done.19
  93.1 4.0 %all-to-all-start.3 = ((f32[8,16,128]{2,1,0:T(8,128)}), f32[8,16,128]{2,1,0:T(8,128)}, u32[]{:S(2)}, u32[]{:S(2)}) async-start(f32[8,16,128]{2,1,0:T(8,128)} %copy-done.19), calls=%async_computation.3 | async-start | bytes 131072 | tf_op jit(solution)/shard_map/all_to_all | solution.py:366
  97.1 0.6 iota_and_fusion
  97.7 1.6 mul.39.cz_ref
  99.3 1.7 copy.91.cy_ref
  101.1 0.6 iota_shift-right-logical_fusion
  101.6 1.3 all-to-all-done.3.pay_ref
  102.9 1.1 copy-done.2
  104.0 2.6 %copy-done.7 = f32[11,64,16,128]{3,2,1,0:T(8,128)S(1)} copy-done((f32[11,64,16,128]{3,2,1,0:T(8,128)S(1)}, f32[11,64,16,128]{3,2,1,0:T(8,128)}, u32[]{:S(2)}) %copy-start.7) | copy-done | bytes 5767192
  106.6 2.3 %copy-done.9 = f32[9,64,16,128]{3,2,1,0:T(8,128)S(1)} copy-done((f32[9,64,16,128]{3,2,1,0:T(8,128)S(1)}, f32[9,64,16,128]{3,2,1,0:T(8,128)}, u32[]{:S(2)}) %copy-start.9) | copy-done | bytes 4718616
  109.0 0.9 copy-done.12
  109.9 0.8 copy-done.17
  110.7 6.3 %combine.2 = f32[16,32,128]{2,1,0:T(8,128)S(1)} custom-call(f32[8,16,128]{2,1,0:T(8,128)} %all-to-all-done.3.pay_ref, f32[16,72,128]{2,1,0:T(8,128)S(1)} %copy-done.2, bf16[13,64,16,128]{3,2,1,0:T(8,128)(2,1)S(1)} %spread_orbitals.1.refs_1_.o_ref, f32[11,64,16,128]{3,2,1,0:T(8,128)S(1)} %copy-done.7, f32[9,64,16,128]{3,2,1,0:T(8,128)S(1)} %copy-done.9, ...), custom_call_target="tpu_custom_call" | custom-call | tf_op jit(solution)/shard_map/combine/pallas_call | solution.py:325
  117.1 0.7 copy-done.14
  117.8 4.4 %all-to-all-start.4 = ((f32[16,32,128]{2,1,0:T(8,128)}), f32[16,32,128]{2,1,0:T(8,128)}, u32[]{:S(2)}, u32[]{:S(2)}) async-start(f32[16,32,128]{2,1,0:T(8,128)} %copy-done.14), calls=%async_computation.4 | async-start | bytes 524288 | tf_op jit(solution)/shard_map/all_to_all | solution.py:363
  122.2 1.1 fusion.10
  123.3 2.0 convolution_select_fusion.cx_ref
  125.3 6.8 %all-to-all-done.4.got_ref = f32[16,32,128]{2,1,0:T(8,128)} async-done(((f32[16,32,128]{2,1,0:T(8,128)}), f32[16,32,128]{2,1,0:T(8,128)}, u32[]{:S(2)}, u32[]{:S(2)}) %all-to-all-start.4) | async-done | bytes 262176 | tf_op jit(solution)/shard_map/all_to_all | solution.py:363
  132.1 0.9 copy-done.15
  133.0 1.4 mapped.1
  134.5 17.8 %all_to_all.45.refs_5_ = f32[16,64,128]{2,1,0:T(8,128)S(1)} all-to-all(f32[16,64,128]{2,1,0:T(8,128)S(1)} %get-tuple-element.18), channel_id=1, replica_groups=mesh['orb'=16,'trial'=2] {'orb'}, dimensions={0} | all-to-all | bytes 1048576 | tf_op jit(solution)/shard_map/all_to_all | solution.py:363
  152.3 10.5 %krylov.3 = (f32[11,64,16,128]{3,2,1,0:T(8,128)S(1)}, f32[9,64,16,128]{3,2,1,0:T(8,128)S(1)}, f32[8,16,128]{2,1,0:T(8,128)S(1)}, f32[16,52,128]{2,1,0:T(8,128)S(1)}, f32[8,128]{1,0:T(8,128)S(1)}) custom-call(s32[2]{0:T(128)S(1)} %pad_add_fusion.refs_0_.flag_ref, bf16[13,64,16,128]{3,2,1,0:T(8,128)(2,1)S(1)} %spread_orbitals.1.refs_1_.o_ref, ...), custom_call_target="tpu_custom_call" | custom-call | tf_op jit(solution)/shard_map/krylov/pallas_call | solution.py:325
  162.8 8.8 %all_to_all.46.pay_ref = f32[8,16,128]{2,1,0:T(8,128)S(1)} all-to-all(f32[8,16,128]{2,1,0:T(8,128)S(1)} %get-tuple-element.19), channel_id=1, replica_groups={{0,2,4,6,8,10,12,14},{16,18,20,22,24,26,28,30},{1,3,5,7,9,11,13,15},{17..., dimensions={0} | all-to-all | bytes 131072 | tf_op jit(solution)/shard_map/all_to_all | solution.py:366
  171.6 5.5 %combine.3 = f32[16,32,128]{2,1,0:T(8,128)S(1)} custom-call(f32[8,16,128]{2,1,0:T(8,128)S(1)} %all_to_all.46.pay_ref, f32[16,52,128]{2,1,0:T(8,128)S(1)} %get-tuple-element.20.v_ref, bf16[13,64,16,128]{3,2,1,0:T(8,128)(2,1)S(1)} %spread_orbitals.1.refs_1_.o_ref, f32[11,64,16,128]{3,2,1,0:T(8,128)S(1)} %get-tuple-element.21.u1_ref, ...), custom_call_target="tpu_custom_call" | custom-call | tf_op jit(solution)/shard_map/combine/pallas_call | solution.py:325
  177.1 11.3 %all_to_all.47.got_ref = f32[16,32,128]{2,1,0:T(8,128)S(1)} all-to-all(f32[16,32,128]{2,1,0:T(8,128)S(1)} %combine.3), channel_id=1, replica_groups=mesh['orb'=16,'trial'=2] {'orb'}, dimensions={0} | all-to-all | bytes 524288 | tf_op jit(solution)/shard_map/all_to_all | solution.py:363
  188.4 0.4 second.1.second_ref
  188.8 1.3 collective-permute-done.2.other_ref
  190.3 12.3 %all_to_all.48.got_ref = f32[16,24,128]{2,1,0:T(8,128)S(1)} all-to-all(f32[16,24,128]{2,1,0:T(8,128)S(1)} %gram.1), channel_id=1, replica_groups=mesh['orb'=16,'trial'=2] {'orb'}, dimensions={0} | all-to-all | bytes 393216 | tf_op jit(solution)/shard_map/all_to_all | solution.py:363
  202.7 1.3 collective-permute-done.3.other_ref
  204.0 0.9 final.1
  205.2 0.9 reshape.93
  (98 shorter events, 3.2 us)
Async XLA Ops:
  0.0 12.3 %copy-start.24 = (s32[2]{0:T(128)S(1)}, s32[2]{0:T(128)}, u32[]{:S(2)}) copy-start(s32[2]{0:T(128)} %param.14) | copy-start | bytes 28
  0.0 12.3 %copy-start.23 = (f32[32]{0:T(128)S(1)}, f32[32]{0:T(128)}, u32[]{:S(2)}) copy-start(f32[32]{0:T(128)} %param.12) | copy-start | bytes 388
  0.0 12.5 %copy-start.26 = (s32[2]{0:T(128)S(1)}, s32[2]{0:T(128)}, u32[]{:S(2)}) copy-start(s32[2]{0:T(128)} %param.15) | copy-start | bytes 28
  0.0 12.5 %copy-start.25 = (f32[8]{0:T(128)S(1)}, f32[8]{0:T(128)}, u32[]{:S(2)}) copy-start(f32[8]{0:T(128)} %param.13) | copy-start | bytes 100
  0.0 13.3 %copy-start.21 = (f32[3,64,64]{2,1,0:T(8,128)S(1)}, f32[3,64,64]{2,1,0:T(8,128)}, u32[]{:S(2)}) copy-start(f32[3,64,64]{2,1,0:T(8,128)} %param.11) | copy-start | bytes 147460
  0.0 13.5 %copy-start.20 = (bf16[2,64,4096]{2,1,0:T(8,128)(2,1)S(1)}, bf16[2,64,4096]{2,1,0:T(8,128)(2,1)}, u32[]{:S(2)}) copy-start(bf16[2,64,4096]{2,1,0:T(8,128)(2,1)} %param.9) | copy-start | bytes 3145732
  3.4 17.0 %all-to-all-start.1 = ((f32[16,20,128]{2,1,0:T(8,128)}), f32[16,20,128]{2,1,0:T(8,128)S(1)}, u32[]{:S(2)}, u32[]{:S(2)}) async-start(f32[16,20,128]{2,1,0:T(8,128)} %copy.85), calls=%async_computation.1 | async-start | bytes 393216 | tf_op jit(solution)/shard_map/all_to_all | solution.py:363
  20.3 25.5 %all-to-all-start = ((f32[8,416,128]{2,1,0:T(8,128)}), f32[8,416,128]{2,1,0:T(8,128)S(1)}, u32[]{:S(2)}, u32[]{:S(2)}) async-start(f32[8,416,128]{2,1,0:T(8,128)} %bitcast.17), calls=%async_computation | async-start | bytes 3407872 | tf_op jit(solution)/shard_map/all_to_all | solution.py:366
  24.5 31.3 %copy-start.22 = (f32[2,2]{1,0:T(2,128)S(1)}, f32[2,2]{1,0:T(2,128)}, u32[]{:S(2)}) copy-start(f32[2,2]{1,0:T(2,128)} %compare_convert_fusion) | copy-start | bytes 52
  45.8 24.6 %copy-start.4 = (f32[8,416,128]{2,1,0:T(8,128)}, f32[8,416,128]{2,1,0:T(8,128)S(1)}, u32[]{:S(2)}) copy-start(f32[8,416,128]{2,1,0:T(8,128)S(1)} %all-to-all-done) | copy-start | bytes 5111812
  46.7 22.1 %all-to-all-start.2 = ((f32[16,72,128]{2,1,0:T(8,128)}), f32[16,72,128]{2,1,0:T(8,128)S(1)}, u32[]{:S(2)}, u32[]{:S(2)}) async-start(f32[16,72,128]{2,1,0:T(8,128)} %bitcast.43), calls=%async_computation.2 | async-start | bytes 1179648 | tf_op jit(solution)/shard_map/all_to_all | solution.py:363
  53.8 17.9 %collective-permute-start = (f32[3328,128]{1,0:T(8,128)S(1)}, f32[3328,128]{1,0:T(8,128)}, u32[]{:S(2)}, u32[]{:S(2)}) collective-permute-start(f32[3328,128]{1,0:T(8,128)S(1)} %bitcast.155), channel_id=1, source_target_pairs={{0,1},{1,0},{2,3},{3,2},{4,5},{5,4},{6,7},{7,6},{8,9},{9,8},{10,11... | collective-permute-start | bytes 5111816 | tf_op jit(solution)/shard_map/ppermute | solution.py:360
  68.8 2.2 %copy-start = (f32[16,72,128]{2,1,0:T(8,128)}, f32[16,72,128]{2,1,0:T(8,128)S(1)}, u32[]{:S(2)}) copy-start(f32[16,72,128]{2,1,0:T(8,128)S(1)} %all-to-all-done.2.refs_4_.v_ref) | copy-start | bytes 1769476
  68.8 1.4 collective-permute-start.1
  71.7 6.0 %copy-start.10 = (f32[2,2,16,13,128]{4,3,2,1,0:T(8,128)}, f32[2,2,16,13,128]{4,3,2,1,0:T(8,128)S(1)}, u32[]{:S(2)}) copy-start(f32[2,2,16,13,128]{4,3,2,1,0:T(8,128)S(1)} %copy.88) | copy-start | bytes 1277956
  71.8 6.0 %copy-start.1 = (f32[16,72,128]{2,1,0:T(8,128)S(1)}, f32[16,72,128]{2,1,0:T(8,128)}, u32[]{:S(2)}) copy-start(f32[16,72,128]{2,1,0:T(8,128)} %copy-done) | copy-start | bytes 1769476
  71.8 1.7 copy-start.5
  87.8 2.5 %copy-start.6 = (f32[11,64,16,128]{3,2,1,0:T(8,128)}, f32[11,64,16,128]{3,2,1,0:T(8,128)S(1)}, u32[]{:S(2)}) copy-start(f32[11,64,16,128]{3,2,1,0:T(8,128)S(1)} %get-tuple-element.16.u1_ref) | copy-start | bytes 17301508
  90.3 2.2 %copy-start.8 = (f32[9,64,16,128]{3,2,1,0:T(8,128)}, f32[9,64,16,128]{3,2,1,0:T(8,128)S(1)}, u32[]{:S(2)}) copy-start(f32[9,64,16,128]{3,2,1,0:T(8,128)S(1)} %get-tuple-element.17.u2_ref) | copy-start | bytes 14155780
  92.5 0.6 copy-start.19
  93.1 9.8 %all-to-all-start.3 = ((f32[8,16,128]{2,1,0:T(8,128)}), f32[8,16,128]{2,1,0:T(8,128)}, u32[]{:S(2)}, u32[]{:S(2)}) async-start(f32[8,16,128]{2,1,0:T(8,128)} %copy-done.19), calls=%async_computation.3 | async-start | bytes 131072 | tf_op jit(solution)/shard_map/all_to_all | solution.py:366
  102.9 1.1 copy-start.2
  104.0 2.6 %copy-start.7 = (f32[11,64,16,128]{3,2,1,0:T(8,128)S(1)}, f32[11,64,16,128]{3,2,1,0:T(8,128)}, u32[]{:S(2)}) copy-start(f32[11,64,16,128]{3,2,1,0:T(8,128)} %copy-done.6) | copy-start | bytes 17301508
  106.6 2.3 %copy-start.9 = (f32[9,64,16,128]{3,2,1,0:T(8,128)S(1)}, f32[9,64,16,128]{3,2,1,0:T(8,128)}, u32[]{:S(2)}) copy-start(f32[9,64,16,128]{3,2,1,0:T(8,128)} %copy-done.8) | copy-start | bytes 14155780
  109.0 0.9 copy-start.12
  109.9 0.8 copy-start.17
  117.1 0.7 copy-start.14
  117.8 14.3 %all-to-all-start.4 = ((f32[16,32,128]{2,1,0:T(8,128)}), f32[16,32,128]{2,1,0:T(8,128)}, u32[]{:S(2)}, u32[]{:S(2)}) async-start(f32[16,32,128]{2,1,0:T(8,128)} %copy-done.14), calls=%async_computation.4 | async-start | bytes 524288 | tf_op jit(solution)/shard_map/all_to_all | solution.py:363
  132.1 1.0 copy-start.15
  133.0 19.3 %copy-start.3 = (f32[16,72,128]{2,1,0:T(8,128)S(1)}, f32[16,72,128]{2,1,0:T(8,128)}, u32[]{:S(2)}) copy-start(f32[16,72,128]{2,1,0:T(8,128)} %copy-done) | copy-start | bytes 1769476
  133.0 19.3 %copy-start.11 = (f32[2,2,16,13,128]{4,3,2,1,0:T(8,128)S(1)}, f32[2,2,16,13,128]{4,3,2,1,0:T(8,128)}, u32[]{:S(2)}) copy-start(f32[2,2,16,13,128]{4,3,2,1,0:T(8,128)} %copy-done.10) | copy-start | bytes 1277956
  152.3 19.3 %copy-start.13 = (f32[64,512]{1,0:T(8,128)S(1)}, f32[64,512]{1,0:T(8,128)}, u32[]{:S(2)}) copy-start(f32[64,512]{1,0:T(8,128)} %copy.91.cy_ref) | copy-start | bytes 393220
  152.3 19.3 %copy-start.18 = (f32[128,128]{1,0:T(8,128)S(1)}, f32[128,128]{1,0:T(8,128)}, u32[]{:S(2)}) copy-start(f32[128,128]{1,0:T(8,128)} %mul.39.cz_ref) | copy-start | bytes 196612
  171.6 16.7 %copy-start.16 = (f32[256,256]{1,0:T(8,128)S(1)}, f32[256,256]{1,0:T(8,128)}, u32[]{:S(2)}) copy-start(f32[256,256]{1,0:T(8,128)} %convolution_select_fusion.cx_ref) | copy-start | bytes 786436
  188.8 1.4 collective-permute-start.2
  202.6 1.4 collective-permute-start.3

commit v3 on v2

--- a/solution.py
+++ b/solution.py
@@ -61,6 +61,76 @@
         return carry
 
     lax.fori_loop(0, window, body, 0)
+
+
+def pack_kernel(slab, window, width, pairs, src_ref, dst_ref):
+    each = src_ref.shape[0]
+    size = window * pairs
+    for j in range(dst_ref.shape[0]):
+        start = (j * slab - LOW) * pairs
+        low, high = max(start, 0), min(start + size, width * pairs)
+        for e in range(each):
+            if low > start:
+                dst_ref[j, e * size : e * size + low - start, :] = jnp.zeros((low - start, 128), F32)
+            if high < start + size:
+                dst_ref[j, e * size + high - start : (e + 1) * size, :] = jnp.zeros(
+                    (start + size - high, 128), F32
+                )
+            dst_ref[j, e * size + low - start : e * size + high - start, :] = src_ref[e, low:high, :]
+
+
+def equal(rows, columns, left, right):
+    a = lax.broadcasted_iota(jnp.int32, (rows, columns), 0)
+    b = lax.broadcasted_iota(jnp.int32, (rows, columns), 1)
+    return left(a) == right(b)
+
+
+def factors_kernel(lines, width, c_ref, cx_ref, cy_ref, cz_ref):
+    size = width * lines
+    pick = jnp.where(equal(size, width, lambda a: a // lines, lambda b: b), 1.0, 0.0)
+    turned = jnp.where(equal(width, size, lambda a: a, lambda b: b // lines), 1.0, 0.0)
+    same = equal(size, size, lambda a: a % lines, lambda b: b % lines)
+    cx_ref[...] = jnp.where(same, dot(dot(pick, c_ref[0]), turned), 0.0)
+    eight = jnp.where(equal(width, 8 * width, lambda a: a, lambda b: b // 8), 1.0, 0.0)
+    cy_ref[...] = dot(c_ref[1], eight)
+    pick = jnp.where(equal(128, width, lambda a: a % width, lambda b: b), 1.0, 0.0)
+    turned = jnp.where(equal(width, 128, lambda a: a, lambda b: b % width), 1.0, 0.0)
+    same = equal(128, 128, lambda a: a // width, lambda b: b // width)
+    cz_ref[...] = jnp.where(same, dot(dot(pick, c_ref[2].T), turned), 0.0)
+
+
+def slab_kernel(rounds, flag_ref, *refs):
+    dst_ref = refs[rounds]
+    rows = refs[0].shape[1]
+    for r in range(rounds):
+        k = lax.rem(flag_ref[2] - r + rounds, rounds)
+        dst_ref[:, pl.ds(pl.multiple_of(k * rows, 8), rows), :] = refs[r][...]
+
+
+def fields_kernel(slab, lines, pairs, slab_ref, low_ref, high_ref, v_ref, d_ref):
+    first_half = lax.broadcasted_iota(jnp.int32, (8, 128), 1) < 64
+
+    def both(a, b):
+        return jnp.where(first_half, a, turn(b)), jnp.where(first_half, turn(a), b)
+
+    for w in range(slab + LOW + HIGH):
+        if w < LOW:
+            ref, at = low_ref, w
+        elif w < LOW + slab:
+            ref, at = slab_ref, w - LOW
+        else:
+            ref, at = high_ref, w - LOW - slab
+        for rb in range(pairs // 8):
+            rows = slice(at * pairs + 8 * rb, at * pairs + 8 * rb + 8)
+            v = both(ref[0, rows, :], ref[1, rows, :])
+            diag = 2.0 * (3.0 - CENTER + ref[2, rows, :])
+            d = both(diag, diag)
+            for i in range(8):
+                for h in range(2):
+                    y = 2 * (8 * rb + i) + h
+                    row = w * lines + y % lines
+                    v_ref[y // lines, row : row + 1, :] = v[h][i : i + 1]
+                    d_ref[y // lines, row : row + 1, :] = d[h][i : i + 1]
 
 
 def krylov_kernel(slab, lines, width, group, filtered, *refs):
@@ -95,7 +165,7 @@
         return v_ref[y // lines, pl.ds(w * lines + y % lines, 1), :]
 
     def d_row(w, y):
-        return d_ref[y % lines, y // lines, pl.ds(w, 1), :]
+        return d_ref[y // lines, pl.ds(w * lines + y % lines, 1), :]
 
     def products(w, carry):
         for y in range(width):
@@ -164,8 +234,16 @@
         pay_ref[peer] = packed
 
 
-def combine_kernel(slab, lines, width, group, pay_ref, v_ref, o_ref, u1_ref, u2_ref, cy_ref, cz_ref, out_ref, field_s):
+def combine_kernel(
+    slab, lines, width, group, share, flag_ref, pay_ref, v_ref, o_ref, u1_ref, u2_ref, cy_ref, cz_ref, out_ref, field_s
+):
     chunks = out_ref.shape[0]
+    if share:
+        rows = share * lines
+        for k in range(chunks):
+            out_ref[k, slab * lines : slab * lines + rows, :] = v_ref[
+                k, pl.ds(flag_ref[2] * rows + LOW * lines, rows), :
+            ]
     total = pay_ref[0]
     for k in range(1, group):
         total = total + pay_ref[k]
@@ -203,8 +281,8 @@
         for y in range(width):
             o = o_ref[w, y].astype(F32)
             b = o * v_ref[y // lines, pl.ds(w * lines + y % lines, 1), :]
-            share = o * (c0 * b + (c1 * u1_ref[x + LOW - 1, y] + c2 * u2_ref[x, y]))
-            field_s[8 * y : 8 * y + 8, :] = share[0:8] + share[8:16]
+            part = o * (c0 * b + (c1 * u1_ref[x + LOW - 1, y] + c2 * u2_ref[x, y]))
+            field_s[8 * y : 8 * y + 8, :] = part[0:8] + part[8:16]
         planes = dot(dot(cy_ref[...], field_s[...]), cz_ref[...])
         for k in range(chunks):
             out_ref[k, pl.ds(x * lines, lines), :] = planes[k * lines : (k + 1) * lines]
@@ -214,17 +292,24 @@
 
 
 def gathered(got_ref, cx_ref, group):
-    n, rows, _ = got_ref.shape
+    n = got_ref.shape[0]
+    rows = cx_ref.shape[0] // group
     parts = []
     for j in range(group):
-        parts.append(tree([got_ref[q * group + j] for q in range(n // group)]))
+        parts.append(tree([got_ref[q * group + j, 0:rows, :] for q in range(n // group)]))
     return dot(cx_ref[...], jnp.concatenate(parts, axis=0))
 
 
-def mapped_kernel(slab, lines, width, group, got_ref, cx_ref, t_ref, mapped_ref, pay_ref):
+def mapped_kernel(slab, lines, width, group, got_ref, cx_ref, mapped_ref, t_ref, pay_ref):
     n, size, _ = pay_ref.shape
     mapped = gathered(got_ref, cx_ref, group)
     mapped_ref[...] = mapped
+    rounds = n // group
+    rows = slab // rounds * lines
+    for j in range(group):
+        for q in range(rounds):
+            at = (j * rounds + q) * rows
+            t_ref[at : at + rows, :] = got_ref[q * group + j, slab * lines : slab * lines + rows, :]
     t = t_ref[...]
     sums = [jnp.sum(a * b, axis=0, keepdims=True) for a, b in ((t, t), (t, mapped), (mapped, mapped))]
     window = (slab + LOW + HIGH) * lines
@@ -321,7 +406,7 @@
     return pl.BlockSpec(memory_space=pltpu.SMEM)
 
 
-def call(kernel, name, shapes, inputs, scratch=(), limit=16, in_smem=()):
+def call(kernel, name, shapes, inputs, scratch=(), limit=4, in_smem=()):
     return pl.pallas_call(
         kernel,
         out_shape=shapes,
@@ -369,20 +454,15 @@
 
     mine = lax.dynamic_slice_in_dim(orbitals, core * each, each, 0).astype(F32)
     mine = mine.reshape(each, width * pairs, 128)
-    mine = jnp.pad(mine, ((0, 0), (LOW * pairs, HIGH * pairs), (0, 0)))
-    sent = jnp.stack(
-        [mine[:, j * slab * pairs : (j * slab + window) * pairs] for j in range(group)], axis=0
-    )
-    own_half = exchange_group(sent.reshape(group, each * window * pairs, 128))
+    sent = call(
+        functools.partial(pack_kernel, slab, window, width, pairs),
+        "pack_orbitals",
+        shape(group, each * window * pairs, 128),
+        (mine,),
+        limit=8,
+    )
+    own_half = exchange_group(sent)
     own_half = own_half.reshape(ORBS // 2 * window * pairs, 128)
-    other_half = swap(own_half)
-    spread_orbitals = call(
-        functools.partial(spread_kernel, window, pairs),
-        "spread_orbitals",
-        jax.ShapeDtypeStruct((window, width, ORBS, 128), jnp.bfloat16),
-        (own_half, other_half),
-        limit=16,
-    )
     shifts = orbital_shifts(orbital_ids, freq_index, energies, frequencies)
     shifts = jnp.where(core == 0, shifts, jnp.roll(shifts, -each))
     slot_rows = [(k // each) * (ORBS // 2) + place * each + k % each for k in range(held)]
@@ -392,55 +472,77 @@
         jnp.where((row == slot_rows[k]) & (lane == SHIFT_LANE), shifts[k], 0.0) for k in range(held)
     )
 
-    t_rows = trials.reshape(count, planes, width, width).transpose(1, 2, 0, 3)
-    t_rows = t_rows.reshape(planes, n, lines, 128).transpose(1, 0, 2, 3).reshape(n, planes * lines, 128)
-    diag = 2.0 * (3.0 - CENTER + potential)
-    shared = lines % (2 * cores) == 0
-    kept = lines // 2 // cores if shared else lines
-    if shared:
-        d_rows = diag.reshape(planes, n, cores, kept, 128)
-        d_rows = lax.dynamic_index_in_dim(d_rows, core, 2, keepdims=False)
+    rounds = n // group
+    flags = jnp.stack([place * slab, core, me // group]).astype(jnp.int32)
+    fields = jnp.concatenate([trials, potential[None]], axis=0).reshape(count + 1, planes * pairs, 128)
+    blocks = [
+        lax.ppermute(
+            fields,
+            "orb",
+            [
+                (j * rounds + k, (k + r) % rounds * group + j)
+                for j in range(group)
+                for k in range(rounds)
+            ],
+        )
+        for r in range(rounds)
+    ]
+    slabs = call(
+        functools.partial(slab_kernel, rounds),
+        "slab",
+        shape(count + 1, slab * pairs, 128),
+        (flags, *blocks),
+        limit=8,
+        in_smem=(0,),
+    )
+    if planes >= HIGH and rounds == 2:
+        last = me % rounds == rounds - 1
+        edge = jnp.where(last, fields[:, (planes - HIGH) * pairs :], fields[:, : HIGH * pairs])
+        first, other = (
+            lax.ppermute(
+                edge,
+                "orb",
+                [((j - 1) * rounds + 1, q * group + j) for j in range(1, group)]
+                + [((j + 1) * rounds, (1 - q) * group + j) for j in range(group - 1)],
+            )
+            for q in range(rounds)
+        )
+        is_first = me // group == 0
+        low = jnp.where(is_first, first, other)[:, (HIGH - LOW) * pairs :]
+        high = jnp.where(is_first, other, first)
     else:
-        d_rows = jnp.tile(diag.reshape(planes, n, lines, width), (1, 1, 1, 128 // width))
-    d_rows = d_rows.transpose(1, 0, 2, 3).reshape(n, planes * kept, 128)
-    got = exchange(jnp.concatenate([t_rows, d_rows], axis=1))
-    trial_rows = got[:, : planes * lines].reshape(width * lines, 128)
-    diag_rows = got[:, planes * lines :].reshape(width * kept, 128)
-
-    def windows(x, per):
-        x = jnp.pad(x, ((LOW * per, HIGH * per), (0, 0)))
-        return jnp.stack([x[j * slab * per : (j * slab + window) * per] for j in range(group)], 0)
-
+        low = lax.ppermute(
+            slabs[:, (slab - LOW) * pairs :], "orb", [(i, i + 1) for i in range(n) if i % group < group - 1]
+        )
+        high = lax.ppermute(slabs[:, : HIGH * pairs], "orb", [(i, i - 1) for i in range(n) if i % group > 0])
     used = window * lines
-    size = up8(used + window * kept)
-    both = jnp.concatenate([windows(trial_rows, lines), windows(diag_rows, kept)], axis=1)
-    both = jnp.pad(both, ((0, 0), (0, size - both.shape[1]), (0, 0)))
-    trial_window = exchange(jnp.tile(both, (n // group, 1, 1)))
-    diag_own = trial_window[:, used : used + window * kept].reshape(n, window, kept, 128)
-    diag_own = diag_own.transpose(2, 0, 1, 3)
-    if shared:
-        diag_other = swap(diag_own)
-        low, high = jnp.where(core == 0, diag_own, diag_other), jnp.where(core == 0, diag_other, diag_own)
-        both = jnp.concatenate([low, high], axis=0)
-        both = jnp.stack(
-            [jnp.tile(both[..., h * width : (h + 1) * width], (1, 1, 1, 2)) for h in range(2)], axis=1
-        )
-        diag_window = both.reshape(lines, n, window, 128)
-    else:
-        diag_window = diag_own
-
-    flags = jnp.stack([place * slab, core]).astype(jnp.int32)
-    cy = jnp.repeat(coulomb[1], 8, axis=1)
-    cz = jnp.kron(jnp.eye(count, dtype=F32), coulomb[2].T)
-    wide = lax.broadcasted_iota(jnp.int32, (width * lines, width), 0) // lines
-    wide = (wide == lax.broadcasted_iota(jnp.int32, (width * lines, width), 1)).astype(F32)
-    cx = jnp.dot(jnp.dot(wide, coulomb[0], precision=HIGHEST), wide.T, precision=HIGHEST)
-    a = lax.broadcasted_iota(jnp.int32, cx.shape, 0) % lines
-    b = lax.broadcasted_iota(jnp.int32, cx.shape, 1) % lines
-    cx = jnp.where(a == b, cx, 0.0)
+    trial_window, diag_window = call(
+        functools.partial(fields_kernel, slab, lines, pairs),
+        "fields",
+        (shape(n, used, 128), shape(n, used, 128)),
+        (slabs, low, high),
+        limit=8,
+    )
+    cx, cy, cz = call(
+        functools.partial(factors_kernel, lines, width),
+        "factors",
+        (shape(width * lines, width * lines), shape(width, 8 * width), shape(128, 128)),
+        (coulomb,),
+    )
+    trial_window, diag_window, cx, cy, cz, shift_rows, own_half = lax.optimization_barrier(
+        (trial_window, diag_window, cx, cy, cz, shift_rows, own_half)
+    )
+    spread_orbitals = call(
+        functools.partial(spread_kernel, window, pairs),
+        "spread_orbitals",
+        jax.ShapeDtypeStruct((window, width, ORBS, 128), jnp.bfloat16),
+        (own_half, swap(own_half)),
+        limit=4,
+    )
 
     def response(fields):
         filtered = len(fields) == 2
+        share = 0 if filtered else slab // rounds
         shapes = [
             shape(slab + 3, width, ORBS, 128), shape(slab + 1, width, ORBS, 128), shape(group, ORBS, 128),
         ]
@@ -452,27 +554,28 @@
             tuple(shapes),
             (flags, spread_orbitals, diag_window, shift_rows, *fields),
             scratch=[pltpu.VMEM((window, width, ORBS, 128), F32)],
-            limit=32,
+            limit=14,
             in_smem=(0,),
         )
         u1, u2, pay = made[:3]
         v = made[3] if filtered else fields[0]
         part = call(
-            functools.partial(combine_kernel, slab, lines, width, group),
+            functools.partial(combine_kernel, slab, lines, width, group, share),
             "combine",
-            shape(n, slab * lines, 128),
-            (exchange_group(pay), v, spread_orbitals, u1, u2, cy, cz),
+            shape(n, up8((slab + share) * lines), 128),
+            (flags, exchange_group(pay), v, spread_orbitals, u1, u2, cy, cz),
             scratch=[pltpu.VMEM((8 * width, 128), F32)],
-            limit=32,
+            limit=4,
+            in_smem=(0,),
         )
         return exchange(part), (made[4] if filtered else None)
 
     got, _ = response((trial_window,))
-    mapped, pay = call(
+    mapped, trial_rows, pay = call(
         functools.partial(mapped_kernel, slab, lines, width, group),
         "mapped",
-        (shape(width * lines, 128), shape(n, up8(used) + 8, 128)),
-        (got, cx, trial_rows),
+        (shape(width * lines, 128), shape(width * lines, 128), shape(n, up8(used) + 8, 128)),
+        (got, cx),
     )
     got, scales = response((trial_window, exchange(pay)))
     second = call(

time: 207 us -> 166 us (0.80)
  local copies, waits for them, and re-layouts: 33.5 us -> 2.72 us
  blocking collectives: 50.2 us -> 79.6 us
  waiting for transfers between devices: 45.7 us -> 20.2 us
  starting transfers between devices: 26.6 us -> 17.9 us
  matrix products: 3.08 us -> 0 us
  other arithmetic: 7 us -> 4.45 us
    all_to_all x2 -> x1, waiting for transfers between devices: 22.5 us -> 0.01 us  [exchange_group(): lax.all_to_all(x, 'orb', split_axis=0, concat_axis=0, tiled=True, axis_in...]
    unnamed x75 -> x15, local copies, waits for them, and re-layouts: 21.5 us -> 0.05 us
    all_to_all x3 -> x0, waiting for transfers between devices: 19.3 us -> none  [exchange(): return lax.all_to_all(x, 'orb', split_axis=0, concat_axis=0, tiled=True)]
    all_to_all x3 -> x0, starting transfers between devices: 18.3 us -> none  [exchange(): return lax.all_to_all(x, 'orb', split_axis=0, concat_axis=0, tiled=True)]
    all_to_all x1 -> x2, blocking collectives: 8.83 us -> 24.4 us  [exchange_group(): lax.all_to_all(x, 'orb', split_axis=0, concat_axis=0, tiled=True, axis_in...]
    ppermute x0 -> x4, waiting for transfers between devices: none -> 14 us  [the longest x2 7.43 us: shards(): lax.ppermute(fields, 'orb', [(j * rounds + k, (k + r) % rounds * group +...]
    all_to_all x3 -> x4, blocking collectives: 41.4 us -> 55.2 us  [exchange(): return lax.all_to_all(x, 'orb', split_axis=0, concat_axis=0, tiled=True)]
    ppermute x0 -> x4, starting transfers between devices: none -> 11.5 us  [the longest x2 9.53 us: shards(): lax.ppermute(fields, 'orb', [(j * rounds + k, (k + r) % rounds * group +...]
  transfers between devices with their start and end apart: 9 -> 8, of which waited for: 8 -> 5; matrix products, arithmetic and copies ran while one was open for 11% -> 3% of each run, Pallas kernels for 0% -> 1%
where the time goes in v3:
time: 166 us
  blocking collectives  79.6 us (48%)
  Pallas kernels  40.7 us (25%)
  waiting for transfers between devices  20.2 us (12%)
  starting transfers between devices  17.9 us (11%)
  other arithmetic  4.45 us (3%)
  local copies, waits for them, and re-layouts  2.72 us (2%)
    all_to_all x4, blocking collectives, exchange(): return lax.all_to_all(x, 'orb', split_axis=0, concat_axis=0, tiled=True)  55.2 us
    pallas_call x13, Pallas kernels, call(): pl.pallas_call(kernel, out_shape=shapes, in_specs=[smem() if k in in_smem...  40.7 us
    all_to_all x2, blocking collectives, exchange_group(): lax.all_to_all(x, 'orb', split_axis=0, concat_axis=0, tiled=True, axis_in...  24.4 us
    ppermute x2, starting transfers between devices, shards(): lax.ppermute(fields, 'orb', [(j * rounds + k, (k + r) % rounds * group +...  9.53 us
    ppermute x2, waiting for transfers between devices, shards(): lax.ppermute(fields, 'orb', [(j * rounds + k, (k + r) % rounds * group +...  7.43 us
    ppermute x2, waiting for transfers between devices, shards(): lax.ppermute(edge, 'orb', [((j - 1) * rounds + 1, q * group + j) for j in...  6.54 us
    ppermute x3, waiting for transfers between devices, swap(): lax.ppermute(x, 'trial', [(k, (k + 1) % cores) for k in range(cores)])  6.25 us
    all_to_all x1, starting transfers between devices, exchange_group(): lax.all_to_all(x, 'orb', split_axis=0, concat_axis=0, tiled=True, axis_in...  6.18 us
  transfers between devices with their start and end apart: 8, of which 5 were waited for; matrix products, arithmetic and copies ran while one was open for 3% of the time, Pallas kernels for 1%

profile of v3, /device:TPU:0, one launch (start us, length us, event | category | flops | bytes accessed | tf_op | source)
XLA Modules:
  0.0 166.0 jit_solution(17423504283972311754)
XLA Ops:
  0.0 0.0 copy-start.2
  0.0 0.0 copy-start.1
  0.0 1.1 dynamic-slice_convert_fusion
  1.2 0.0 copy-start.3
  1.2 0.0 copy-start.4
  1.2 0.0 copy-start.5
  1.2 0.0 copy-start.6
  1.2 0.0 copy-start
  1.2 0.2 reshape.28.src_ref
  1.4 1.3 pack_orbitals.1
  2.7 6.2 %all-to-all-start = ((f32[8,416,128]{2,1,0:T(8,128)}), f32[8,416,128]{2,1,0:T(8,128)S(1)}, u32[]{:S(2)}, u32[]{:S(2)}) async-start(f32[8,416,128]{2,1,0:T(8,128)} %pack_orbitals.1), calls=%async_computation | async-start | bytes 3407872 | tf_op jit(solution)/shard_map/all_to_all | solution.py:451
  8.9 0.0 copy-done.2
  9.0 0.0 copy-done.1
  9.0 0.1 concatenate.12
  9.1 1.3 collective-permute-start.3
  10.4 0.7 collective-permute-start.2
  11.1 8.9 %collective-permute-start.1 = (f32[3,128,128]{2,1,0:T(8,128)S(1)}, f32[3,128,128]{2,1,0:T(8,128)S(1)}, u32[]{:S(2)}, u32[]{:S(2)}) collective-permute-start(f32[3,128,128]{2,1,0:T(8,128)S(1)} %constant_dynamic-update-slice_fusion), channel_id=1, source_target_pairs={{0,16},{2,0},{4,18},{6,2},{8,20},{10,4},{12,22},{14,6},{16,24},{18... | collective-permute-start | bytes 589832 | tf_op jit(solution)/shard_map/ppermute | solution.py:479
  20.0 0.7 collective-permute-start
  20.7 0.0 copy-done.3
  20.7 0.0 copy-done.4
  20.7 0.2 fusion.1
  20.9 0.0 copy-done.5
  20.9 0.0 copy-done.6
  20.9 0.2 fusion
  21.1 0.6 fusion.3
  21.7 1.4 broadcast_select_fusion.1
  23.1 0.6 fusion.2
  23.7 1.4 select_add_fusion.refs_3_
  25.1 0.0 copy-done
  25.1 0.9 factors.1
  26.1 0.1 pad_add_fusion.flag_ref.refs_0_
  26.1 6.5 %collective-permute-done.3 = f32[3,96,128]{2,1,0:T(8,128)S(1)} collective-permute-done((f32[3,96,128]{2,1,0:T(8,128)S(1)}, f32[3,96,128]{2,1,0:T(8,128)S(1)}, u32[]{:S(2)}, u32[]{:S(2)}) %collective-permute-start.3) | collective-permute-done | bytes 147488 | tf_op jit(solution)/shard_map/ppermute | solution.py:502
  32.7 0.0 collective-permute-done.2
  32.7 7.4 %collective-permute-done.1.refs_1_ = f32[3,128,128]{2,1,0:T(8,128)S(1)} collective-permute-done((f32[3,128,128]{2,1,0:T(8,128)S(1)}, f32[3,128,128]{2,1,0:T(8,128)S(1)}, u32[]{:S(2)}, u32[]{:S(2)}) %collective-permute-start.1) | collective-permute-done | bytes 196640 | tf_op jit(solution)/shard_map/ppermute | solution.py:479
  40.2 0.0 collective-permute-done.refs_0_
  40.2 0.6 slab.1.slab_ref
  40.7 0.3 fields.1
  41.1 0.0 all-to-all-done
  41.1 0.1 collective-permute-start.4
  41.1 3.6 %collective-permute-done.4.other_ref = f32[3328,128]{1,0:T(8,128)S(1)} collective-permute-done((f32[3328,128]{1,0:T(8,128)S(1)}, f32[3328,128]{1,0:T(8,128)S(1)}, u32[]{:S(2)}, u32[]{:S(2)}) %collective-permute-start.4) | collective-permute-done | bytes 1703968 | tf_op jit(solution)/shard_map/ppermute | solution.py:445
  44.7 2.9 %spread_orbitals.1.refs_1_.o_ref = bf16[13,64,16,128]{3,2,1,0:T(8,128)(2,1)S(1)} custom-call(f32[3328,128]{1,0:T(8,128)S(1)} %bitcast.8, f32[3328,128]{1,0:T(8,128)S(1)} %collective-permute-done.4.other_ref), custom_call_target="tpu_custom_call" | custom-call | tf_op jit(solution)/shard_map/spread_orbitals/pallas_call | solution.py:410
  47.6 10.1 %krylov.2 = (f32[11,64,16,128]{3,2,1,0:T(8,128)S(1)}, f32[9,64,16,128]{3,2,1,0:T(8,128)S(1)}, f32[8,16,128]{2,1,0:T(8,128)S(1)}) custom-call(s32[3]{0:T(128)S(1)} %pad_add_fusion.flag_ref.refs_0_, bf16[13,64,16,128]{3,2,1,0:T(8,128)(2,1)S(1)} %spread_orbitals.1.refs_1_.o_ref, f32[16,52,128]{2,1,0:T(8,128)S(1)} %get-tuple-element.34.refs_2_, ...), custom_call_target="tpu_custom_call" | custom-call | tf_op jit(solution)/shard_map/krylov/pallas_call | solution.py:410
  57.7 15.6 %all_to_all.35.pay_ref = f32[8,16,128]{2,1,0:T(8,128)S(1)} all-to-all(f32[8,16,128]{2,1,0:T(8,128)S(1)} %get-tuple-element.37), channel_id=1, replica_groups={{0,2,4,6,8,10,12,14},{16,18,20,22,24,26,28,30},{1,3,5,7,9,11,13,15},{17..., dimensions={0} | all-to-all | bytes 131072 | tf_op jit(solution)/shard_map/all_to_all | solution.py:451
  73.3 6.1 %combine.2 = f32[16,48,128]{2,1,0:T(8,128)S(1)} custom-call(s32[3]{0:T(128)S(1)} %pad_add_fusion.flag_ref.refs_0_, f32[8,16,128]{2,1,0:T(8,128)S(1)} %all_to_all.35.pay_ref, f32[16,52,128]{2,1,0:T(8,128)S(1)} %get-tuple-element.36.refs_4_.v_ref, bf16[13,64,16,128]{3,2,1,0:T(8,128)(2,1)S(1)} %spread_orbitals.1.refs_1_.o_ref, ...), custom_call_target="tpu_custom_call" | custom-call | tf_op jit(solution)/shard_map/combine/pallas_call | solution.py:410
  79.5 14.3 %all_to_all.36.got_ref = f32[16,48,128]{2,1,0:T(8,128)S(1)} all-to-all(f32[16,48,128]{2,1,0:T(8,128)S(1)} %combine.2), channel_id=1, replica_groups=mesh['orb'=16,'trial'=2] {'orb'}, dimensions={0} | all-to-all | bytes 786432 | tf_op jit(solution)/shard_map/all_to_all | solution.py:448
  93.8 0.4 mapped.1
  94.2 17.4 %all_to_all.37.refs_5_ = f32[16,64,128]{2,1,0:T(8,128)S(1)} all-to-all(f32[16,64,128]{2,1,0:T(8,128)S(1)} %get-tuple-element.43), channel_id=1, replica_groups=mesh['orb'=16,'trial'=2] {'orb'}, dimensions={0} | all-to-all | bytes 1048576 | tf_op jit(solution)/shard_map/all_to_all | solution.py:448
  111.6 10.5 %krylov.3 = (f32[11,64,16,128]{3,2,1,0:T(8,128)S(1)}, f32[9,64,16,128]{3,2,1,0:T(8,128)S(1)}, f32[8,16,128]{2,1,0:T(8,128)S(1)}, f32[16,52,128]{2,1,0:T(8,128)S(1)}, f32[8,128]{1,0:T(8,128)S(1)}) custom-call(s32[3]{0:T(128)S(1)} %pad_add_fusion.flag_ref.refs_0_, bf16[13,64,16,128]{3,2,1,0:T(8,128)(2,1)S(1)} %spread_orbitals.1.refs_1_.o_ref, ...), custom_call_target="tpu_custom_call" | custom-call | tf_op jit(solution)/shard_map/krylov/pallas_call | solution.py:410
  122.1 8.8 %all_to_all.38.pay_ref = f32[8,16,128]{2,1,0:T(8,128)S(1)} all-to-all(f32[8,16,128]{2,1,0:T(8,128)S(1)} %get-tuple-element.44), channel_id=1, replica_groups={{0,2,4,6,8,10,12,14},{16,18,20,22,24,26,28,30},{1,3,5,7,9,11,13,15},{17..., dimensions={0} | all-to-all | bytes 131072 | tf_op jit(solution)/shard_map/all_to_all | solution.py:451
  130.9 6.1 %combine.3 = f32[16,32,128]{2,1,0:T(8,128)S(1)} custom-call(s32[3]{0:T(128)S(1)} %pad_add_fusion.flag_ref.refs_0_, f32[8,16,128]{2,1,0:T(8,128)S(1)} %all_to_all.38.pay_ref, f32[16,52,128]{2,1,0:T(8,128)S(1)} %get-tuple-element.45.v_ref, bf16[13,64,16,128]{3,2,1,0:T(8,128)(2,1)S(1)} %spread_orbitals.1.refs_1_.o_ref, ...), custom_call_target="tpu_custom_call" | custom-call | tf_op jit(solution)/shard_map/combine/pallas_call | solution.py:410
  137.1 11.2 %all_to_all.39.got_ref = f32[16,32,128]{2,1,0:T(8,128)S(1)} all-to-all(f32[16,32,128]{2,1,0:T(8,128)S(1)} %combine.3), channel_id=1, replica_groups=mesh['orb'=16,'trial'=2] {'orb'}, dimensions={0} | all-to-all | bytes 524288 | tf_op jit(solution)/shard_map/all_to_all | solution.py:448
  148.3 0.4 second.1.second_ref
  148.7 0.1 collective-permute-start.5
  148.8 1.3 collective-permute-done.5.other_ref
  150.1 0.2 gram.1
  150.3 12.3 %all_to_all.40.got_ref = f32[16,24,128]{2,1,0:T(8,128)S(1)} all-to-all(f32[16,24,128]{2,1,0:T(8,128)S(1)} %gram.1), channel_id=1, replica_groups=mesh['orb'=16,'trial'=2] {'orb'}, dimensions={0} | all-to-all | bytes 393216 | tf_op jit(solution)/shard_map/all_to_all | solution.py:448
  162.5 0.1 collective-permute-start.6
  162.6 1.3 collective-permute-done.6.other_ref
  163.9 0.9 final.1
  164.8 0.2 reshape.25
  165.0 0.1 copy.10
  165.1 0.9 reshape.26
  (10 shorter events, 0.1 us)
Async XLA Ops:
  0.0 8.9 %copy-start.2 = (f32[4,4096]{1,0:T(4,128)S(1)}, f32[4,4096]{1,0:T(4,128)}, u32[]{:S(2)}) copy-start(f32[4,4096]{1,0:T(4,128)} %param.10) | copy-start | bytes 196612
  0.0 9.0 %copy-start.1 = (f32[2,4,4096]{2,1,0:T(4,128)S(1)}, f32[2,4,4096]{2,1,0:T(4,128)}, u32[]{:S(2)}) copy-start(f32[2,4,4096]{2,1,0:T(4,128)} %param.8) | copy-start | bytes 393220
  1.2 19.5 %copy-start.3 = (f32[32]{0:T(128)S(1)}, f32[32]{0:T(128)}, u32[]{:S(2)}) copy-start(f32[32]{0:T(128)} %param.12) | copy-start | bytes 388
  1.2 19.5 %copy-start.4 = (s32[2]{0:T(128)S(1)}, s32[2]{0:T(128)}, u32[]{:S(2)}) copy-start(s32[2]{0:T(128)} %param.14) | copy-start | bytes 28
  1.2 19.7 %copy-start.5 = (f32[8]{0:T(128)S(1)}, f32[8]{0:T(128)}, u32[]{:S(2)}) copy-start(f32[8]{0:T(128)} %param.13) | copy-start | bytes 100
  1.2 19.7 %copy-start.6 = (s32[2]{0:T(128)S(1)}, s32[2]{0:T(128)}, u32[]{:S(2)}) copy-start(s32[2]{0:T(128)} %param.15) | copy-start | bytes 28
  1.2 23.9 %copy-start = (f32[3,64,64]{2,1,0:T(8,128)S(1)}, f32[3,64,64]{2,1,0:T(8,128)}, u32[]{:S(2)}) copy-start(f32[3,64,64]{2,1,0:T(8,128)} %c_ref.1) | copy-start | bytes 147460
  2.7 38.3 %all-to-all-start = ((f32[8,416,128]{2,1,0:T(8,128)}), f32[8,416,128]{2,1,0:T(8,128)S(1)}, u32[]{:S(2)}, u32[]{:S(2)}) async-start(f32[8,416,128]{2,1,0:T(8,128)} %pack_orbitals.1), calls=%async_computation | async-start | bytes 3407872 | tf_op jit(solution)/shard_map/all_to_all | solution.py:451
  9.1 23.5 %collective-permute-start.3 = (f32[3,96,128]{2,1,0:T(8,128)S(1)}, f32[3,96,128]{2,1,0:T(8,128)S(1)}, u32[]{:S(2)}, u32[]{:S(2)}) collective-permute-start(f32[3,96,128]{2,1,0:T(8,128)S(1)} %slice_select_fusion), channel_id=1, source_target_pairs={{2,18},{6,20},{10,22},{14,24},{18,26},{22,28},{26,30},{4,0},{8,2},... | collective-permute-start | bytes 442376 | tf_op jit(solution)/shard_map/ppermute | solution.py:502
  10.4 22.2 %collective-permute-start.2 = (f32[3,96,128]{2,1,0:T(8,128)S(1)}, f32[3,96,128]{2,1,0:T(8,128)S(1)}, u32[]{:S(2)}, u32[]{:S(2)}) collective-permute-start(f32[3,96,128]{2,1,0:T(8,128)S(1)} %slice_select_fusion), channel_id=1, source_target_pairs={{2,2},{6,4},{10,6},{14,8},{18,10},{22,12},{26,14},{4,16},{8,18},{1... | collective-permute-start | bytes 442376 | tf_op jit(solution)/shard_map/ppermute | solution.py:502
  11.1 29.0 %collective-permute-start.1 = (f32[3,128,128]{2,1,0:T(8,128)S(1)}, f32[3,128,128]{2,1,0:T(8,128)S(1)}, u32[]{:S(2)}, u32[]{:S(2)}) collective-permute-start(f32[3,128,128]{2,1,0:T(8,128)S(1)} %constant_dynamic-update-slice_fusion), channel_id=1, source_target_pairs={{0,16},{2,0},{4,18},{6,2},{8,20},{10,4},{12,22},{14,6},{16,24},{18... | collective-permute-start | bytes 589832 | tf_op jit(solution)/shard_map/ppermute | solution.py:479
  20.0 20.2 %collective-permute-start = (f32[3,128,128]{2,1,0:T(8,128)S(1)}, f32[3,128,128]{2,1,0:T(8,128)S(1)}, u32[]{:S(2)}, u32[]{:S(2)}) collective-permute-start(f32[3,128,128]{2,1,0:T(8,128)S(1)} %constant_dynamic-update-slice_fusion), channel_id=1, source_target_pairs={{0,0},{2,16},{4,2},{6,18},{8,4},{10,20},{12,6},{14,22},{16,8},{18,... | collective-permute-start | bytes 589832 | tf_op jit(solution)/shard_map/ppermute | solution.py:479
  41.1 3.7 %collective-permute-start.4 = (f32[3328,128]{1,0:T(8,128)S(1)}, f32[3328,128]{1,0:T(8,128)S(1)}, u32[]{:S(2)}, u32[]{:S(2)}) collective-permute-start(f32[3328,128]{1,0:T(8,128)S(1)} %bitcast.7), channel_id=1, source_target_pairs={{0,1},{1,0},{2,3},{3,2},{4,5},{5,4},{6,7},{7,6},{8,9},{9,8},{10,11... | collective-permute-start | bytes 5111816 | tf_op jit(solution)/shard_map/ppermute | solution.py:445
  148.7 1.4 collective-permute-start.5
  162.5 1.4 collective-permute-start.6

commit v4 on v3

--- a/solution.py
+++ b/solution.py
@@ -85,14 +85,12 @@
     return left(a) == right(b)
 
 
-def factors_kernel(lines, width, c_ref, cx_ref, cy_ref, cz_ref):
+def factors_kernel(lines, width, c_ref, cx_ref, cz_ref):
     size = width * lines
     pick = jnp.where(equal(size, width, lambda a: a // lines, lambda b: b), 1.0, 0.0)
     turned = jnp.where(equal(width, size, lambda a: a, lambda b: b // lines), 1.0, 0.0)
     same = equal(size, size, lambda a: a % lines, lambda b: b % lines)
     cx_ref[...] = jnp.where(same, dot(dot(pick, c_ref[0]), turned), 0.0)
-    eight = jnp.where(equal(width, 8 * width, lambda a: a, lambda b: b // 8), 1.0, 0.0)
-    cy_ref[...] = dot(c_ref[1], eight)
     pick = jnp.where(equal(128, width, lambda a: a % width, lambda b: b), 1.0, 0.0)
     turned = jnp.where(equal(width, 128, lambda a: a, lambda b: b % width), 1.0, 0.0)
     same = equal(128, 128, lambda a: a // width, lambda b: b // width)
@@ -148,10 +146,11 @@
     n = t_ref.shape[0]
 
     if filtered:
-        base = m_ref.shape[1] - 8
-        total = m_ref[0, base : base + 8, :]
+        base = window * lines
+        total = m_ref[0, base : base + 3, :]
         for k in range(1, n):
-            total = total + m_ref[k, base : base + 8, :]
+            total = total + m_ref[k, base : base + 3, :]
+        total = jnp.concatenate([total, jnp.zeros((5, 128), F32)], axis=0)
         total = dot(total, halves(8, width))
         center = total[1:2] / total[0:1]
         inverse = 1.0 / jnp.sqrt(total[2:3] / total[0:1])
@@ -204,12 +203,16 @@
     own = (LOW, LOW + slab)
     halo(b_s, 0, u1_ref, 1, LOW - 1, first < 1)
     m0, m1, m2 = lax.fori_loop(
-        *own, lambda w, c: apply(b_s, 0, u1_ref, 1, w, c, ((0, 0), (0, 1), (1, 1))), (zero,) * 3
+        *own,
+        lambda w, c: apply(b_s, 0, u1_ref, 1, w, c, ((0, 0), (0, 1), (1, 1))), (zero,) * 3,
+        unroll=True,
     )
     halo(b_s, 0, u1_ref, 1, LOW + slab, first + slab >= width)
     halo(b_s, 0, u1_ref, 1, LOW + slab + 1, first + slab + 1 >= width)
     m3, m4 = lax.fori_loop(
-        *own, lambda w, c: apply(u1_ref, 1, u2_ref, LOW, w, c, ((0, 1), (1, 1))), (zero,) * 2
+        *own,
+        lambda w, c: apply(u1_ref, 1, u2_ref, LOW, w, c, ((0, 1), (1, 1))), (zero,) * 2,
+        unroll=True,
     )
     halo(u1_ref, 1, u2_ref, LOW, LOW + slab, first + slab >= width)
 
@@ -224,7 +227,7 @@
             terms.append(mid * (d_row(w, y) * mid - 2.0 * above))
         return carry + tree(terms)
 
-    m5 = lax.fori_loop(*own, last, zero)
+    m5 = lax.fori_loop(*own, last, zero, unroll=True)
     column = lax.broadcasted_iota(jnp.int32, (128, 128), 1)
     half = lax.broadcasted_iota(jnp.int32, (128, 128), 0) // width
     packed = sh_ref[...]
@@ -276,19 +279,38 @@
     c1 = (-0.25 / 8.0) * y1
     c2 = (-0.25 / 64.0) * y2
 
+    sublane = lax.broadcasted_iota(jnp.int32, (8, 128), 0)
+    takes = [(sublane // step) % 2 == 0 for step in (1, 2, 4)]
+
+    def merge(values):
+        for take, step in zip(takes, (1, 2, 4)):
+            values = [
+                jnp.where(take, a, b) + pltpu.roll(jnp.where(take, b, a), step, 0)
+                for a, b in zip(values[::2], values[1::2])
+            ]
+        return values[0]
+
     def plane(x, carry):
         w = x + LOW
-        for y in range(width):
-            o = o_ref[w, y].astype(F32)
-            b = o * v_ref[y // lines, pl.ds(w * lines + y % lines, 1), :]
-            part = o * (c0 * b + (c1 * u1_ref[x + LOW - 1, y] + c2 * u2_ref[x, y]))
-            field_s[8 * y : 8 * y + 8, :] = part[0:8] + part[8:16]
-        planes = dot(dot(cy_ref[...], field_s[...]), cz_ref[...])
+        for y0 in range(0, width, 8):
+            values = []
+            for y in range(y0, y0 + 8):
+                o = o_ref[w, y].astype(F32)
+                b = o * v_ref[y // lines, pl.ds(w * lines + y % lines, 1), :]
+                part = o * (c0 * b + (c1 * u1_ref[x + LOW - 1, y] + c2 * u2_ref[x, y]))
+                values.append(part[0:8] + part[8:16])
+            field_s[pl.ds(pl.multiple_of(x * width + y0, 8), 8), :] = merge(values)
+        return carry
+
+    lax.fori_loop(0, slab, plane, 0)
+    turned = dot(field_s[...], cz_ref[...])
+    turned = jnp.concatenate([turned[x * width : (x + 1) * width] for x in range(slab)], axis=1)
+    planes = dot(cy_ref[...], turned)
+    for x in range(slab):
         for k in range(chunks):
-            out_ref[k, pl.ds(x * lines, lines), :] = planes[k * lines : (k + 1) * lines]
-        return carry
-
-    lax.fori_loop(0, slab, plane, 0)
+            out_ref[k, x * lines : (x + 1) * lines, :] = planes[
+                k * lines : (k + 1) * lines, x * 128 : (x + 1) * 128
+            ]
 
 
 def gathered(got_ref, cx_ref, group):
@@ -319,7 +341,7 @@
         pay_ref[k] = jnp.zeros((size, 128), F32)
         pay_ref[k, low - start : high - start, :] = mapped_ref[low:high, :]
         for i, s in enumerate(sums):
-            pay_ref[k, size - 8 + i : size - 7 + i, :] = s
+            pay_ref[k, window + i : window + i + 1, :] = s
 
 
 def second_kernel(group, got_ref, cx_ref, t_ref, mapped_ref, cs_ref, second_ref):
@@ -523,10 +545,11 @@
         (slabs, low, high),
         limit=8,
     )
-    cx, cy, cz = call(
+    cy = coulomb[1]
+    cx, cz = call(
         functools.partial(factors_kernel, lines, width),
         "factors",
-        (shape(width * lines, width * lines), shape(width, 8 * width), shape(128, 128)),
+        (shape(width * lines, width * lines), shape(128, 128)),
         (coulomb,),
     )
     trial_window, diag_window, cx, cy, cz, shift_rows, own_half = lax.optimization_barrier(
@@ -564,7 +587,7 @@
             "combine",
             shape(n, up8((slab + share) * lines), 128),
             (flags, exchange_group(pay), v, spread_orbitals, u1, u2, cy, cz),
-            scratch=[pltpu.VMEM((8 * width, 128), F32)],
+            scratch=[pltpu.VMEM((slab * width, 128), F32)],
             limit=4,
             in_smem=(0,),
         )
@@ -574,7 +597,7 @@
     mapped, trial_rows, pay = call(
         functools.partial(mapped_kernel, slab, lines, width, group),
         "mapped",
-        (shape(width * lines, 128), shape(width * lines, 128), shape(n, up8(used) + 8, 128)),
+        (shape(width * lines, 128), shape(width * lines, 128), shape(n, up8(used + 3), 128)),
         (got, cx),
     )
     got, scales = response((trial_window, exchange(pay)))

time: 166 us -> 156 us (0.940)
  Pallas kernels: 40.7 us -> 32.1 us
    pallas_call x13, Pallas kernels: 40.7 us -> 32.1 us  [call(): pl.pallas_call(kernel, out_shape=shapes, in_specs=[smem() if k in in_smem...]
where the time goes in v4:
time: 156 us
  blocking collectives  78.1 us (50%)
  Pallas kernels  32.1 us (21%)
  waiting for transfers between devices  20.3 us (13%)
  starting transfers between devices  17.9 us (11%)
  other arithmetic  4.45 us (3%)
  local copies, waits for them, and re-layouts  2.73 us (2%)
    all_to_all x4, blocking collectives, exchange(): return lax.all_to_all(x, 'orb', split_axis=0, concat_axis=0, tiled=True)  53.8 us
    pallas_call x13, Pallas kernels, call(): pl.pallas_call(kernel, out_shape=shapes, in_specs=[smem() if k in in_smem...  32.1 us
    all_to_all x2, blocking collectives, exchange_group(): lax.all_to_all(x, 'orb', split_axis=0, concat_axis=0, tiled=True, axis_in...  24.3 us
    ppermute x2, starting transfers between devices, shards(): lax.ppermute(fields, 'orb', [(j * rounds + k, (k + r) % rounds * group +...  9.53 us
    ppermute x2, waiting for transfers between devices, shards(): lax.ppermute(fields, 'orb', [(j * rounds + k, (k + r) % rounds * group +...  7.43 us
    ppermute x2, waiting for transfers between devices, shards(): lax.ppermute(edge, 'orb', [((j - 1) * rounds + 1, q * group + j) for j in...  6.63 us
    ppermute x3, waiting for transfers between devices, swap(): lax.ppermute(x, 'trial', [(k, (k + 1) % cores) for k in range(cores)])  6.25 us
    all_to_all x1, starting transfers between devices, exchange_group(): lax.all_to_all(x, 'orb', split_axis=0, concat_axis=0, tiled=True, axis_in...  6.18 us
  transfers between devices with their start and end apart: 8, of which 5 were waited for; matrix products, arithmetic and copies ran while one was open for 3% of the time, Pallas kernels for 1%

profile of v4, /device:TPU:0, one launch (start us, length us, event | category | flops | bytes accessed | tf_op | source)
XLA Modules:
  0.0 155.9 jit_solution(1400436203418630807)
XLA Ops:
  0.0 0.0 copy-start.2
  0.0 0.0 copy-start.1
  0.0 1.1 dynamic-slice_convert_fusion
  1.2 0.0 copy-start.3
  1.2 0.0 copy-start.4
  1.2 0.0 copy-start.5
  1.2 0.0 copy-start.6
  1.2 0.0 copy-start
  1.2 0.2 reshape.28.src_ref
  1.4 1.3 pack_orbitals.1
  2.7 6.2 %all-to-all-start = ((f32[8,416,128]{2,1,0:T(8,128)}), f32[8,416,128]{2,1,0:T(8,128)S(1)}, u32[]{:S(2)}, u32[]{:S(2)}) async-start(f32[8,416,128]{2,1,0:T(8,128)} %pack_orbitals.1), calls=%async_computation | async-start | bytes 3407872 | tf_op jit(solution)/shard_map/all_to_all | solution.py:473
  8.9 0.0 copy-done.2
  9.0 0.0 copy-done.1
  9.0 0.1 concatenate.12
  9.1 1.3 collective-permute-start.3
  10.4 0.7 collective-permute-start.2
  11.1 8.9 %collective-permute-start.1 = (f32[3,128,128]{2,1,0:T(8,128)S(1)}, f32[3,128,128]{2,1,0:T(8,128)S(1)}, u32[]{:S(2)}, u32[]{:S(2)}) collective-permute-start(f32[3,128,128]{2,1,0:T(8,128)S(1)} %constant_dynamic-update-slice_fusion), channel_id=1, source_target_pairs={{0,16},{2,0},{4,18},{6,2},{8,20},{10,4},{12,22},{14,6},{16,24},{18... | collective-permute-start | bytes 589832 | tf_op jit(solution)/shard_map/ppermute | solution.py:501
  20.0 0.7 collective-permute-start
  20.7 0.0 copy-done.3
  20.7 0.0 copy-done.4
  20.7 0.2 fusion.1
  20.9 0.0 copy-done.5
  20.9 0.0 copy-done.6
  20.9 0.2 fusion
  21.1 0.6 fusion.3
  21.7 1.4 broadcast_select_fusion.1
  23.1 0.6 fusion.2
  23.7 0.0 copy-done
  23.7 1.4 select_add_fusion.refs_3_
  25.1 0.8 factors.1
  26.0 0.1 pad_add_fusion.flag_ref.refs_0_
  26.1 6.6 %collective-permute-done.3 = f32[3,96,128]{2,1,0:T(8,128)S(1)} collective-permute-done((f32[3,96,128]{2,1,0:T(8,128)S(1)}, f32[3,96,128]{2,1,0:T(8,128)S(1)}, u32[]{:S(2)}, u32[]{:S(2)}) %collective-permute-start.3) | collective-permute-done | bytes 147488 | tf_op jit(solution)/shard_map/ppermute | solution.py:524
  32.7 0.0 collective-permute-done.2
  32.7 7.4 %collective-permute-done.1.refs_1_ = f32[3,128,128]{2,1,0:T(8,128)S(1)} collective-permute-done((f32[3,128,128]{2,1,0:T(8,128)S(1)}, f32[3,128,128]{2,1,0:T(8,128)S(1)}, u32[]{:S(2)}, u32[]{:S(2)}) %collective-permute-start.1) | collective-permute-done | bytes 196640 | tf_op jit(solution)/shard_map/ppermute | solution.py:501
  40.2 0.0 collective-permute-done.refs_0_
  40.2 0.6 slab.1.slab_ref
  40.7 0.3 fields.1
  41.1 0.0 all-to-all-done
  41.1 0.1 collective-permute-start.4
  41.1 3.6 %collective-permute-done.4.other_ref = f32[3328,128]{1,0:T(8,128)S(1)} collective-permute-done((f32[3328,128]{1,0:T(8,128)S(1)}, f32[3328,128]{1,0:T(8,128)S(1)}, u32[]{:S(2)}, u32[]{:S(2)}) %collective-permute-start.4) | collective-permute-done | bytes 1703968 | tf_op jit(solution)/shard_map/ppermute | solution.py:467
  44.7 2.9 %spread_orbitals.1.refs_1_.o_ref = bf16[13,64,16,128]{3,2,1,0:T(8,128)(2,1)S(1)} custom-call(f32[3328,128]{1,0:T(8,128)S(1)} %bitcast.10, f32[3328,128]{1,0:T(8,128)S(1)} %collective-permute-done.4.other_ref), custom_call_target="tpu_custom_call" | custom-call | tf_op jit(solution)/shard_map/spread_orbitals/pallas_call | solution.py:432
  47.6 8.4 %krylov.2 = (f32[11,64,16,128]{3,2,1,0:T(8,128)S(1)}, f32[9,64,16,128]{3,2,1,0:T(8,128)S(1)}, f32[8,16,128]{2,1,0:T(8,128)S(1)}) custom-call(s32[3]{0:T(128)S(1)} %pad_add_fusion.flag_ref.refs_0_, bf16[13,64,16,128]{3,2,1,0:T(8,128)(2,1)S(1)} %spread_orbitals.1.refs_1_.o_ref, f32[16,52,128]{2,1,0:T(8,128)S(1)} %get-tuple-element.32.refs_2_, ...), custom_call_target="tpu_custom_call" | custom-call | tf_op jit(solution)/shard_map/krylov/pallas_call | solution.py:432
  56.0 15.6 %all_to_all.35.pay_ref = f32[8,16,128]{2,1,0:T(8,128)S(1)} all-to-all(f32[8,16,128]{2,1,0:T(8,128)S(1)} %get-tuple-element.35), channel_id=1, replica_groups={{0,2,4,6,8,10,12,14},{16,18,20,22,24,26,28,30},{1,3,5,7,9,11,13,15},{17..., dimensions={0} | all-to-all | bytes 131072 | tf_op jit(solution)/shard_map/all_to_all | solution.py:473
  71.6 3.6 %combine.2 = f32[16,48,128]{2,1,0:T(8,128)S(1)} custom-call(s32[3]{0:T(128)S(1)} %pad_add_fusion.flag_ref.refs_0_, f32[8,16,128]{2,1,0:T(8,128)S(1)} %all_to_all.35.pay_ref, f32[16,52,128]{2,1,0:T(8,128)S(1)} %get-tuple-element.34.refs_4_.v_ref, bf16[13,64,16,128]{3,2,1,0:T(8,128)(2,1)S(1)} %spread_orbitals.1.refs_1_.o_ref, ...), custom_call_target="tpu_custom_call" | custom-call | tf_op jit(solution)/shard_map/combine/pallas_call | solution.py:432
  75.2 14.3 %all_to_all.36.got_ref = f32[16,48,128]{2,1,0:T(8,128)S(1)} all-to-all(f32[16,48,128]{2,1,0:T(8,128)S(1)} %combine.2), channel_id=1, replica_groups=mesh['orb'=16,'trial'=2] {'orb'}, dimensions={0} | all-to-all | bytes 786432 | tf_op jit(solution)/shard_map/all_to_all | solution.py:470
  89.5 0.4 mapped.1
  89.9 16.0 %all_to_all.37.refs_5_ = f32[16,56,128]{2,1,0:T(8,128)S(1)} all-to-all(f32[16,56,128]{2,1,0:T(8,128)S(1)} %get-tuple-element.41), channel_id=1, replica_groups=mesh['orb'=16,'trial'=2] {'orb'}, dimensions={0} | all-to-all | bytes 917504 | tf_op jit(solution)/shard_map/all_to_all | solution.py:470
  106.0 8.8 %krylov.3 = (f32[11,64,16,128]{3,2,1,0:T(8,128)S(1)}, f32[9,64,16,128]{3,2,1,0:T(8,128)S(1)}, f32[8,16,128]{2,1,0:T(8,128)S(1)}, f32[16,52,128]{2,1,0:T(8,128)S(1)}, f32[8,128]{1,0:T(8,128)S(1)}) custom-call(s32[3]{0:T(128)S(1)} %pad_add_fusion.flag_ref.refs_0_, bf16[13,64,16,128]{3,2,1,0:T(8,128)(2,1)S(1)} %spread_orbitals.1.refs_1_.o_ref, ...), custom_call_target="tpu_custom_call" | custom-call | tf_op jit(solution)/shard_map/krylov/pallas_call | solution.py:432
  114.8 8.7 %all_to_all.38.pay_ref = f32[8,16,128]{2,1,0:T(8,128)S(1)} all-to-all(f32[8,16,128]{2,1,0:T(8,128)S(1)} %get-tuple-element.42), channel_id=1, replica_groups={{0,2,4,6,8,10,12,14},{16,18,20,22,24,26,28,30},{1,3,5,7,9,11,13,15},{17..., dimensions={0} | all-to-all | bytes 131072 | tf_op jit(solution)/shard_map/all_to_all | solution.py:473
  123.5 3.6 %combine.3 = f32[16,32,128]{2,1,0:T(8,128)S(1)} custom-call(s32[3]{0:T(128)S(1)} %pad_add_fusion.flag_ref.refs_0_, f32[8,16,128]{2,1,0:T(8,128)S(1)} %all_to_all.38.pay_ref, f32[16,52,128]{2,1,0:T(8,128)S(1)} %get-tuple-element.43.v_ref, bf16[13,64,16,128]{3,2,1,0:T(8,128)(2,1)S(1)} %spread_orbitals.1.refs_1_.o_ref, ...), custom_call_target="tpu_custom_call" | custom-call | tf_op jit(solution)/shard_map/combine/pallas_call | solution.py:432
  127.1 11.2 %all_to_all.39.got_ref = f32[16,32,128]{2,1,0:T(8,128)S(1)} all-to-all(f32[16,32,128]{2,1,0:T(8,128)S(1)} %combine.3), channel_id=1, replica_groups=mesh['orb'=16,'trial'=2] {'orb'}, dimensions={0} | all-to-all | bytes 524288 | tf_op jit(solution)/shard_map/all_to_all | solution.py:470
  138.2 0.4 second.1.second_ref
  138.6 0.1 collective-permute-start.5
  138.7 1.3 collective-permute-done.5.other_ref
  140.0 0.2 gram.1
  140.2 12.3 %all_to_all.40.got_ref = f32[16,24,128]{2,1,0:T(8,128)S(1)} all-to-all(f32[16,24,128]{2,1,0:T(8,128)S(1)} %gram.1), channel_id=1, replica_groups=mesh['orb'=16,'trial'=2] {'orb'}, dimensions={0} | all-to-all | bytes 393216 | tf_op jit(solution)/shard_map/all_to_all | solution.py:470
  152.5 0.1 collective-permute-start.6
  152.6 1.3 collective-permute-done.6.other_ref
  153.9 0.9 final.1
  154.8 0.2 reshape.25
  155.0 0.1 copy.10
  155.1 0.9 reshape.26
  (11 shorter events, 0.2 us)
Async XLA Ops:
  0.0 8.9 %copy-start.2 = (f32[4,4096]{1,0:T(4,128)S(1)}, f32[4,4096]{1,0:T(4,128)}, u32[]{:S(2)}) copy-start(f32[4,4096]{1,0:T(4,128)} %param.10) | copy-start | bytes 196612
  0.0 9.0 %copy-start.1 = (f32[2,4,4096]{2,1,0:T(4,128)S(1)}, f32[2,4,4096]{2,1,0:T(4,128)}, u32[]{:S(2)}) copy-start(f32[2,4,4096]{2,1,0:T(4,128)} %param.8) | copy-start | bytes 393220
  1.2 19.5 %copy-start.3 = (f32[32]{0:T(128)S(1)}, f32[32]{0:T(128)}, u32[]{:S(2)}) copy-start(f32[32]{0:T(128)} %param.12) | copy-start | bytes 388
  1.2 19.5 %copy-start.4 = (s32[2]{0:T(128)S(1)}, s32[2]{0:T(128)}, u32[]{:S(2)}) copy-start(s32[2]{0:T(128)} %param.14) | copy-start | bytes 28
  1.2 19.7 %copy-start.5 = (f32[8]{0:T(128)S(1)}, f32[8]{0:T(128)}, u32[]{:S(2)}) copy-start(f32[8]{0:T(128)} %param.13) | copy-start | bytes 100
  1.2 19.7 %copy-start.6 = (s32[2]{0:T(128)S(1)}, s32[2]{0:T(128)}, u32[]{:S(2)}) copy-start(s32[2]{0:T(128)} %param.15) | copy-start | bytes 28
  1.2 22.5 %copy-start = (f32[3,64,64]{2,1,0:T(8,128)S(1)}, f32[3,64,64]{2,1,0:T(8,128)}, u32[]{:S(2)}) copy-start(f32[3,64,64]{2,1,0:T(8,128)} %c_ref.1) | copy-start | bytes 147460
  2.7 38.3 %all-to-all-start = ((f32[8,416,128]{2,1,0:T(8,128)}), f32[8,416,128]{2,1,0:T(8,128)S(1)}, u32[]{:S(2)}, u32[]{:S(2)}) async-start(f32[8,416,128]{2,1,0:T(8,128)} %pack_orbitals.1), calls=%async_computation | async-start | bytes 3407872 | tf_op jit(solution)/shard_map/all_to_all | solution.py:473
  9.1 23.5 %collective-permute-start.3 = (f32[3,96,128]{2,1,0:T(8,128)S(1)}, f32[3,96,128]{2,1,0:T(8,128)S(1)}, u32[]{:S(2)}, u32[]{:S(2)}) collective-permute-start(f32[3,96,128]{2,1,0:T(8,128)S(1)} %slice_select_fusion), channel_id=1, source_target_pairs={{2,18},{6,20},{10,22},{14,24},{18,26},{22,28},{26,30},{4,0},{8,2},... | collective-permute-start | bytes 442376 | tf_op jit(solution)/shard_map/ppermute | solution.py:524
  10.4 22.2 %collective-permute-start.2 = (f32[3,96,128]{2,1,0:T(8,128)S(1)}, f32[3,96,128]{2,1,0:T(8,128)S(1)}, u32[]{:S(2)}, u32[]{:S(2)}) collective-permute-start(f32[3,96,128]{2,1,0:T(8,128)S(1)} %slice_select_fusion), channel_id=1, source_target_pairs={{2,2},{6,4},{10,6},{14,8},{18,10},{22,12},{26,14},{4,16},{8,18},{1... | collective-permute-start | bytes 442376 | tf_op jit(solution)/shard_map/ppermute | solution.py:524
  11.1 29.0 %collective-permute-start.1 = (f32[3,128,128]{2,1,0:T(8,128)S(1)}, f32[3,128,128]{2,1,0:T(8,128)S(1)}, u32[]{:S(2)}, u32[]{:S(2)}) collective-permute-start(f32[3,128,128]{2,1,0:T(8,128)S(1)} %constant_dynamic-update-slice_fusion), channel_id=1, source_target_pairs={{0,16},{2,0},{4,18},{6,2},{8,20},{10,4},{12,22},{14,6},{16,24},{18... | collective-permute-start | bytes 589832 | tf_op jit(solution)/shard_map/ppermute | solution.py:501
  20.0 20.2 %collective-permute-start = (f32[3,128,128]{2,1,0:T(8,128)S(1)}, f32[3,128,128]{2,1,0:T(8,128)S(1)}, u32[]{:S(2)}, u32[]{:S(2)}) collective-permute-start(f32[3,128,128]{2,1,0:T(8,128)S(1)} %constant_dynamic-update-slice_fusion), channel_id=1, source_target_pairs={{0,0},{2,16},{4,2},{6,18},{8,4},{10,20},{12,6},{14,22},{16,8},{18,... | collective-permute-start | bytes 589832 | tf_op jit(solution)/shard_map/ppermute | solution.py:501
  41.1 3.7 %collective-permute-start.4 = (f32[3328,128]{1,0:T(8,128)S(1)}, f32[3328,128]{1,0:T(8,128)S(1)}, u32[]{:S(2)}, u32[]{:S(2)}) collective-permute-start(f32[3328,128]{1,0:T(8,128)S(1)} %bitcast.9), channel_id=1, source_target_pairs={{0,1},{1,0},{2,3},{3,2},{4,5},{5,4},{6,7},{7,6},{8,9},{9,8},{10,11... | collective-permute-start | bytes 5111816 | tf_op jit(solution)/shard_map/ppermute | solution.py:467
  138.6 1.4 collective-permute-start.5
  152.5 1.4 collective-permute-start.6

commit v5 on v4

--- a/solution.py
+++ b/solution.py
@@ -10,6 +10,7 @@
 HIGH = 3
 CENTER = 4.25
 ORBS = 16
+HALF = 8
 SHIFT_LANE = 12
 MOMENTS = 6
 HIGHEST = lax.Precision.HIGHEST
@@ -46,18 +47,16 @@
     return picked_freq - picked_energy
 
 
-def spread_kernel(window, pairs, own_ref, other_ref, dst_ref):
-    half = ORBS // 2
+def spread_kernel(window, pairs, src_ref, dst_ref):
     rows = window * pairs
-    first_half = lax.broadcasted_iota(jnp.int32, (ORBS, 128), 1) < 64
+    first_half = lax.broadcasted_iota(jnp.int32, (HALF, 128), 1) < 64
 
     def body(w, carry):
         for i in range(pairs):
-            at = pl.ds(w * pairs + i, half, stride=rows)
-            pair = jnp.concatenate([own_ref[at, :], other_ref[at, :]], axis=0)
+            pair = src_ref[pl.ds(w * pairs + i, HALF, stride=rows), :]
             turned = pltpu.roll(pair, 64, 1)
-            dst_ref[w, 2 * i] = jnp.where(first_half, pair, turned).astype(jnp.bfloat16)
-            dst_ref[w, 2 * i + 1] = jnp.where(first_half, turned, pair).astype(jnp.bfloat16)
+            dst_ref[w, 2 * i] = jnp.where(first_half, pair, turned)
+            dst_ref[w, 2 * i + 1] = jnp.where(first_half, turned, pair)
         return carry
 
     lax.fori_loop(0, window, body, 0)
@@ -131,18 +130,22 @@
                     d_ref[y // lines, row : row + 1, :] = d[h][i : i + 1]
 
 
-def krylov_kernel(slab, lines, width, group, filtered, *refs):
-    flag_ref, o_ref, d_ref, sh_ref, t_ref = refs[:5]
-    if filtered:
-        m_ref, u1_ref, u2_ref, pay_ref, v_ref, cs_ref, b_s = refs[5:]
-    else:
-        u1_ref, u2_ref, pay_ref, b_s = refs[5:]
-        v_ref = t_ref
+def krylov_kernel(slab, lines, width, group, filtered, parts, before, *refs):
+    refs = list(refs)
+    take = lambda k: [refs.pop(0) for _ in range(k)]
+    flag_ref, d_ref, sh_ref, t_ref = take(4)
+    (m_ref,) = take(1) if filtered else (None,)
+    packed_refs = take(before)
+    o_refs = take(len(parts))
+    u_refs = [take(2) for _ in parts]
+    (pay_ref,) = take(1)
+    v_ref, cs_ref = take(2) if filtered else (t_ref, None)
+    (b_s,) = refs
     window = slab + LOW + HIGH
-    lane = lax.broadcasted_iota(jnp.int32, (ORBS, 128), 1)
+    lane = lax.broadcasted_iota(jnp.int32, (HALF, 128), 1)
     at_low = lane % width == 0
     at_high = lane % width == width - 1
-    zero = jnp.zeros((ORBS, 128), F32)
+    zero = jnp.zeros((HALF, 128), F32)
     n = t_ref.shape[0]
 
     if filtered:
@@ -166,80 +169,97 @@
     def d_row(w, y):
         return d_ref[y // lines, pl.ds(w * lines + y % lines, 1), :]
 
+    b_refs = [b_s.at[k] for k in range(len(parts))]
+    u1_refs, u2_refs = zip(*u_refs)
+
     def products(w, carry):
         for y in range(width):
-            b_s[w, y] = o_ref[w, y].astype(F32) * v_row(w, y)
+            v = v_row(w, y)
+            for b_ref, o_ref in zip(b_refs, o_refs):
+                b_ref[w, y] = o_ref[w, y] * v
         return carry
 
+    def apply(srcs, src_at, dsts, dst_at, w, carry, pairs, keep=None):
+        fields = [[zero] + [src[w - src_at, y] for y in range(width)] + [zero] for src in srcs]
+        terms = [[] for _ in srcs for _ in pairs]
+        for y in range(width):
+            diag = d_row(w, y)
+            for k, (rows, src, dst) in enumerate(zip(fields, srcs, dsts)):
+                mid = rows[y + 1]
+                around = (rows[y] + rows[y + 2]) + (src[w - 1 - src_at, y] + src[w + 1 - src_at, y])
+                around = around + (
+                    jnp.where(at_low, 0.0, pltpu.roll(mid, 1, 1))
+                    + jnp.where(at_high, 0.0, pltpu.roll(mid, 127, 1))
+                )
+                new = diag * mid - around
+                if keep is not None:
+                    new = new * keep
+                dst[w - dst_at, y] = new
+                both = (mid, new)
+                for i, (a, b) in enumerate(pairs):
+                    terms[k * len(pairs) + i].append(both[a] * both[b])
+        return tuple(old + tree(t) for old, t in zip(carry, terms))
+
+    def last(w, carry):
+        fields = [[u2_ref[w - LOW, y] for y in range(width)] + [zero] for u2_ref in u2_refs]
+        terms = [[] for _ in fields]
+        for y in range(width):
+            diag = d_row(w, y)
+            for k, (rows, u2_ref) in enumerate(zip(fields, u2_refs)):
+                mid = rows[y]
+                above = (rows[y + 1] + u2_ref[w + 1 - LOW, y]) + jnp.where(
+                    at_high, 0.0, pltpu.roll(mid, 127, 1)
+                )
+                terms[k].append(mid * (diag * mid - 2.0 * above))
+        return tuple(old + tree(t) for old, t in zip(carry, terms))
+
+    first = flag_ref[0]
+    own, top = (LOW, LOW + slab), LOW + slab
+    inside = {
+        LOW - 1: jnp.where(first < 1, 0.0, 1.0),
+        top: jnp.where(first + slab >= width, 0.0, 1.0),
+        top + 1: jnp.where(first + slab + 1 >= width, 0.0, 1.0),
+    }
     lax.fori_loop(0, window, products, 0)
-
-    def apply(src, src_at, dst, dst_at, w, carry, pairs):
-        rows = [zero] + [src[w - src_at, y] for y in range(width)] + [zero]
-        terms = [[] for _ in carry]
-        for y in range(width):
-            mid = rows[y + 1]
-            around = (rows[y] + rows[y + 2]) + (src[w - 1 - src_at, y] + src[w + 1 - src_at, y])
-            around = around + (
-                jnp.where(at_low, 0.0, pltpu.roll(mid, 1, 1))
-                + jnp.where(at_high, 0.0, pltpu.roll(mid, 127, 1))
-            )
-            new = d_row(w, y) * mid - around
-            dst[w - dst_at, y] = new
-            both = (mid, new)
-            for list_at, (a, b) in zip(terms, pairs):
-                list_at.append(both[a] * both[b])
-        return tuple(old + tree(t) for old, t in zip(carry, terms))
-
-    def halo(src, src_at, dst, dst_at, w, outside):
-        @pl.when(outside)
-        def _():
-            dst[w - dst_at] = jnp.zeros((width, ORBS, 128), F32)
-
-        @pl.when(jnp.logical_not(outside))
-        def _():
-            apply(src, src_at, dst, dst_at, w, (), ())
-
-    first = flag_ref[0]
-    own = (LOW, LOW + slab)
-    halo(b_s, 0, u1_ref, 1, LOW - 1, first < 1)
-    m0, m1, m2 = lax.fori_loop(
+    for w, keep in inside.items():
+        apply(b_refs, 0, u1_refs, 1, w, (), (), keep)
+    low_pairs, high_pairs = ((0, 0), (0, 1), (1, 1)), ((0, 1), (1, 1))
+    lows = lax.fori_loop(
         *own,
-        lambda w, c: apply(b_s, 0, u1_ref, 1, w, c, ((0, 0), (0, 1), (1, 1))), (zero,) * 3,
+        lambda w, c: apply(b_refs, 0, u1_refs, 1, w, c, low_pairs),
+        (zero,) * 3 * len(parts),
         unroll=True,
     )
-    halo(b_s, 0, u1_ref, 1, LOW + slab, first + slab >= width)
-    halo(b_s, 0, u1_ref, 1, LOW + slab + 1, first + slab + 1 >= width)
-    m3, m4 = lax.fori_loop(
+    apply(u1_refs, 1, u2_refs, LOW, top, (), (), inside[top])
+    highs = lax.fori_loop(
         *own,
-        lambda w, c: apply(u1_ref, 1, u2_ref, LOW, w, c, ((0, 1), (1, 1))), (zero,) * 2,
+        lambda w, c: apply(u1_refs, 1, u2_refs, LOW, w, c, high_pairs),
+        (zero,) * 2 * len(parts),
         unroll=True,
     )
-    halo(u1_ref, 1, u2_ref, LOW, LOW + slab, first + slab >= width)
-
-    def last(w, carry):
-        rows = [u2_ref[w - LOW, y] for y in range(width)] + [zero]
-        terms = []
-        for y in range(width):
-            mid = rows[y]
-            above = (rows[y + 1] + u2_ref[w + 1 - LOW, y]) + jnp.where(
-                at_high, 0.0, pltpu.roll(mid, 127, 1)
-            )
-            terms.append(mid * (d_row(w, y) * mid - 2.0 * above))
-        return carry + tree(terms)
-
-    m5 = lax.fori_loop(*own, last, zero, unroll=True)
+    lasts = lax.fori_loop(*own, last, (zero,) * len(parts), unroll=True)
     column = lax.broadcasted_iota(jnp.int32, (128, 128), 1)
-    half = lax.broadcasted_iota(jnp.int32, (128, 128), 0) // width
-    packed = sh_ref[...]
-    for k, moment in enumerate((m0, m1, m2, m3, m4, m5)):
-        packed = packed + dot(moment, jnp.where(column == 2 * k + half, 1.0, 0.0))
-    for peer in range(group):
-        pay_ref[peer] = packed
+    trial = lax.broadcasted_iota(jnp.int32, (128, 128), 0) // width
+    packed = [ref[...] for ref in packed_refs]
+    for k, part in enumerate(parts):
+        made = sh_ref[part * HALF : (part + 1) * HALF, :]
+        moments = (*lows[3 * k : 3 * k + 3], *highs[2 * k : 2 * k + 2], lasts[k])
+        for i, moment in enumerate(moments):
+            made = made + dot(moment, jnp.where(column == 2 * i + trial, 1.0, 0.0))
+        packed.append(made)
+    if len(packed) * HALF == ORBS:
+        for peer in range(group):
+            for k, made in enumerate(packed):
+                pay_ref[peer, k * HALF : (k + 1) * HALF, :] = made
+    else:
+        pay_ref[...] = packed[0]
 
 
 def combine_kernel(
-    slab, lines, width, group, share, flag_ref, pay_ref, v_ref, o_ref, u1_ref, u2_ref, cy_ref, cz_ref, out_ref, field_s
+    slab, lines, width, group, share, flag_ref, pay_ref, v_ref, cy_ref, cz_ref, *refs
 ):
+    o_refs, u_refs = refs[0:2], (refs[2:4], refs[4:6])
+    out_ref, field_s = refs[6:]
     chunks = out_ref.shape[0]
     if share:
         rows = share * lines
@@ -295,10 +315,14 @@
         for y0 in range(0, width, 8):
             values = []
             for y in range(y0, y0 + 8):
-                o = o_ref[w, y].astype(F32)
-                b = o * v_ref[y // lines, pl.ds(w * lines + y % lines, 1), :]
-                part = o * (c0 * b + (c1 * u1_ref[x + LOW - 1, y] + c2 * u2_ref[x, y]))
-                values.append(part[0:8] + part[8:16])
+                v = v_ref[y // lines, pl.ds(w * lines + y % lines, 1), :]
+                both = []
+                for k, (o_ref, (u1_ref, u2_ref)) in enumerate(zip(o_refs, u_refs)):
+                    at = slice(k * HALF, (k + 1) * HALF)
+                    o = o_ref[w, y]
+                    u = c1[at] * u1_ref[x + LOW - 1, y] + c2[at] * u2_ref[x, y]
+                    both.append(o * (c0[at] * (o * v) + u))
+                values.append(both[0] + both[1])
             field_s[pl.ds(pl.multiple_of(x * width + y0, 8), 8), :] = merge(values)
         return carry
 
@@ -368,7 +392,7 @@
         pay_ref[k, size - 8 : size, :] = block
 
 
-def final_kernel(per, width, flag_ref, got_ref, other_ref, out_ref):
+def final_kernel(per, width, flag_ref, got_ref, other_ref, out_ref, rows_s):
     n, size, _ = got_ref.shape
     total = tree([got_ref[k, size - 8 : size, :] for k in range(n)])
     total = dot(total, halves(8, width)) / float(width**3)
@@ -417,7 +441,19 @@
     ]
     for k in range(n):
         a, b = got_ref[k, 0:per, :], other_ref[k]
-        out_ref[k] = (c[0] * a + c[1] * turn(a)) + (c[2] * b + c[3] * turn(b))
+        rows_s[k] = (c[0] * a + c[1] * turn(a)) + (c[2] * b + c[3] * turn(b))
+    planes = out_ref.shape[1]
+    first_half = lax.broadcasted_iota(jnp.int32, (planes, 128), 1) < width
+    lines = per // planes
+
+    def line(y):
+        return rows_s[y // lines, pl.ds(y % lines, planes, stride=lines), :]
+
+    for pair in range(width // 2):
+        even, odd = line(2 * pair), line(2 * pair + 1)
+        at = slice(pair * 128, (pair + 1) * 128)
+        out_ref[0, :, at] = jnp.where(first_half, even, turn(odd))
+        out_ref[1, :, at] = jnp.where(first_half, turn(even), odd)
 
 
 def vmem():
@@ -484,10 +520,10 @@
         limit=8,
     )
     own_half = exchange_group(sent)
-    own_half = own_half.reshape(ORBS // 2 * window * pairs, 128)
+    own_half = own_half.reshape(HALF * window * pairs, 128)
     shifts = orbital_shifts(orbital_ids, freq_index, energies, frequencies)
     shifts = jnp.where(core == 0, shifts, jnp.roll(shifts, -each))
-    slot_rows = [(k // each) * (ORBS // 2) + place * each + k % each for k in range(held)]
+    slot_rows = [(k // each) * HALF + place * each + k % each for k in range(held)]
     row = lax.broadcasted_iota(jnp.int32, (ORBS, 128), 0)
     lane = lax.broadcasted_iota(jnp.int32, (ORBS, 128), 1)
     shift_rows = sum(
@@ -555,52 +591,57 @@
     trial_window, diag_window, cx, cy, cz, shift_rows, own_half = lax.optimization_barrier(
         (trial_window, diag_window, cx, cy, cz, shift_rows, own_half)
     )
-    spread_orbitals = call(
-        functools.partial(spread_kernel, window, pairs),
-        "spread_orbitals",
-        jax.ShapeDtypeStruct((window, width, ORBS, 128), jnp.bfloat16),
-        (own_half, swap(own_half)),
-        limit=4,
-    )
-
-    def response(fields):
+    spread_orbitals = [
+        call(
+            functools.partial(spread_kernel, window, pairs),
+            "spread_orbitals",
+            shape(window, width, HALF, 128),
+            (rows,),
+        )
+        for rows in (own_half, swap(own_half))
+    ]
+
+    def krylov(parts, fields, packed):
         filtered = len(fields) == 2
-        share = 0 if filtered else slab // rounds
-        shapes = [
-            shape(slab + 3, width, ORBS, 128), shape(slab + 1, width, ORBS, 128), shape(group, ORBS, 128),
-        ]
+        complete = len(packed) + len(parts) == 2
+        shapes = [shape(slab + 3, width, HALF, 128), shape(slab + 1, width, HALF, 128)] * len(parts)
+        shapes.append(shape(group, ORBS, 128) if complete else shape(HALF, 128))
         if filtered:
             shapes += [shape(n, used, 128), shape(8, 128)]
-        made = call(
-            functools.partial(krylov_kernel, slab, lines, width, group, filtered),
+        return call(
+            functools.partial(krylov_kernel, slab, lines, width, group, filtered, parts, len(packed)),
             "krylov",
             tuple(shapes),
-            (flags, spread_orbitals, diag_window, shift_rows, *fields),
-            scratch=[pltpu.VMEM((window, width, ORBS, 128), F32)],
+            (flags, diag_window, shift_rows, *fields, *packed, *[spread_orbitals[k] for k in parts]),
+            scratch=[pltpu.VMEM((len(parts), window, width, HALF, 128), F32)],
             limit=14,
             in_smem=(0,),
         )
-        u1, u2, pay = made[:3]
-        v = made[3] if filtered else fields[0]
+
+    def combine(pay, v, us, share):
         part = call(
             functools.partial(combine_kernel, slab, lines, width, group, share),
             "combine",
             shape(n, up8((slab + share) * lines), 128),
-            (flags, exchange_group(pay), v, spread_orbitals, u1, u2, cy, cz),
+            (flags, exchange_group(pay), v, cy, cz, *spread_orbitals, *us),
             scratch=[pltpu.VMEM((slab * width, 128), F32)],
             limit=4,
             in_smem=(0,),
         )
-        return exchange(part), (made[4] if filtered else None)
-
-    got, _ = response((trial_window,))
+        return exchange(part)
+
+    own_u1, own_u2, packed = krylov((0,), (trial_window,), ())
+    other_u1, other_u2, pay = krylov((1,), (trial_window,), (packed,))
+    got = combine(pay, trial_window, (own_u1, own_u2, other_u1, other_u2), slab // rounds)
     mapped, trial_rows, pay = call(
         functools.partial(mapped_kernel, slab, lines, width, group),
         "mapped",
         (shape(width * lines, 128), shape(width * lines, 128), shape(n, up8(used + 3), 128)),
         (got, cx),
     )
-    got, scales = response((trial_window, exchange(pay)))
+    made = krylov((0, 1), (trial_window, exchange(pay)), ())
+    pay, v, scales = made[4:]
+    got = combine(pay, v, made[:4], 0)
     second = call(
         functools.partial(second_kernel, group),
         "second",
@@ -610,15 +651,14 @@
     per = planes * lines
     pay = call(functools.partial(gram_kernel, per), "gram", shape(n, up8(per) + 8, 128), (second, swap(second)))
     got = exchange(pay)
-    result = call(
+    return call(
         functools.partial(final_kernel, per, width),
         "final",
-        shape(n, per, 128),
+        shape(count, planes, cells),
         (flags, got, swap(got[:, :per])),
+        scratch=[pltpu.VMEM((n, per, 128), F32)],
         in_smem=(0,),
     )
-    result = result.reshape(n, planes, lines, count, width).transpose(3, 1, 0, 2, 4)
-    return result.reshape(count, planes, cells)
 
 
 def solution(mesh):

time: 156 us -> 155 us (level)
  waiting for transfers between devices: 20.3 us -> 17.1 us
  Pallas kernels: 32.1 us -> 35 us
    ppermute x3, waiting for transfers between devices: 6.25 us -> 2.67 us  [swap(): lax.ppermute(x, 'trial', [(k, (k + 1) % cores) for k in range(cores)])]
    pallas_call x13 -> x15, Pallas kernels: 32.1 us -> 35 us  [call(): pl.pallas_call(kernel, out_shape=shapes, in_specs=[smem() if k in in_smem...]
  transfers between devices with their start and end apart: 8 -> 8, of which waited for: 5 -> 4; matrix products, arithmetic and copies ran while one was open for 3% -> 3% of each run, Pallas kernels for 1% -> 5%
where the time goes in v5:
time: 155 us; the launch traced here: 154 us
  blocking collectives  78.2 us (50%)
  Pallas kernels  35 us (23%)
  starting transfers between devices  18 us (12%)
  waiting for transfers between devices  17.1 us (11%)
  other arithmetic  4.16 us (3%)
    all_to_all x4, blocking collectives, exchange(): return lax.all_to_all(x, 'orb', split_axis=0, concat_axis=0, tiled=True)  54.5 us
    pallas_call x15, Pallas kernels, call(): pl.pallas_call(kernel, out_shape=shapes, in_specs=[smem() if k in in_smem...  35 us
    all_to_all x2, blocking collectives, exchange_group(): lax.all_to_all(x, 'orb', split_axis=0, concat_axis=0, tiled=True, axis_in...  23.7 us
    ppermute x2, starting transfers between devices, shards(): lax.ppermute(fields, 'orb', [(j * rounds + k, (k + r) % rounds * group +...  9.53 us
    ppermute x2, waiting for transfers between devices, shards(): lax.ppermute(fields, 'orb', [(j * rounds + k, (k + r) % rounds * group +...  7.43 us
    ppermute x2, waiting for transfers between devices, shards(): lax.ppermute(edge, 'orb', [((j - 1) * rounds + 1, q * group + j) for j in...  6.97 us
    all_to_all x1, starting transfers between devices, exchange_group(): lax.all_to_all(x, 'orb', split_axis=0, concat_axis=0, tiled=True, axis_in...  6.33 us
  transfers between devices with their start and end apart: 8, of which 4 were waited for; matrix products, arithmetic and copies ran while one was open for 3% of the time, Pallas kernels for 5%

profile of v5, /device:TPU:0, one launch (start us, length us, event | category | flops | bytes accessed | tf_op | source)
XLA Modules:
  0.0 154.3 jit_solution(3889788624457247354)
XLA Ops:
  0.0 1.1 dynamic-slice_convert_fusion
  1.1 0.2 reshape.20.src_ref
  1.3 1.3 pack_orbitals.1
  2.6 0.0 copy-start.2
  2.6 0.0 copy-start.1
  2.6 0.0 copy-start.3
  2.6 0.0 copy-start.4
  2.6 0.0 copy-start.5
  2.6 0.0 copy-start.6
  2.6 0.0 copy-start
  2.7 6.3 %all-to-all-start = ((f32[8,416,128]{2,1,0:T(8,128)}), f32[8,416,128]{2,1,0:T(8,128)S(1)}, u32[]{:S(2)}, u32[]{:S(2)}) async-start(f32[8,416,128]{2,1,0:T(8,128)} %pack_orbitals.1), calls=%async_computation | async-start | bytes 3407872 | tf_op jit(solution)/shard_map/all_to_all | solution.py:509
  9.0 0.0 copy-done.2
  9.0 0.0 copy-done.1
  9.1 0.1 concatenate.12
  9.2 1.3 collective-permute-start.3
  10.5 0.7 collective-permute-start.2
  11.2 8.9 %collective-permute-start.1 = (f32[3,128,128]{2,1,0:T(8,128)S(1)}, f32[3,128,128]{2,1,0:T(8,128)S(1)}, u32[]{:S(2)}, u32[]{:S(2)}) collective-permute-start(f32[3,128,128]{2,1,0:T(8,128)S(1)} %constant_dynamic-update-slice_fusion), channel_id=1, source_target_pairs={{0,16},{2,0},{4,18},{6,2},{8,20},{10,4},{12,22},{14,6},{16,24},{18... | collective-permute-start | bytes 589832 | tf_op jit(solution)/shard_map/ppermute | solution.py:537
  20.1 0.7 collective-permute-start
  20.8 0.0 copy-done.3
  20.8 0.0 copy-done.4
  20.8 0.2 fusion.1
  21.0 0.0 copy-done.5
  21.0 0.0 copy-done.6
  21.0 0.2 fusion
  21.2 0.6 fusion.3
  21.8 1.3 broadcast_select_fusion.1
  23.0 0.6 fusion.2
  23.6 0.0 copy-done
  23.6 1.3 select_add_fusion.refs_2_
  24.9 0.8 factors.1
  25.7 0.1 pad_add_fusion.flag_ref.refs_0_
  25.8 7.0 %collective-permute-done.3 = f32[3,96,128]{2,1,0:T(8,128)S(1)} collective-permute-done((f32[3,96,128]{2,1,0:T(8,128)S(1)}, f32[3,96,128]{2,1,0:T(8,128)S(1)}, u32[]{:S(2)}, u32[]{:S(2)}) %collective-permute-start.3) | collective-permute-done | bytes 147488 | tf_op jit(solution)/shard_map/ppermute | solution.py:560
  32.8 0.0 collective-permute-done.2
  32.8 7.4 %collective-permute-done.1.refs_1_ = f32[3,128,128]{2,1,0:T(8,128)S(1)} collective-permute-done((f32[3,128,128]{2,1,0:T(8,128)S(1)}, f32[3,128,128]{2,1,0:T(8,128)S(1)}, u32[]{:S(2)}, u32[]{:S(2)}) %collective-permute-start.1) | collective-permute-done | bytes 196640 | tf_op jit(solution)/shard_map/ppermute | solution.py:537
  40.2 0.0 collective-permute-done.refs_0_
  40.2 0.6 slab.1.slab_ref
  40.8 0.3 fields.1
  41.1 0.0 all-to-all-done
  41.2 0.1 collective-permute-start.4
  41.2 1.8 %spread_orbitals.2.refs_4_.refs_0_.refs_5_ = f32[13,64,8,128]{3,2,1,0:T(8,128)S(1)} custom-call(f32[3328,128]{1,0:T(8,128)S(1)} %bitcast.9), custom_call_target="tpu_custom_call" | custom-call | tf_op jit(solution)/shard_map/spread_orbitals/pallas_call | solution.py:468
  43.1 4.6 %krylov.3 = (f32[11,64,8,128]{3,2,1,0:T(8,128)S(1)}, f32[9,64,8,128]{3,2,1,0:T(8,128)S(1)}, f32[8,128]{1,0:T(8,128)S(1)}) custom-call(s32[3]{0:T(128)S(1)} %pad_add_fusion.flag_ref.refs_0_, f32[16,52,128]{2,1,0:T(8,128)S(1)} %get-tuple-element.36.refs_1_, f32[16,128]{1,0:T(8,128)S(1)} %select_add_fusion.refs_2_, ...), custom_call_target="tpu_custom_call" | custom-call | tf_op jit(solution)/shard_map/krylov/pallas_call | solution.py:468
  47.6 0.0 collective-permute-done.4.src_ref
  47.6 1.8 %spread_orbitals.3.refs_5_.refs_1_.refs_6_ = f32[13,64,8,128]{3,2,1,0:T(8,128)S(1)} custom-call(f32[3328,128]{1,0:T(8,128)S(1)} %collective-permute-done.4.src_ref), custom_call_target="tpu_custom_call" | custom-call | tf_op jit(solution)/shard_map/spread_orbitals/pallas_call | solution.py:468
  49.5 4.7 %krylov.4 = (f32[11,64,8,128]{3,2,1,0:T(8,128)S(1)}, f32[9,64,8,128]{3,2,1,0:T(8,128)S(1)}, f32[8,16,128]{2,1,0:T(8,128)S(1)}) custom-call(s32[3]{0:T(128)S(1)} %pad_add_fusion.flag_ref.refs_0_, f32[16,52,128]{2,1,0:T(8,128)S(1)} %get-tuple-element.36.refs_1_, f32[16,128]{1,0:T(8,128)S(1)} %select_add_fusion.refs_2_, ...), custom_call_target="tpu_custom_call" | custom-call | tf_op jit(solution)/shard_map/krylov/pallas_call | solution.py:468
  54.1 15.3 %all_to_all.35.pay_ref = f32[8,16,128]{2,1,0:T(8,128)S(1)} all-to-all(f32[8,16,128]{2,1,0:T(8,128)S(1)} %get-tuple-element.41), channel_id=1, replica_groups={{0,2,4,6,8,10,12,14},{16,18,20,22,24,26,28,30},{1,3,5,7,9,11,13,15},{17..., dimensions={0} | all-to-all | bytes 131072 | tf_op jit(solution)/shard_map/all_to_all | solution.py:509
  69.4 3.6 %combine.2 = f32[16,48,128]{2,1,0:T(8,128)S(1)} custom-call(s32[3]{0:T(128)S(1)} %pad_add_fusion.flag_ref.refs_0_, f32[8,16,128]{2,1,0:T(8,128)S(1)} %all_to_all.35.pay_ref, f32[16,52,128]{2,1,0:T(8,128)S(1)} %get-tuple-element.38.refs_3_.v_ref, f32[64,64]{1,0:T(8,128)S(1)} %slice_bitcast_fusion.cy_ref, f32[128,128]{1,0:T(8,128)S(1)} %get-tuple-element.43.cz_ref, ...), custom_call_target="tpu_custom_call" | custom-call | tf_op jit(solution)/shard_map/combine/pallas_call | solution.py:468
  73.1 14.7 %all_to_all.36.got_ref = f32[16,48,128]{2,1,0:T(8,128)S(1)} all-to-all(f32[16,48,128]{2,1,0:T(8,128)S(1)} %combine.2), channel_id=1, replica_groups=mesh['orb'=16,'trial'=2] {'orb'}, dimensions={0} | all-to-all | bytes 786432 | tf_op jit(solution)/shard_map/all_to_all | solution.py:506
  87.7 0.4 mapped.1
  88.2 16.4 %all_to_all.37.refs_4_ = f32[16,56,128]{2,1,0:T(8,128)S(1)} all-to-all(f32[16,56,128]{2,1,0:T(8,128)S(1)} %get-tuple-element.49), channel_id=1, replica_groups=mesh['orb'=16,'trial'=2] {'orb'}, dimensions={0} | all-to-all | bytes 917504 | tf_op jit(solution)/shard_map/all_to_all | solution.py:506
  104.5 9.2 %krylov.5 = (f32[11,64,8,128]{3,2,1,0:T(8,128)S(1)}, f32[9,64,8,128]{3,2,1,0:T(8,128)S(1)}, f32[11,64,8,128]{3,2,1,0:T(8,128)S(1)}, f32[9,64,8,128]{3,2,1,0:T(8,...) custom-call(s32[3]{0:T(128)S(1)} %pad_add_fusion.flag_ref.refs_0_, ...), custom_call_target="tpu_custom_call" | custom-call | tf_op jit(solution)/shard_map/krylov/pallas_call | solution.py:468
  113.8 8.4 %all_to_all.38.pay_ref = f32[8,16,128]{2,1,0:T(8,128)S(1)} all-to-all(f32[8,16,128]{2,1,0:T(8,128)S(1)} %get-tuple-element.50), channel_id=1, replica_groups={{0,2,4,6,8,10,12,14},{16,18,20,22,24,26,28,30},{1,3,5,7,9,11,13,15},{17..., dimensions={0} | all-to-all | bytes 131072 | tf_op jit(solution)/shard_map/all_to_all | solution.py:509
  122.1 3.6 %combine.3 = f32[16,32,128]{2,1,0:T(8,128)S(1)} custom-call(s32[3]{0:T(128)S(1)} %pad_add_fusion.flag_ref.refs_0_, f32[8,16,128]{2,1,0:T(8,128)S(1)} %all_to_all.38.pay_ref, f32[16,52,128]{2,1,0:T(8,128)S(1)} %get-tuple-element.51.v_ref, f32[64,64]{1,0:T(8,128)S(1)} %slice_bitcast_fusion.cy_ref, f32[128,128]{1,0:T(8,128)S(1)} %get-tuple-element.43.cz_ref, ...), custom_call_target="tpu_custom_call" | custom-call | tf_op jit(solution)/shard_map/combine/pallas_call | solution.py:468
  125.8 11.2 %all_to_all.39.got_ref = f32[16,32,128]{2,1,0:T(8,128)S(1)} all-to-all(f32[16,32,128]{2,1,0:T(8,128)S(1)} %combine.3), channel_id=1, replica_groups=mesh['orb'=16,'trial'=2] {'orb'}, dimensions={0} | all-to-all | bytes 524288 | tf_op jit(solution)/shard_map/all_to_all | solution.py:506
  137.0 0.4 second.1.second_ref
  137.3 0.1 collective-permute-start.5
  137.4 1.3 collective-permute-done.5.other_ref
  138.8 0.1 gram.1
  138.9 12.3 %all_to_all.40.got_ref = f32[16,24,128]{2,1,0:T(8,128)S(1)} all-to-all(f32[16,24,128]{2,1,0:T(8,128)S(1)} %gram.1), channel_id=1, replica_groups=mesh['orb'=16,'trial'=2] {'orb'}, dimensions={0} | all-to-all | bytes 393216 | tf_op jit(solution)/shard_map/all_to_all | solution.py:506
  151.2 0.1 collective-permute-start.6
  151.3 1.3 collective-permute-done.6.other_ref
  152.6 1.7 %final.1 = f32[2,4,4096]{2,1,0:T(4,128)} custom-call(s32[3]{0:T(128)S(1)} %pad_add_fusion.flag_ref.refs_0_, f32[16,24,128]{2,1,0:T(8,128)S(1)} %all_to_all.40.got_ref, f32[16,16,128]{2,1,0:T(8,128)S(1)} %collective-permute-done.6.other_ref), custom_call_target="tpu_custom_call" | custom-call | tf_op jit(solution)/shard_map/final/pallas_call | solution.py:468
  (11 shorter events, 0.2 us)
Async XLA Ops:
  2.6 6.4 %copy-start.2 = (f32[4,4096]{1,0:T(4,128)S(1)}, f32[4,4096]{1,0:T(4,128)}, u32[]{:S(2)}) copy-start(f32[4,4096]{1,0:T(4,128)} %param.10) | copy-start | bytes 196612
  2.6 6.4 %copy-start.1 = (f32[2,4,4096]{2,1,0:T(4,128)S(1)}, f32[2,4,4096]{2,1,0:T(4,128)}, u32[]{:S(2)}) copy-start(f32[2,4,4096]{2,1,0:T(4,128)} %param.8) | copy-start | bytes 393220
  2.6 18.1 %copy-start.3 = (f32[32]{0:T(128)S(1)}, f32[32]{0:T(128)}, u32[]{:S(2)}) copy-start(f32[32]{0:T(128)} %param.12) | copy-start | bytes 388
  2.6 18.1 %copy-start.4 = (s32[2]{0:T(128)S(1)}, s32[2]{0:T(128)}, u32[]{:S(2)}) copy-start(s32[2]{0:T(128)} %param.14) | copy-start | bytes 28
  2.6 18.3 %copy-start.5 = (f32[8]{0:T(128)S(1)}, f32[8]{0:T(128)}, u32[]{:S(2)}) copy-start(f32[8]{0:T(128)} %param.13) | copy-start | bytes 100
  2.6 18.3 %copy-start.6 = (s32[2]{0:T(128)S(1)}, s32[2]{0:T(128)}, u32[]{:S(2)}) copy-start(s32[2]{0:T(128)} %param.15) | copy-start | bytes 28
  2.6 20.9 %copy-start = (f32[3,64,64]{2,1,0:T(8,128)S(1)}, f32[3,64,64]{2,1,0:T(8,128)}, u32[]{:S(2)}) copy-start(f32[3,64,64]{2,1,0:T(8,128)} %c_ref.1) | copy-start | bytes 147460
  2.7 38.5 %all-to-all-start = ((f32[8,416,128]{2,1,0:T(8,128)}), f32[8,416,128]{2,1,0:T(8,128)S(1)}, u32[]{:S(2)}, u32[]{:S(2)}) async-start(f32[8,416,128]{2,1,0:T(8,128)} %pack_orbitals.1), calls=%async_computation | async-start | bytes 3407872 | tf_op jit(solution)/shard_map/all_to_all | solution.py:509
  9.2 23.5 %collective-permute-start.3 = (f32[3,96,128]{2,1,0:T(8,128)S(1)}, f32[3,96,128]{2,1,0:T(8,128)S(1)}, u32[]{:S(2)}, u32[]{:S(2)}) collective-permute-start(f32[3,96,128]{2,1,0:T(8,128)S(1)} %slice_select_fusion), channel_id=1, source_target_pairs={{2,18},{6,20},{10,22},{14,24},{18,26},{22,28},{26,30},{4,0},{8,2},... | collective-permute-start | bytes 442376 | tf_op jit(solution)/shard_map/ppermute | solution.py:560
  10.5 22.2 %collective-permute-start.2 = (f32[3,96,128]{2,1,0:T(8,128)S(1)}, f32[3,96,128]{2,1,0:T(8,128)S(1)}, u32[]{:S(2)}, u32[]{:S(2)}) collective-permute-start(f32[3,96,128]{2,1,0:T(8,128)S(1)} %slice_select_fusion), channel_id=1, source_target_pairs={{2,2},{6,4},{10,6},{14,8},{18,10},{22,12},{26,14},{4,16},{8,18},{1... | collective-permute-start | bytes 442376 | tf_op jit(solution)/shard_map/ppermute | solution.py:560
  11.2 29.0 %collective-permute-start.1 = (f32[3,128,128]{2,1,0:T(8,128)S(1)}, f32[3,128,128]{2,1,0:T(8,128)S(1)}, u32[]{:S(2)}, u32[]{:S(2)}) collective-permute-start(f32[3,128,128]{2,1,0:T(8,128)S(1)} %constant_dynamic-update-slice_fusion), channel_id=1, source_target_pairs={{0,16},{2,0},{4,18},{6,2},{8,20},{10,4},{12,22},{14,6},{16,24},{18... | collective-permute-start | bytes 589832 | tf_op jit(solution)/shard_map/ppermute | solution.py:537
  20.1 20.2 %collective-permute-start = (f32[3,128,128]{2,1,0:T(8,128)S(1)}, f32[3,128,128]{2,1,0:T(8,128)S(1)}, u32[]{:S(2)}, u32[]{:S(2)}) collective-permute-start(f32[3,128,128]{2,1,0:T(8,128)S(1)} %constant_dynamic-update-slice_fusion), channel_id=1, source_target_pairs={{0,0},{2,16},{4,2},{6,18},{8,4},{10,20},{12,6},{14,22},{16,8},{18,... | collective-permute-start | bytes 589832 | tf_op jit(solution)/shard_map/ppermute | solution.py:537
  41.2 6.5 %collective-permute-start.4 = (f32[3328,128]{1,0:T(8,128)S(1)}, f32[3328,128]{1,0:T(8,128)S(1)}, u32[]{:S(2)}, u32[]{:S(2)}) collective-permute-start(f32[3328,128]{1,0:T(8,128)S(1)} %bitcast.8), channel_id=1, source_target_pairs={{0,1},{1,0},{2,3},{3,2},{4,5},{5,4},{6,7},{7,6},{8,9},{9,8},{10,11... | collective-permute-start | bytes 5111816 | tf_op jit(solution)/shard_map/ppermute | solution.py:503
  137.3 1.4 collective-permute-start.5
  151.2 1.4 collective-permute-start.6

commit v6 on v5

--- a/solution.py
+++ b/solution.py
@@ -47,19 +47,18 @@
     return picked_freq - picked_energy
 
 
-def spread_kernel(window, pairs, src_ref, dst_ref):
+def spread_kernel(window, pairs, src_ref, dst_ref, rows_s):
     rows = window * pairs
+    stride = rows + 1
     first_half = lax.broadcasted_iota(jnp.int32, (HALF, 128), 1) < 64
-
-    def body(w, carry):
+    for k in range(HALF):
+        rows_s[k * stride : k * stride + rows, :] = src_ref[k * rows : (k + 1) * rows, :]
+    for w in range(window):
         for i in range(pairs):
-            pair = src_ref[pl.ds(w * pairs + i, HALF, stride=rows), :]
+            pair = rows_s[pl.ds(w * pairs + i, HALF, stride=stride), :]
             turned = pltpu.roll(pair, 64, 1)
             dst_ref[w, 2 * i] = jnp.where(first_half, pair, turned)
             dst_ref[w, 2 * i + 1] = jnp.where(first_half, turned, pair)
-        return carry
-
-    lax.fori_loop(0, window, body, 0)
 
 
 def pack_kernel(slab, window, width, pairs, src_ref, dst_ref):
@@ -220,7 +219,7 @@
         top: jnp.where(first + slab >= width, 0.0, 1.0),
         top + 1: jnp.where(first + slab + 1 >= width, 0.0, 1.0),
     }
-    lax.fori_loop(0, window, products, 0)
+    lax.fori_loop(0, window, products, 0, unroll=True)
     for w, keep in inside.items():
         apply(b_refs, 0, u1_refs, 1, w, (), (), keep)
     low_pairs, high_pairs = ((0, 0), (0, 1), (1, 1)), ((0, 1), (1, 1))
@@ -597,6 +596,7 @@
             "spread_orbitals",
             shape(window, width, HALF, 128),
             (rows,),
+            scratch=[pltpu.VMEM((HALF * (window * pairs + 1), 128), F32)],
         )
         for rows in (own_half, swap(own_half))
     ]

time: 155 us -> 152 us (0.981)
  Pallas kernels: 35 us -> 31.8 us
    pallas_call x15, Pallas kernels: 35 us -> 31.8 us  [call(): pl.pallas_call(kernel, out_shape=shapes, in_specs=[smem() if k in in_smem...]
  transfers between devices with their start and end apart: 8 -> 8, of which waited for: 4 -> 4; matrix products, arithmetic and copies ran while one was open for 3% -> 3% of each run, Pallas kernels for 5% -> 4%
where the time goes in v6:
time: 152 us; the launch traced here: 151 us
  blocking collectives  78.2 us (51%)
  Pallas kernels  31.8 us (21%)
  starting transfers between devices  18 us (12%)
  waiting for transfers between devices  17.1 us (11%)
  other arithmetic  4.16 us (3%)
    all_to_all x4, blocking collectives, exchange(): return lax.all_to_all(x, 'orb', split_axis=0, concat_axis=0, tiled=True)  54.5 us
    pallas_call x15, Pallas kernels, call(): pl.pallas_call(kernel, out_shape=shapes, in_specs=[smem() if k in in_smem...  31.8 us
    all_to_all x2, blocking collectives, exchange_group(): lax.all_to_all(x, 'orb', split_axis=0, concat_axis=0, tiled=True, axis_in...  23.7 us
    ppermute x2, starting transfers between devices, shards(): lax.ppermute(fields, 'orb', [(j * rounds + k, (k + r) % rounds * group +...  9.53 us
    ppermute x2, waiting for transfers between devices, shards(): lax.ppermute(fields, 'orb', [(j * rounds + k, (k + r) % rounds * group +...  7.43 us
    ppermute x2, waiting for transfers between devices, shards(): lax.ppermute(edge, 'orb', [((j - 1) * rounds + 1, q * group + j) for j in...  6.97 us
    all_to_all x1, starting transfers between devices, exchange_group(): lax.all_to_all(x, 'orb', split_axis=0, concat_axis=0, tiled=True, axis_in...  6.33 us
  transfers between devices with their start and end apart: 8, of which 4 were waited for; matrix products, arithmetic and copies ran while one was open for 3% of the time, Pallas kernels for 4%

profile of v6, /device:TPU:0, one launch (start us, length us, event | category | flops | bytes accessed | tf_op | source)
XLA Modules:
  0.0 151.1 jit_solution(15638201146730303611)
XLA Ops:
  0.0 1.1 dynamic-slice_convert_fusion
  1.1 0.2 reshape.20.src_ref
  1.3 1.3 pack_orbitals.1
  2.6 0.0 copy-start.2
  2.6 0.0 copy-start.1
  2.6 0.0 copy-start.3
  2.6 0.0 copy-start.4
  2.6 0.0 copy-start.5
  2.6 0.0 copy-start.6
  2.6 0.0 copy-start
  2.7 6.3 %all-to-all-start = ((f32[8,416,128]{2,1,0:T(8,128)}), f32[8,416,128]{2,1,0:T(8,128)S(1)}, u32[]{:S(2)}, u32[]{:S(2)}) async-start(f32[8,416,128]{2,1,0:T(8,128)} %pack_orbitals.1), calls=%async_computation | async-start | bytes 3407872 | tf_op jit(solution)/shard_map/all_to_all | solution.py:508
  9.0 0.0 copy-done.2
  9.0 0.0 copy-done.1
  9.1 0.1 concatenate.12
  9.2 1.3 collective-permute-start.3
  10.5 0.7 collective-permute-start.2
  11.2 8.9 %collective-permute-start.1 = (f32[3,128,128]{2,1,0:T(8,128)S(1)}, f32[3,128,128]{2,1,0:T(8,128)S(1)}, u32[]{:S(2)}, u32[]{:S(2)}) collective-permute-start(f32[3,128,128]{2,1,0:T(8,128)S(1)} %constant_dynamic-update-slice_fusion), channel_id=1, source_target_pairs={{0,16},{2,0},{4,18},{6,2},{8,20},{10,4},{12,22},{14,6},{16,24},{18... | collective-permute-start | bytes 589832 | tf_op jit(solution)/shard_map/ppermute | solution.py:536
  20.1 0.7 collective-permute-start
  20.8 0.0 copy-done.3
  20.8 0.0 copy-done.4
  20.8 0.2 fusion.1
  21.0 0.0 copy-done.5
  21.0 0.0 copy-done.6
  21.0 0.2 fusion
  21.2 0.6 fusion.3
  21.8 1.3 broadcast_select_fusion.1
  23.0 0.6 fusion.2
  23.6 0.0 copy-done
  23.6 1.3 select_add_fusion.refs_2_
  24.9 0.8 factors.1
  25.7 0.1 pad_add_fusion.flag_ref.refs_0_
  25.8 7.0 %collective-permute-done.3 = f32[3,96,128]{2,1,0:T(8,128)S(1)} collective-permute-done((f32[3,96,128]{2,1,0:T(8,128)S(1)}, f32[3,96,128]{2,1,0:T(8,128)S(1)}, u32[]{:S(2)}, u32[]{:S(2)}) %collective-permute-start.3) | collective-permute-done | bytes 147488 | tf_op jit(solution)/shard_map/ppermute | solution.py:559
  32.8 0.0 collective-permute-done.2
  32.8 7.4 %collective-permute-done.1.refs_1_ = f32[3,128,128]{2,1,0:T(8,128)S(1)} collective-permute-done((f32[3,128,128]{2,1,0:T(8,128)S(1)}, f32[3,128,128]{2,1,0:T(8,128)S(1)}, u32[]{:S(2)}, u32[]{:S(2)}) %collective-permute-start.1) | collective-permute-done | bytes 196640 | tf_op jit(solution)/shard_map/ppermute | solution.py:536
  40.2 0.0 collective-permute-done.refs_0_
  40.2 0.6 slab.1.slab_ref
  40.8 0.3 fields.1
  41.1 0.0 all-to-all-done
  41.2 0.1 collective-permute-start.4
  41.2 0.5 spread_orbitals.2.refs_4_.refs_0_.refs_5_
  41.8 4.2 %krylov.3 = (f32[11,64,8,128]{3,2,1,0:T(8,128)S(1)}, f32[9,64,8,128]{3,2,1,0:T(8,128)S(1)}, f32[8,128]{1,0:T(8,128)S(1)}) custom-call(s32[3]{0:T(128)S(1)} %pad_add_fusion.flag_ref.refs_0_, f32[16,52,128]{2,1,0:T(8,128)S(1)} %get-tuple-element.36.refs_1_, f32[16,128]{1,0:T(8,128)S(1)} %select_add_fusion.refs_2_, ...), custom_call_target="tpu_custom_call" | custom-call | tf_op jit(solution)/shard_map/krylov/pallas_call | solution.py:467
  46.0 0.0 collective-permute-done.4.src_ref
  46.0 0.6 spread_orbitals.3.refs_5_.refs_1_.refs_6_
  46.6 4.3 %krylov.4 = (f32[11,64,8,128]{3,2,1,0:T(8,128)S(1)}, f32[9,64,8,128]{3,2,1,0:T(8,128)S(1)}, f32[8,16,128]{2,1,0:T(8,128)S(1)}) custom-call(s32[3]{0:T(128)S(1)} %pad_add_fusion.flag_ref.refs_0_, f32[16,52,128]{2,1,0:T(8,128)S(1)} %get-tuple-element.36.refs_1_, f32[16,128]{1,0:T(8,128)S(1)} %select_add_fusion.refs_2_, ...), custom_call_target="tpu_custom_call" | custom-call | tf_op jit(solution)/shard_map/krylov/pallas_call | solution.py:467
  50.9 15.3 %all_to_all.35.pay_ref = f32[8,16,128]{2,1,0:T(8,128)S(1)} all-to-all(f32[8,16,128]{2,1,0:T(8,128)S(1)} %get-tuple-element.41), channel_id=1, replica_groups={{0,2,4,6,8,10,12,14},{16,18,20,22,24,26,28,30},{1,3,5,7,9,11,13,15},{17..., dimensions={0} | all-to-all | bytes 131072 | tf_op jit(solution)/shard_map/all_to_all | solution.py:508
  66.2 3.6 %combine.2 = f32[16,48,128]{2,1,0:T(8,128)S(1)} custom-call(s32[3]{0:T(128)S(1)} %pad_add_fusion.flag_ref.refs_0_, f32[8,16,128]{2,1,0:T(8,128)S(1)} %all_to_all.35.pay_ref, f32[16,52,128]{2,1,0:T(8,128)S(1)} %get-tuple-element.38.refs_3_.v_ref, f32[64,64]{1,0:T(8,128)S(1)} %slice_bitcast_fusion.cy_ref, f32[128,128]{1,0:T(8,128)S(1)} %get-tuple-element.43.cz_ref, ...), custom_call_target="tpu_custom_call" | custom-call | tf_op jit(solution)/shard_map/combine/pallas_call | solution.py:467
  69.8 14.7 %all_to_all.36.got_ref = f32[16,48,128]{2,1,0:T(8,128)S(1)} all-to-all(f32[16,48,128]{2,1,0:T(8,128)S(1)} %combine.2), channel_id=1, replica_groups=mesh['orb'=16,'trial'=2] {'orb'}, dimensions={0} | all-to-all | bytes 786432 | tf_op jit(solution)/shard_map/all_to_all | solution.py:505
  84.5 0.4 mapped.1
  84.9 16.4 %all_to_all.37.refs_4_ = f32[16,56,128]{2,1,0:T(8,128)S(1)} all-to-all(f32[16,56,128]{2,1,0:T(8,128)S(1)} %get-tuple-element.49), channel_id=1, replica_groups=mesh['orb'=16,'trial'=2] {'orb'}, dimensions={0} | all-to-all | bytes 917504 | tf_op jit(solution)/shard_map/all_to_all | solution.py:505
  101.3 9.3 %krylov.5 = (f32[11,64,8,128]{3,2,1,0:T(8,128)S(1)}, f32[9,64,8,128]{3,2,1,0:T(8,128)S(1)}, f32[11,64,8,128]{3,2,1,0:T(8,128)S(1)}, f32[9,64,8,128]{3,2,1,0:T(8,...) custom-call(s32[3]{0:T(128)S(1)} %pad_add_fusion.flag_ref.refs_0_, ...), custom_call_target="tpu_custom_call" | custom-call | tf_op jit(solution)/shard_map/krylov/pallas_call | solution.py:467
  110.6 8.4 %all_to_all.38.pay_ref = f32[8,16,128]{2,1,0:T(8,128)S(1)} all-to-all(f32[8,16,128]{2,1,0:T(8,128)S(1)} %get-tuple-element.50), channel_id=1, replica_groups={{0,2,4,6,8,10,12,14},{16,18,20,22,24,26,28,30},{1,3,5,7,9,11,13,15},{17..., dimensions={0} | all-to-all | bytes 131072 | tf_op jit(solution)/shard_map/all_to_all | solution.py:508
  118.9 3.6 %combine.3 = f32[16,32,128]{2,1,0:T(8,128)S(1)} custom-call(s32[3]{0:T(128)S(1)} %pad_add_fusion.flag_ref.refs_0_, f32[8,16,128]{2,1,0:T(8,128)S(1)} %all_to_all.38.pay_ref, f32[16,52,128]{2,1,0:T(8,128)S(1)} %get-tuple-element.51.v_ref, f32[64,64]{1,0:T(8,128)S(1)} %slice_bitcast_fusion.cy_ref, f32[128,128]{1,0:T(8,128)S(1)} %get-tuple-element.43.cz_ref, ...), custom_call_target="tpu_custom_call" | custom-call | tf_op jit(solution)/shard_map/combine/pallas_call | solution.py:467
  122.6 11.2 %all_to_all.39.got_ref = f32[16,32,128]{2,1,0:T(8,128)S(1)} all-to-all(f32[16,32,128]{2,1,0:T(8,128)S(1)} %combine.3), channel_id=1, replica_groups=mesh['orb'=16,'trial'=2] {'orb'}, dimensions={0} | all-to-all | bytes 524288 | tf_op jit(solution)/shard_map/all_to_all | solution.py:505
  133.8 0.4 second.1.second_ref
  134.1 0.1 collective-permute-start.5
  134.2 1.3 collective-permute-done.5.other_ref
  135.6 0.1 gram.1
  135.7 12.3 %all_to_all.40.got_ref = f32[16,24,128]{2,1,0:T(8,128)S(1)} all-to-all(f32[16,24,128]{2,1,0:T(8,128)S(1)} %gram.1), channel_id=1, replica_groups=mesh['orb'=16,'trial'=2] {'orb'}, dimensions={0} | all-to-all | bytes 393216 | tf_op jit(solution)/shard_map/all_to_all | solution.py:505
  148.0 0.1 collective-permute-start.6
  148.1 1.3 collective-permute-done.6.other_ref
  149.4 1.7 %final.1 = f32[2,4,4096]{2,1,0:T(4,128)} custom-call(s32[3]{0:T(128)S(1)} %pad_add_fusion.flag_ref.refs_0_, f32[16,24,128]{2,1,0:T(8,128)S(1)} %all_to_all.40.got_ref, f32[16,16,128]{2,1,0:T(8,128)S(1)} %collective-permute-done.6.other_ref), custom_call_target="tpu_custom_call" | custom-call | tf_op jit(solution)/shard_map/final/pallas_call | solution.py:467
  (11 shorter events, 0.2 us)
Async XLA Ops:
  2.6 6.4 %copy-start.2 = (f32[4,4096]{1,0:T(4,128)S(1)}, f32[4,4096]{1,0:T(4,128)}, u32[]{:S(2)}) copy-start(f32[4,4096]{1,0:T(4,128)} %param.10) | copy-start | bytes 196612
  2.6 6.4 %copy-start.1 = (f32[2,4,4096]{2,1,0:T(4,128)S(1)}, f32[2,4,4096]{2,1,0:T(4,128)}, u32[]{:S(2)}) copy-start(f32[2,4,4096]{2,1,0:T(4,128)} %param.8) | copy-start | bytes 393220
  2.6 18.1 %copy-start.3 = (f32[32]{0:T(128)S(1)}, f32[32]{0:T(128)}, u32[]{:S(2)}) copy-start(f32[32]{0:T(128)} %param.12) | copy-start | bytes 388
  2.6 18.1 %copy-start.4 = (s32[2]{0:T(128)S(1)}, s32[2]{0:T(128)}, u32[]{:S(2)}) copy-start(s32[2]{0:T(128)} %param.14) | copy-start | bytes 28
  2.6 18.3 %copy-start.5 = (f32[8]{0:T(128)S(1)}, f32[8]{0:T(128)}, u32[]{:S(2)}) copy-start(f32[8]{0:T(128)} %param.13) | copy-start | bytes 100
  2.6 18.3 %copy-start.6 = (s32[2]{0:T(128)S(1)}, s32[2]{0:T(128)}, u32[]{:S(2)}) copy-start(s32[2]{0:T(128)} %param.15) | copy-start | bytes 28
  2.6 20.9 %copy-start = (f32[3,64,64]{2,1,0:T(8,128)S(1)}, f32[3,64,64]{2,1,0:T(8,128)}, u32[]{:S(2)}) copy-start(f32[3,64,64]{2,1,0:T(8,128)} %c_ref.1) | copy-start | bytes 147460
  2.7 38.5 %all-to-all-start = ((f32[8,416,128]{2,1,0:T(8,128)}), f32[8,416,128]{2,1,0:T(8,128)S(1)}, u32[]{:S(2)}, u32[]{:S(2)}) async-start(f32[8,416,128]{2,1,0:T(8,128)} %pack_orbitals.1), calls=%async_computation | async-start | bytes 3407872 | tf_op jit(solution)/shard_map/all_to_all | solution.py:508
  9.2 23.5 %collective-permute-start.3 = (f32[3,96,128]{2,1,0:T(8,128)S(1)}, f32[3,96,128]{2,1,0:T(8,128)S(1)}, u32[]{:S(2)}, u32[]{:S(2)}) collective-permute-start(f32[3,96,128]{2,1,0:T(8,128)S(1)} %slice_select_fusion), channel_id=1, source_target_pairs={{2,18},{6,20},{10,22},{14,24},{18,26},{22,28},{26,30},{4,0},{8,2},... | collective-permute-start | bytes 442376 | tf_op jit(solution)/shard_map/ppermute | solution.py:559
  10.5 22.2 %collective-permute-start.2 = (f32[3,96,128]{2,1,0:T(8,128)S(1)}, f32[3,96,128]{2,1,0:T(8,128)S(1)}, u32[]{:S(2)}, u32[]{:S(2)}) collective-permute-start(f32[3,96,128]{2,1,0:T(8,128)S(1)} %slice_select_fusion), channel_id=1, source_target_pairs={{2,2},{6,4},{10,6},{14,8},{18,10},{22,12},{26,14},{4,16},{8,18},{1... | collective-permute-start | bytes 442376 | tf_op jit(solution)/shard_map/ppermute | solution.py:559
  11.2 29.0 %collective-permute-start.1 = (f32[3,128,128]{2,1,0:T(8,128)S(1)}, f32[3,128,128]{2,1,0:T(8,128)S(1)}, u32[]{:S(2)}, u32[]{:S(2)}) collective-permute-start(f32[3,128,128]{2,1,0:T(8,128)S(1)} %constant_dynamic-update-slice_fusion), channel_id=1, source_target_pairs={{0,16},{2,0},{4,18},{6,2},{8,20},{10,4},{12,22},{14,6},{16,24},{18... | collective-permute-start | bytes 589832 | tf_op jit(solution)/shard_map/ppermute | solution.py:536
  20.1 20.2 %collective-permute-start = (f32[3,128,128]{2,1,0:T(8,128)S(1)}, f32[3,128,128]{2,1,0:T(8,128)S(1)}, u32[]{:S(2)}, u32[]{:S(2)}) collective-permute-start(f32[3,128,128]{2,1,0:T(8,128)S(1)} %constant_dynamic-update-slice_fusion), channel_id=1, source_target_pairs={{0,0},{2,16},{4,2},{6,18},{8,4},{10,20},{12,6},{14,22},{16,8},{18,... | collective-permute-start | bytes 589832 | tf_op jit(solution)/shard_map/ppermute | solution.py:536
  41.2 4.8 %collective-permute-start.4 = (f32[3328,128]{1,0:T(8,128)S(1)}, f32[3328,128]{1,0:T(8,128)S(1)}, u32[]{:S(2)}, u32[]{:S(2)}) collective-permute-start(f32[3328,128]{1,0:T(8,128)S(1)} %bitcast.8), channel_id=1, source_target_pairs={{0,1},{1,0},{2,3},{3,2},{4,5},{5,4},{6,7},{7,6},{8,9},{9,8},{10,11... | collective-permute-start | bytes 5111816 | tf_op jit(solution)/shard_map/ppermute | solution.py:502
  134.1 1.4 collective-permute-start.5
  148.0 1.4 collective-permute-start.6

commit v7 on v6

--- a/solution.py
+++ b/solution.py
@@ -45,6 +45,10 @@
         jnp.where(freq_index[:, None] == freq_slots, frequencies[None, :], 0.0), axis=1
     )
     return picked_freq - picked_energy
+
+
+def placed(k, crossed):
+    return k // 4 * 4 + k % 2 * 2 + k // 2 % 2 if crossed else k
 
 
 def spread_kernel(window, pairs, src_ref, dst_ref, rows_s):
@@ -61,11 +65,11 @@
             dst_ref[w, 2 * i + 1] = jnp.where(first_half, turned, pair)
 
 
-def pack_kernel(slab, window, width, pairs, src_ref, dst_ref):
+def pack_kernel(slab, window, width, pairs, crossed, src_ref, dst_ref):
     each = src_ref.shape[0]
     size = window * pairs
     for j in range(dst_ref.shape[0]):
-        start = (j * slab - LOW) * pairs
+        start = (placed(j, crossed) * slab - LOW) * pairs
         low, high = max(start, 0), min(start + size, width * pairs)
         for e in range(each):
             if low > start:
@@ -336,30 +340,30 @@
             ]
 
 
-def gathered(got_ref, cx_ref, group):
+def gathered(got_ref, cx_ref, group, crossed):
     n = got_ref.shape[0]
     rows = cx_ref.shape[0] // group
     parts = []
     for j in range(group):
-        parts.append(tree([got_ref[q * group + j, 0:rows, :] for q in range(n // group)]))
+        parts.append(tree([got_ref[q * group + placed(j, crossed), 0:rows, :] for q in range(n // group)]))
     return dot(cx_ref[...], jnp.concatenate(parts, axis=0))
 
 
-def mapped_kernel(slab, lines, width, group, got_ref, cx_ref, mapped_ref, t_ref, pay_ref):
+def mapped_kernel(slab, lines, width, group, crossed, got_ref, cx_ref, mapped_ref, t_ref, pay_ref):
     n, size, _ = pay_ref.shape
-    mapped = gathered(got_ref, cx_ref, group)
+    mapped = gathered(got_ref, cx_ref, group, crossed)
     mapped_ref[...] = mapped
     rounds = n // group
     rows = slab // rounds * lines
     for j in range(group):
         for q in range(rounds):
             at = (j * rounds + q) * rows
-            t_ref[at : at + rows, :] = got_ref[q * group + j, slab * lines : slab * lines + rows, :]
+            t_ref[at : at + rows, :] = got_ref[q * group + placed(j, crossed), slab * lines : slab * lines + rows, :]
     t = t_ref[...]
     sums = [jnp.sum(a * b, axis=0, keepdims=True) for a, b in ((t, t), (t, mapped), (mapped, mapped))]
     window = (slab + LOW + HIGH) * lines
     for k in range(n):
-        start = (k % group) * slab * lines - LOW * lines
+        start = placed(k % group, crossed) * slab * lines - LOW * lines
         low, high = max(start, 0), min(start + window, width * lines)
         pay_ref[k] = jnp.zeros((size, 128), F32)
         pay_ref[k, low - start : high - start, :] = mapped_ref[low:high, :]
@@ -367,8 +371,8 @@
             pay_ref[k, window + i : window + i + 1, :] = s
 
 
-def second_kernel(group, got_ref, cx_ref, t_ref, mapped_ref, cs_ref, second_ref):
-    again = gathered(got_ref, cx_ref, group)
+def second_kernel(group, crossed, got_ref, cx_ref, t_ref, mapped_ref, cs_ref, second_ref):
+    again = gathered(got_ref, cx_ref, group, crossed)
     center, inverse = cs_ref[0:1], cs_ref[1:2]
     t = t_ref[...]
     first = (mapped_ref[...] - center * t) * inverse
@@ -494,6 +498,8 @@
     me = lax.axis_index("orb")
     core = lax.axis_index("trial")
     place = me % group
+    direct = planes >= HIGH and n // group == 2
+    crossed = direct and group == 8
     pairs = cells // 128
     each = held // cores
     groups = [list(range(q * group, (q + 1) * group)) for q in range(n // group)]
@@ -512,7 +518,7 @@
     mine = lax.dynamic_slice_in_dim(orbitals, core * each, each, 0).astype(F32)
     mine = mine.reshape(each, width * pairs, 128)
     sent = call(
-        functools.partial(pack_kernel, slab, window, width, pairs),
+        functools.partial(pack_kernel, slab, window, width, pairs, crossed),
         "pack_orbitals",
         shape(group, each * window * pairs, 128),
         (mine,),
@@ -530,14 +536,14 @@
     )
 
     rounds = n // group
-    flags = jnp.stack([place * slab, core, me // group]).astype(jnp.int32)
+    flags = jnp.stack([placed(place, crossed) * slab, core, me // group]).astype(jnp.int32)
     fields = jnp.concatenate([trials, potential[None]], axis=0).reshape(count + 1, planes * pairs, 128)
     blocks = [
         lax.ppermute(
             fields,
             "orb",
             [
-                (j * rounds + k, (k + r) % rounds * group + j)
+                (j * rounds + k, (k + r) % rounds * group + placed(j, crossed))
                 for j in range(group)
                 for k in range(rounds)
             ],
@@ -552,15 +558,15 @@
         limit=8,
         in_smem=(0,),
     )
-    if planes >= HIGH and rounds == 2:
+    if direct:
         last = me % rounds == rounds - 1
         edge = jnp.where(last, fields[:, (planes - HIGH) * pairs :], fields[:, : HIGH * pairs])
         first, other = (
             lax.ppermute(
                 edge,
                 "orb",
-                [((j - 1) * rounds + 1, q * group + j) for j in range(1, group)]
-                + [((j + 1) * rounds, (1 - q) * group + j) for j in range(group - 1)],
+                [((j - 1) * rounds + 1, q * group + placed(j, crossed)) for j in range(1, group)]
+                + [((j + 1) * rounds, (1 - q) * group + placed(j, crossed)) for j in range(group - 1)],
             )
             for q in range(rounds)
         )
@@ -634,7 +640,7 @@
     other_u1, other_u2, pay = krylov((1,), (trial_window,), (packed,))
     got = combine(pay, trial_window, (own_u1, own_u2, other_u1, other_u2), slab // rounds)
     mapped, trial_rows, pay = call(
-        functools.partial(mapped_kernel, slab, lines, width, group),
+        functools.partial(mapped_kernel, slab, lines, width, group, crossed),
         "mapped",
         (shape(width * lines, 128), shape(width * lines, 128), shape(n, up8(used + 3), 128)),
         (got, cx),
@@ -643,7 +649,7 @@
     pay, v, scales = made[4:]
     got = combine(pay, v, made[:4], 0)
     second = call(
-        functools.partial(second_kernel, group),
+        functools.partial(second_kernel, group, crossed),
         "second",
         shape(width * lines, 128),
         (got, cx, trial_rows, mapped, scales),

time: 152 us -> 147 us (0.967)
  blocking collectives: 78.2 us -> 74.7 us
    all_to_all x2, blocking collectives: 23.7 us -> 19.4 us  [exchange_group(): lax.all_to_all(x, 'orb', split_axis=0, concat_axis=0, tiled=True, axis_in...]
where the time goes in v7:
time: 147 us
  blocking collectives  74.7 us (51%)
  Pallas kernels  30.6 us (21%)
  starting transfers between devices  18 us (12%)
  waiting for transfers between devices  17.2 us (12%)
  other arithmetic  4.16 us (3%)
  local copies, waits for them, and re-layouts  1.5 us (1%)
    all_to_all x4, blocking collectives, exchange(): return lax.all_to_all(x, 'orb', split_axis=0, concat_axis=0, tiled=True)  55.3 us
    pallas_call x15, Pallas kernels, call(): pl.pallas_call(kernel, out_shape=shapes, in_specs=[smem() if k in in_smem...  30.6 us
    all_to_all x2, blocking collectives, exchange_group(): lax.all_to_all(x, 'orb', split_axis=0, concat_axis=0, tiled=True, axis_in...  19.4 us
    ppermute x2, starting transfers between devices, shards(): lax.ppermute(fields, 'orb', [(j * rounds + k, (k + r) % rounds * group +...  9.53 us
    ppermute x2, waiting for transfers between devices, shards(): lax.ppermute(fields, 'orb', [(j * rounds + k, (k + r) % rounds * group +...  7.58 us
    ppermute x2, waiting for transfers between devices, shards(): lax.ppermute(edge, 'orb', [((j - 1) * rounds + 1, q * group + placed(j, c...  6.93 us
    all_to_all x1, starting transfers between devices, exchange_group(): lax.all_to_all(x, 'orb', split_axis=0, concat_axis=0, tiled=True, axis_in...  6.33 us
  transfers between devices with their start and end apart: 8, of which 4 were waited for; matrix products, arithmetic and copies ran while one was open for 3% of the time, Pallas kernels for 4%

profile of v7, /device:TPU:0, one launch (start us, length us, event | category | flops | bytes accessed | tf_op | source)
XLA Modules:
  0.0 146.6 jit_solution(1895921943597613326)
XLA Ops:
  0.0 1.1 dynamic-slice_convert_fusion
  1.1 0.2 reshape.20.src_ref
  1.3 1.3 pack_orbitals.1
  2.6 0.0 copy-start.2
  2.6 0.0 copy-start.1
  2.6 0.0 copy-start.3
  2.6 0.0 copy-start.4
  2.6 0.0 copy-start.5
  2.6 0.0 copy-start.6
  2.6 0.0 copy-start
  2.7 6.3 %all-to-all-start = ((f32[8,416,128]{2,1,0:T(8,128)}), f32[8,416,128]{2,1,0:T(8,128)S(1)}, u32[]{:S(2)}, u32[]{:S(2)}) async-start(f32[8,416,128]{2,1,0:T(8,128)} %pack_orbitals.1), calls=%async_computation | async-start | bytes 3407872 | tf_op jit(solution)/shard_map/all_to_all | solution.py:514
  9.0 0.0 copy-done.2
  9.0 0.0 copy-done.1
  9.1 0.1 concatenate.12
  9.2 1.3 collective-permute-start.3
  10.5 0.7 collective-permute-start.2
  11.2 8.9 %collective-permute-start.1 = (f32[3,128,128]{2,1,0:T(8,128)S(1)}, f32[3,128,128]{2,1,0:T(8,128)S(1)}, u32[]{:S(2)}, u32[]{:S(2)}) collective-permute-start(f32[3,128,128]{2,1,0:T(8,128)S(1)} %constant_dynamic-update-slice_fusion), channel_id=1, source_target_pairs={{0,16},{2,0},{4,20},{6,4},{8,18},{10,2},{12,22},{14,6},{16,24},{18... | collective-permute-start | bytes 589832 | tf_op jit(solution)/shard_map/ppermute | solution.py:542
  20.1 0.7 collective-permute-start
  20.7 0.0 copy-done.3
  20.8 0.0 copy-done.4
  20.8 0.2 fusion.1
  21.0 0.0 copy-done.5
  21.0 0.0 copy-done.6
  21.0 0.2 fusion
  21.2 0.6 fusion.3
  21.8 1.3 broadcast_select_fusion.1
  23.0 0.6 fusion.2
  23.6 0.0 copy-done
  23.6 1.3 select_add_fusion.refs_2_
  24.9 0.8 factors.1
  25.8 0.1 pad_add_fusion.flag_ref.refs_0_
  25.8 6.9 %collective-permute-done.3 = f32[3,96,128]{2,1,0:T(8,128)S(1)} collective-permute-done((f32[3,96,128]{2,1,0:T(8,128)S(1)}, f32[3,96,128]{2,1,0:T(8,128)S(1)}, u32[]{:S(2)}, u32[]{:S(2)}) %collective-permute-start.3) | collective-permute-done | bytes 147488 | tf_op jit(solution)/shard_map/ppermute | solution.py:565
  32.8 0.0 collective-permute-done.2
  32.8 7.6 %collective-permute-done.1.refs_1_ = f32[3,128,128]{2,1,0:T(8,128)S(1)} collective-permute-done((f32[3,128,128]{2,1,0:T(8,128)S(1)}, f32[3,128,128]{2,1,0:T(8,128)S(1)}, u32[]{:S(2)}, u32[]{:S(2)}) %collective-permute-start.1) | collective-permute-done | bytes 196640 | tf_op jit(solution)/shard_map/ppermute | solution.py:542
  40.4 0.0 collective-permute-done.refs_0_
  40.4 0.6 slab.1.slab_ref
  41.0 0.3 fields.1
  41.3 0.0 all-to-all-done
  41.3 0.1 collective-permute-start.4
  41.4 0.5 spread_orbitals.2.refs_4_.refs_0_.refs_5_
  41.9 4.2 %krylov.3 = (f32[11,64,8,128]{3,2,1,0:T(8,128)S(1)}, f32[9,64,8,128]{3,2,1,0:T(8,128)S(1)}, f32[8,128]{1,0:T(8,128)S(1)}) custom-call(s32[3]{0:T(128)S(1)} %pad_add_fusion.flag_ref.refs_0_, f32[16,52,128]{2,1,0:T(8,128)S(1)} %get-tuple-element.36.refs_1_, f32[16,128]{1,0:T(8,128)S(1)} %select_add_fusion.refs_2_, ...), custom_call_target="tpu_custom_call" | custom-call | tf_op jit(solution)/shard_map/krylov/pallas_call | solution.py:471
  46.1 0.0 collective-permute-done.4.src_ref
  46.1 0.6 spread_orbitals.3.refs_5_.refs_1_.refs_6_
  46.7 4.2 %krylov.4 = (f32[11,64,8,128]{3,2,1,0:T(8,128)S(1)}, f32[9,64,8,128]{3,2,1,0:T(8,128)S(1)}, f32[8,16,128]{2,1,0:T(8,128)S(1)}) custom-call(s32[3]{0:T(128)S(1)} %pad_add_fusion.flag_ref.refs_0_, f32[16,52,128]{2,1,0:T(8,128)S(1)} %get-tuple-element.36.refs_1_, f32[16,128]{1,0:T(8,128)S(1)} %select_add_fusion.refs_2_, ...), custom_call_target="tpu_custom_call" | custom-call | tf_op jit(solution)/shard_map/krylov/pallas_call | solution.py:471
  50.9 11.0 %all_to_all.35.pay_ref = f32[8,16,128]{2,1,0:T(8,128)S(1)} all-to-all(f32[8,16,128]{2,1,0:T(8,128)S(1)} %get-tuple-element.41), channel_id=1, replica_groups={{0,2,4,6,8,10,12,14},{16,18,20,22,24,26,28,30},{1,3,5,7,9,11,13,15},{17..., dimensions={0} | all-to-all | bytes 131072 | tf_op jit(solution)/shard_map/all_to_all | solution.py:514
  61.9 3.4 %combine.2 = f32[16,48,128]{2,1,0:T(8,128)S(1)} custom-call(s32[3]{0:T(128)S(1)} %pad_add_fusion.flag_ref.refs_0_, f32[8,16,128]{2,1,0:T(8,128)S(1)} %all_to_all.35.pay_ref, f32[16,52,128]{2,1,0:T(8,128)S(1)} %get-tuple-element.38.refs_3_.v_ref, f32[64,64]{1,0:T(8,128)S(1)} %slice_bitcast_fusion.cy_ref, f32[128,128]{1,0:T(8,128)S(1)} %get-tuple-element.43.cz_ref, ...), custom_call_target="tpu_custom_call" | custom-call | tf_op jit(solution)/shard_map/combine/pallas_call | solution.py:471
  65.4 15.5 %all_to_all.36.got_ref = f32[16,48,128]{2,1,0:T(8,128)S(1)} all-to-all(f32[16,48,128]{2,1,0:T(8,128)S(1)} %combine.2), channel_id=1, replica_groups=mesh['orb'=16,'trial'=2] {'orb'}, dimensions={0} | all-to-all | bytes 786432 | tf_op jit(solution)/shard_map/all_to_all | solution.py:511
  80.8 0.4 mapped.1
  81.2 16.4 %all_to_all.37.refs_4_ = f32[16,56,128]{2,1,0:T(8,128)S(1)} all-to-all(f32[16,56,128]{2,1,0:T(8,128)S(1)} %get-tuple-element.49), channel_id=1, replica_groups=mesh['orb'=16,'trial'=2] {'orb'}, dimensions={0} | all-to-all | bytes 917504 | tf_op jit(solution)/shard_map/all_to_all | solution.py:511
  97.6 8.6 %krylov.5 = (f32[11,64,8,128]{3,2,1,0:T(8,128)S(1)}, f32[9,64,8,128]{3,2,1,0:T(8,128)S(1)}, f32[11,64,8,128]{3,2,1,0:T(8,128)S(1)}, f32[9,64,8,128]{3,2,1,0:T(8,...) custom-call(s32[3]{0:T(128)S(1)} %pad_add_fusion.flag_ref.refs_0_, ...), custom_call_target="tpu_custom_call" | custom-call | tf_op jit(solution)/shard_map/krylov/pallas_call | solution.py:471
  106.3 8.4 %all_to_all.38.pay_ref = f32[8,16,128]{2,1,0:T(8,128)S(1)} all-to-all(f32[8,16,128]{2,1,0:T(8,128)S(1)} %get-tuple-element.50), channel_id=1, replica_groups={{0,2,4,6,8,10,12,14},{16,18,20,22,24,26,28,30},{1,3,5,7,9,11,13,15},{17..., dimensions={0} | all-to-all | bytes 131072 | tf_op jit(solution)/shard_map/all_to_all | solution.py:514
  114.6 3.4 %combine.3 = f32[16,32,128]{2,1,0:T(8,128)S(1)} custom-call(s32[3]{0:T(128)S(1)} %pad_add_fusion.flag_ref.refs_0_, f32[8,16,128]{2,1,0:T(8,128)S(1)} %all_to_all.38.pay_ref, f32[16,52,128]{2,1,0:T(8,128)S(1)} %get-tuple-element.51.v_ref, f32[64,64]{1,0:T(8,128)S(1)} %slice_bitcast_fusion.cy_ref, f32[128,128]{1,0:T(8,128)S(1)} %get-tuple-element.43.cz_ref, ...), custom_call_target="tpu_custom_call" | custom-call | tf_op jit(solution)/shard_map/combine/pallas_call | solution.py:471
  118.1 11.2 %all_to_all.39.got_ref = f32[16,32,128]{2,1,0:T(8,128)S(1)} all-to-all(f32[16,32,128]{2,1,0:T(8,128)S(1)} %combine.3), channel_id=1, replica_groups=mesh['orb'=16,'trial'=2] {'orb'}, dimensions={0} | all-to-all | bytes 524288 | tf_op jit(solution)/shard_map/all_to_all | solution.py:511
  129.2 0.4 second.1.second_ref
  129.6 0.1 collective-permute-start.5
  129.7 1.3 collective-permute-done.5.other_ref
  131.0 0.1 gram.1
  131.2 12.3 %all_to_all.40.got_ref = f32[16,24,128]{2,1,0:T(8,128)S(1)} all-to-all(f32[16,24,128]{2,1,0:T(8,128)S(1)} %gram.1), channel_id=1, replica_groups=mesh['orb'=16,'trial'=2] {'orb'}, dimensions={0} | all-to-all | bytes 393216 | tf_op jit(solution)/shard_map/all_to_all | solution.py:511
  143.5 0.1 collective-permute-start.6
  143.6 1.3 collective-permute-done.6.other_ref
  144.9 1.7 %final.1 = f32[2,4,4096]{2,1,0:T(4,128)} custom-call(s32[3]{0:T(128)S(1)} %pad_add_fusion.flag_ref.refs_0_, f32[16,24,128]{2,1,0:T(8,128)S(1)} %all_to_all.40.got_ref, f32[16,16,128]{2,1,0:T(8,128)S(1)} %collective-permute-done.6.other_ref), custom_call_target="tpu_custom_call" | custom-call | tf_op jit(solution)/shard_map/final/pallas_call | solution.py:471
  (11 shorter events, 0.2 us)
Async XLA Ops:
  2.6 6.4 %copy-start.2 = (f32[4,4096]{1,0:T(4,128)S(1)}, f32[4,4096]{1,0:T(4,128)}, u32[]{:S(2)}) copy-start(f32[4,4096]{1,0:T(4,128)} %param.10) | copy-start | bytes 196612
  2.6 6.4 %copy-start.1 = (f32[2,4,4096]{2,1,0:T(4,128)S(1)}, f32[2,4,4096]{2,1,0:T(4,128)}, u32[]{:S(2)}) copy-start(f32[2,4,4096]{2,1,0:T(4,128)} %param.8) | copy-start | bytes 393220
  2.6 18.1 %copy-start.3 = (f32[32]{0:T(128)S(1)}, f32[32]{0:T(128)}, u32[]{:S(2)}) copy-start(f32[32]{0:T(128)} %param.12) | copy-start | bytes 388
  2.6 18.1 %copy-start.4 = (s32[2]{0:T(128)S(1)}, s32[2]{0:T(128)}, u32[]{:S(2)}) copy-start(s32[2]{0:T(128)} %param.14) | copy-start | bytes 28
  2.6 18.3 %copy-start.5 = (f32[8]{0:T(128)S(1)}, f32[8]{0:T(128)}, u32[]{:S(2)}) copy-start(f32[8]{0:T(128)} %param.13) | copy-start | bytes 100
  2.6 18.3 %copy-start.6 = (s32[2]{0:T(128)S(1)}, s32[2]{0:T(128)}, u32[]{:S(2)}) copy-start(s32[2]{0:T(128)} %param.15) | copy-start | bytes 28
  2.6 20.9 %copy-start = (f32[3,64,64]{2,1,0:T(8,128)S(1)}, f32[3,64,64]{2,1,0:T(8,128)}, u32[]{:S(2)}) copy-start(f32[3,64,64]{2,1,0:T(8,128)} %c_ref.1) | copy-start | bytes 147460
  2.7 38.6 %all-to-all-start = ((f32[8,416,128]{2,1,0:T(8,128)}), f32[8,416,128]{2,1,0:T(8,128)S(1)}, u32[]{:S(2)}, u32[]{:S(2)}) async-start(f32[8,416,128]{2,1,0:T(8,128)} %pack_orbitals.1), calls=%async_computation | async-start | bytes 3407872 | tf_op jit(solution)/shard_map/all_to_all | solution.py:514
  9.2 23.5 %collective-permute-start.3 = (f32[3,96,128]{2,1,0:T(8,128)S(1)}, f32[3,96,128]{2,1,0:T(8,128)S(1)}, u32[]{:S(2)}, u32[]{:S(2)}) collective-permute-start(f32[3,96,128]{2,1,0:T(8,128)S(1)} %slice_select_fusion), channel_id=1, source_target_pairs={{2,20},{6,18},{10,22},{14,24},{18,28},{22,26},{26,30},{4,0},{8,4},... | collective-permute-start | bytes 442376 | tf_op jit(solution)/shard_map/ppermute | solution.py:565
  10.5 22.2 %collective-permute-start.2 = (f32[3,96,128]{2,1,0:T(8,128)S(1)}, f32[3,96,128]{2,1,0:T(8,128)S(1)}, u32[]{:S(2)}, u32[]{:S(2)}) collective-permute-start(f32[3,96,128]{2,1,0:T(8,128)S(1)} %slice_select_fusion), channel_id=1, source_target_pairs={{2,4},{6,2},{10,6},{14,8},{18,12},{22,10},{26,14},{4,16},{8,20},{1... | collective-permute-start | bytes 442376 | tf_op jit(solution)/shard_map/ppermute | solution.py:565
  11.2 29.2 %collective-permute-start.1 = (f32[3,128,128]{2,1,0:T(8,128)S(1)}, f32[3,128,128]{2,1,0:T(8,128)S(1)}, u32[]{:S(2)}, u32[]{:S(2)}) collective-permute-start(f32[3,128,128]{2,1,0:T(8,128)S(1)} %constant_dynamic-update-slice_fusion), channel_id=1, source_target_pairs={{0,16},{2,0},{4,20},{6,4},{8,18},{10,2},{12,22},{14,6},{16,24},{18... | collective-permute-start | bytes 589832 | tf_op jit(solution)/shard_map/ppermute | solution.py:542
  20.1 20.3 %collective-permute-start = (f32[3,128,128]{2,1,0:T(8,128)S(1)}, f32[3,128,128]{2,1,0:T(8,128)S(1)}, u32[]{:S(2)}, u32[]{:S(2)}) collective-permute-start(f32[3,128,128]{2,1,0:T(8,128)S(1)} %constant_dynamic-update-slice_fusion), channel_id=1, source_target_pairs={{0,0},{2,16},{4,4},{6,20},{8,2},{10,18},{12,6},{14,22},{16,8},{18,... | collective-permute-start | bytes 589832 | tf_op jit(solution)/shard_map/ppermute | solution.py:542
  41.3 4.8 %collective-permute-start.4 = (f32[3328,128]{1,0:T(8,128)S(1)}, f32[3328,128]{1,0:T(8,128)S(1)}, u32[]{:S(2)}, u32[]{:S(2)}) collective-permute-start(f32[3328,128]{1,0:T(8,128)S(1)} %bitcast.8), channel_id=1, source_target_pairs={{0,1},{1,0},{2,3},{3,2},{4,5},{5,4},{6,7},{7,6},{8,9},{9,8},{10,11... | collective-permute-start | bytes 5111816 | tf_op jit(solution)/shard_map/ppermute | solution.py:508
  129.6 1.4 collective-permute-start.5
  143.5 1.4 collective-permute-start.6
